TPU v7x, 32 devices: a whole 2x2x4 slice. The times are simulated.
32 devices in a mesh: grp: 2 (over y), row: 16 (over z, x, core).
Axes of the slice: x: 2, y: 2, z: 4, core: 2. Of those that a mesh axis runs over, the one named last changes fastest.
Arguments:
- queries: bfloat16 [4096, 4096], P(('grp', 'row')), parts along dimension 0, may hold values from -130 to 130
- answer_keys: bfloat16 [4096, 512], P(('grp', 'row')), parts along dimension 0, may hold values from -6 to 6
- answer_values: bfloat16 [4096, 512], P(('grp', 'row')), parts along dimension 0, may hold values from -6 to 6
- prompt_keys: bfloat16 [256, 512], P(('grp', 'row')), parts along dimension 0, may hold values from -4 to 4
- prompt_values: bfloat16 [256, 512], P(('grp', 'row')), parts along dimension 0, may hold values from -6 to 6
- out_grad: bfloat16 [4096, 4096], P(('grp', 'row')), parts along dimension 0, may hold values from -6 to 6
- weights: float32 [4096], P(('grp', 'row')), parts along dimension 0, may hold values from 0.25 to 4
- lengths: int32 [64], P('grp'), parts along dimension 0, may hold values from 1 to 256, as said below
Outputs:
- attn_out: bfloat16 [4096, 4096], P(('grp', 'row')), parts along dimension 0
- q_grad: bfloat16 [4096, 4096], P(('grp', 'row')), parts along dimension 0
- answer_key_grad: bfloat16 [4096, 512], P(('grp', 'row')), parts along dimension 0
- answer_value_grad: bfloat16 [4096, 512], P(('grp', 'row')), parts along dimension 0
- prompt_key_grad: float32 [256, 512], P(('grp', 'row')), parts along dimension 0
- prompt_value_grad: float32 [256, 512], P(('grp', 'row')), parts along dimension 0
There are 2 independent parts, one for each index of `grp`. A program takes and returns all parts, laid end to end along the dimension named above; each array names one. Nothing has to cross between parts.
Inputs may be any that keep to these rules, and one draw needn't show every extreme that they name: `lengths`: the answers fill the 2048 packed rows in order; the longest has exactly 256 rows.
All inputs are finite; a program needn't handle non-finite values.
Results may differ from a plain program's by a relative error of at most 0.02.
Values may be sent and summed in bfloat16 or wider, within the bound.
No kernel may reach another device: no remote copies, remote signals or barrier semaphores. Data moves between devices by JAX's collectives and lax.ppermute only.
A program may use at most 192 MiB of HBM per device.

v0:
```python
import jax
import jax.numpy as jnp
from jax import lax
from jax.sharding import PartitionSpec as P

HEAD_DIM = 128


MASKED = -1e30


def shifted(x, axis, by):
    length = lax.axis_size(axis)
    pairs = [(i, i + by) for i in range(length) if 0 <= i + by < length]
    return lax.ppermute(x, axis, pairs)


def times_transposed(former, latter):
    return lax.dot_general(
        former, latter, (((1,), (1,)), ((), ())), preferred_element_type=jnp.float32
    )


def transposed_times(former, latter):
    return lax.dot_general(
        former, latter, (((0,), (0,)), ((), ())), preferred_element_type=jnp.float32
    )


def segment_of(positions, lengths):
    finish = jnp.cumsum(lengths, dtype=jnp.int32)
    starts = finish - lengths
    covered = (starts[None, :] <= positions[:, None]).astype(jnp.int32)
    return jnp.sum(covered, axis=1, dtype=jnp.int32) - 1


def probabilities(flat_queries, key_rows, allowed, group_size):
    key_count = key_rows.shape[0]
    height = allowed.shape[0]
    factor = key_rows.shape[1] ** (-0.5)
    scores = (times_transposed(flat_queries, key_rows) * factor).reshape(
        height, group_size, key_count
    )
    window = jnp.concatenate(
        [jnp.ones((height, key_count - allowed.shape[1]), dtype=jnp.bool_), allowed], axis=1
    )
    scores = jnp.where(window[:, None, :], scores, MASKED)
    highest = jnp.max(scores, axis=2, keepdims=True)
    powers = jnp.exp(scores - highest)
    totals = jnp.sum(powers, axis=2, keepdims=True)
    return ((powers / totals).reshape(height * group_size, key_count), highest, totals)


def per_device(
    queries, answer_keys, answer_values, prompt_keys, prompt_values, out_grad, weights, lengths
):
    height = queries.shape[0]
    head_dim = HEAD_DIM
    columns = answer_keys.shape[1]
    kv_heads = columns // head_dim
    group_size = queries.shape[1] // columns
    span_cols = group_size * head_dim
    factor = head_dim ** (-0.5)
    prompt_count = prompt_keys.shape[0] * lax.axis_size("row")
    device_place = lax.axis_index("row")
    own_pos = device_place * height + jnp.arange(height, dtype=jnp.int32)
    key_pos = (device_place - 2) * height + jnp.arange(3 * height, dtype=jnp.int32)
    own_seg = segment_of(own_pos, lengths)
    key_seg = segment_of(key_pos, lengths)
    allowed = (
        (key_pos[None, :] >= 0)
        & (key_pos[None, :] <= own_pos[:, None])
        & (key_seg[None, :] == own_seg[:, None])
    )
    earlier = (answer_keys, answer_values)
    received = []
    for repeat in range(2):
        earlier = shifted((earlier[0], earlier[1]), "row", 1)
        received.insert(0, earlier)
    window_keys = jnp.concatenate([received[0][0], received[1][0], answer_keys], axis=0)
    window_values = jnp.concatenate([received[0][1], received[1][1], answer_values], axis=0)
    cotangent = (weights[:, None] * out_grad.astype(jnp.float32)).astype(jnp.bfloat16)

    def head_slices(kv_index, gathered_keys, gathered_values):
        flat_queries = queries[:, kv_index * span_cols : (kv_index + 1) * span_cols].reshape(
            height * group_size, head_dim
        )
        flat_cot = cotangent[:, kv_index * span_cols : (kv_index + 1) * span_cols].reshape(
            height * group_size, head_dim
        )
        key_rows = jnp.concatenate(
            [
                gathered_keys[:, kv_index * head_dim : (kv_index + 1) * head_dim],
                window_keys[:, kv_index * head_dim : (kv_index + 1) * head_dim],
            ],
            axis=0,
        )
        value_rows = jnp.concatenate(
            [
                gathered_values[:, kv_index * head_dim : (kv_index + 1) * head_dim],
                window_values[:, kv_index * head_dim : (kv_index + 1) * head_dim],
            ],
            axis=0,
        )
        return (flat_queries, flat_cot, key_rows, value_rows)

    gathered_keys, gathered_values = (
        lax.all_gather(prompt_keys, "row", axis=0, tiled=True),
        lax.all_gather(prompt_values, "row", axis=0, tiled=True),
    )
    attended_list = []
    records = []
    for kv_index in range(kv_heads):
        flat_queries, flat_cot, key_rows, value_rows = head_slices(
            kv_index, gathered_keys, gathered_values
        )
        chances, highest, totals = probabilities(flat_queries, key_rows, allowed, group_size)
        attended_list.append(
            jnp.dot(
                chances.astype(jnp.bfloat16), value_rows, preferred_element_type=jnp.float32
            ).astype(jnp.bfloat16)
        )
    source_keys, source_values = (
        lax.all_gather(prompt_keys, "row", axis=0, tiled=True),
        lax.all_gather(prompt_values, "row", axis=0, tiled=True),
    )
    for kv_index in range(kv_heads):
        flat_queries, flat_cot, key_rows, value_rows = head_slices(
            kv_index, source_keys, source_values
        )
        chances, highest, totals = probabilities(flat_queries, key_rows, allowed, group_size)
        rounded = chances.astype(jnp.bfloat16)
        row_delta = jnp.sum(
            flat_cot.astype(jnp.float32) * attended_list[kv_index].astype(jnp.float32),
            axis=1,
            keepdims=True,
        )
        head_slopes = times_transposed(flat_cot, value_rows)
        head_score_grad = (chances * (head_slopes - row_delta)).astype(jnp.bfloat16)
        q_part = (
            jnp.dot(head_score_grad, key_rows, preferred_element_type=jnp.float32) * factor
        ).astype(jnp.bfloat16)
        key_part = transposed_times(head_score_grad[:, prompt_count:], flat_queries) * factor
        value_part = transposed_times(rounded[:, prompt_count:], flat_cot)
        q_part, key_part, value_part, row_delta = (q_part, key_part, value_part, row_delta)
        records.append((q_part, key_part, value_part, row_delta, highest, totals))
    attn_out = jnp.concatenate([item.reshape(height, span_cols) for item in attended_list], axis=1)
    q_grad = jnp.concatenate([record[0].reshape(height, span_cols) for record in records], axis=1)
    key_terms = jnp.concatenate([record[1] for record in records], axis=1)
    value_terms = jnp.concatenate([record[2] for record in records], axis=1)
    row_count = lax.axis_size("row") * prompt_keys.shape[0]
    key_parts = []
    value_parts = []
    for kv_index in range(kv_heads):
        flat_queries = queries[:, kv_index * span_cols : (kv_index + 1) * span_cols].reshape(
            height * group_size, head_dim
        )
        flat_cot = cotangent[:, kv_index * span_cols : (kv_index + 1) * span_cols].reshape(
            height * group_size, head_dim
        )
        key_piece = source_keys[:, kv_index * head_dim : (kv_index + 1) * head_dim]
        value_piece = source_values[:, kv_index * head_dim : (kv_index + 1) * head_dim]
        row_delta, highest, totals = (
            records[kv_index][3],
            records[kv_index][4],
            records[kv_index][5],
        )
        scores = (times_transposed(flat_queries, key_piece) * factor).reshape(
            height, group_size, row_count
        )
        chances = (jnp.exp(scores - highest) / totals).reshape(height * group_size, row_count)
        slopes = times_transposed(flat_cot, value_piece)
        score_grad = (chances * (slopes - row_delta)).astype(jnp.bfloat16)
        key_parts.append(transposed_times(score_grad, flat_queries) * factor)
        value_parts.append(transposed_times(chances.astype(jnp.bfloat16), flat_cot))
    stacked = lax.psum_scatter(
        jnp.concatenate(key_parts + value_parts, axis=1), "row", scatter_dimension=0, tiled=True
    )
    prompt_key_grad = stacked[:, :columns]
    prompt_value_grad = stacked[:, columns:]
    pending = (key_terms[:height], value_terms[:height])
    for nearer in (
        (key_terms[height : 2 * height], value_terms[height : 2 * height]),
        (key_terms[2 * height :], value_terms[2 * height :]),
    ):
        arrived = shifted((pending[0], pending[1]), "row", -1)
        pending = (nearer[0] + arrived[0], nearer[1] + arrived[1])
    answer_key_grad = pending[0].astype(jnp.bfloat16)
    answer_value_grad = pending[1].astype(jnp.bfloat16)
    return (
        attn_out,
        q_grad,
        answer_key_grad,
        answer_value_grad,
        prompt_key_grad,
        prompt_value_grad,
    )


def solution(mesh):
    in_specs = (
        P(("grp", "row"), None),
        P(("grp", "row"), None),
        P(("grp", "row"), None),
        P(("grp", "row"), None),
        P(("grp", "row"), None),
        P(("grp", "row"), None),
        P(("grp", "row")),
        P("grp"),
    )
    out_specs = (
        P(("grp", "row"), None),
        P(("grp", "row"), None),
        P(("grp", "row"), None),
        P(("grp", "row"), None),
        P(("grp", "row"), None),
        P(("grp", "row"), None),
    )
    return jax.shard_map(
        per_device, mesh=mesh, in_specs=in_specs, out_specs=out_specs, check_vma=False
    )
```

profile of v0, /device:TPU:0, one launch (start us, length us, event | category | flops | bytes accessed | tf_op | source)
XLA Modules:
  0.0 189.2 jit_solution(16702698366994527907)
XLA Ops:
  7.2 2.4 %collective-permute-start = (bf16[128,512]{1,0:T(8,128)(2,1)}, bf16[128,512]{1,0:T(8,128)(2,1)S(1)}, u32[]{:S(2)}, u32[]{:S(2)}) collective-permute-start(bf16[128,512]{1,0:T(8,128)(2,1)} %param.9), channel_id=1, source_target_pairs={{0,1},{1,2},{2,3},{3,4},{4,5},{5,6},{6,7},{7,8},{8,9},{9,10},{10,1... | collective-permute-start | bytes 393224 | tf_op jit(solution)/shard_map/ppermute | solution.py:15
  9.6 4.5 %collective-permute-start.2 = (bf16[128,512]{1,0:T(8,128)(2,1)}, bf16[128,512]{1,0:T(8,128)(2,1)S(1)}, u32[]{:S(2)}, u32[]{:S(2)}) collective-permute-start(bf16[128,512]{1,0:T(8,128)(2,1)} %param.10), channel_id=1, source_target_pairs={{0,1},{1,2},{2,3},{3,4},{4,5},{5,6},{6,7},{7,8},{8,9},{9,10},{10,1... | collective-permute-start | bytes 393224 | tf_op jit(solution)/shard_map/ppermute | solution.py:15
  15.9 20.6 %all_gather.9 = bf16[128,512]{1,0:T(8,128)(2,1)S(1)} all-gather(bf16[8,512]{1,0:T(8,128)(2,1)} %param.12), channel_id=1, replica_groups=mesh['grp'=2,'row'=16] {'row'}, dimensions={0}, use_global_device_ids=true | all-gather | bytes 139264 | tf_op jit(solution)/shard_map/all_gather | solution.py:109
  37.0 1.6 multiply_convert_fusion.4
  44.5 17.8 %all_gather.8 = bf16[128,512]{1,0:T(8,128)(2,1)S(1)} all-gather(bf16[8,512]{1,0:T(8,128)(2,1)S(1)} %copy-done.23), channel_id=1, replica_groups=mesh['grp'=2,'row'=16] {'row'}, dimensions={0}, use_global_device_ids=true | all-gather | bytes 139264 | tf_op jit(solution)/shard_map/all_gather | solution.py:108
  62.2 2.2 %collective-permute-start.1 = (bf16[128,512]{1,0:T(8,128)(2,1)S(1)}, bf16[128,512]{1,0:T(8,128)(2,1)S(1)}, u32[]{:S(2)}, u32[]{:S(2)}) collective-permute-start(bf16[128,512]{1,0:T(8,128)(2,1)S(1)} %collective-permute-done), channel_id=1, source_target_pairs={{0,1},{1,2},{2,3},{3,4},{4,5},{5,6},{6,7},{7,8},{8,9},{9,10},{10,1... | collective-permute-start | bytes 393224 | tf_op jit(solution)/shard_map/ppermute | solution.py:15
  64.5 3.5 %collective-permute-start.3 = (bf16[128,512]{1,0:T(8,128)(2,1)S(1)}, bf16[128,512]{1,0:T(8,128)(2,1)S(1)}, u32[]{:S(2)}, u32[]{:S(2)}) collective-permute-start(bf16[128,512]{1,0:T(8,128)(2,1)S(1)} %collective-permute-done.2), channel_id=1, source_target_pairs={{0,1},{1,2},{2,3},{3,4},{4,5},{5,6},{6,7},{7,8},{8,9},{9,10},{10,1... | collective-permute-start | bytes 393224 | tf_op jit(solution)/shard_map/ppermute | solution.py:15
  70.9 1.1 multiply_reduce_fusion.1
  72.5 1.2 fusion.30
  73.7 1.1 convolution_multiply_fusion.9
  75.6 1.2 fusion.22
  77.1 1.1 fusion.44
  78.2 1.1 multiply_reduce_fusion
  79.8 1.2 fusion.31
  81.0 1.1 convolution_multiply_fusion.8
  83.0 1.2 fusion.14
  84.5 1.1 fusion.48
  85.6 1.1 multiply_reduce_fusion.2
  87.2 1.2 fusion.29
  88.4 1.0 convolution_multiply_fusion.10
  90.3 1.2 fusion.10
  91.9 1.1 fusion.50
  92.9 1.3 multiply_reduce_fusion.3
  94.8 1.2 fusion.28
  96.0 1.0 convolution_multiply_fusion.11
  97.1 2.1 %fusion.43 = f32[128,1024]{0,1:T(8,128)} fusion(bf16[1024,128]{1,0:T(8,128)(2,1)S(1)} %reshape.229, f32[1024,128]{1,0:T(8,128)} %fusion.10, bf16[1024,128]{1,0:T(8,128)(2,1)S(1)} %reshape.237, f32[1024]{0:T(1024)S(1)} %get-tuple-element.70, bf16[128,512]{1,0:T(8,128)(2,1)S(1)} %all_gather.9), kind=kOutput, calls=%fused_computation.80 | convolution fusion | flops 67518464 | bytes 1150976 | tf_op jit(solution)/shard_map/dot_general | solution.py:25
  99.2 2.1 %fusion.41 = f32[128,1024]{0,1:T(8,128)} fusion(f32[128,1024]{0,1:T(8,128)} %fusion.43, bf16[1024,128]{1,0:T(8,128)(2,1)S(1)} %reshape.231, f32[1024,128]{1,0:T(8,128)} %fusion.14, bf16[1024,128]{1,0:T(8,128)(2,1)S(1)} %reshape.239, f32[1024]{0:T(1024)S(1)} %get-tuple-element.68, bf16[128,512]{1,0:T(8,128)(2,1)S(1)} %all_gather.9), kind=kOutput, calls=%fused_computation.78 | convolution fusion | flops 67518464 | bytes 1150976 | tf_op jit(solution)/shard_map/dot_general | solution.py:25
  101.3 1.1 fusion.39
  102.4 1.1 fusion.37
  103.5 2.0 %convolution_dynamic-update-slice_fusion.3 = f32[128,1024]{0,1:T(8,128)} fusion(f32[128,1024]{0,1:T(8,128)} %fusion.37, bf16[1024,128]{1,0:T(8,128)(2,1)S(1)} %reshape.237, f32[1024,128]{1,0:T(8,128)} %fusion.10), kind=kOutput, calls=%fused_computation.72 | convolution fusion | flops 33685504 | bytes 851968 | tf_op jit(solution)/shard_map/dot_general | solution.py:25
  108.2 1.4 collective-permute-start.6
  110.4 1.3 collective-permute-start.4
  113.3 1.1 reshape.244
  114.4 1.1 copy.69
  115.7 1.1 reshape.240
  116.7 1.8 copy.67
  118.5 1.1 reshape.230
  119.6 1.8 reshape.238
  121.4 2.0 %copy.90 = f32[128,1024]{1,0:T(8,128)} copy(f32[128,1024]{0,1:T(8,128)} %convolution_dynamic-update-slice_fusion) | data formatting | bytes 1048576
  123.4 1.0 slice_add_fusion
  124.4 1.3 collective-permute-start.7
  125.7 1.7 slice_add_fusion.2
  127.4 1.3 collective-permute-start.5
  128.7 2.4 %pad_maximum_fusion = (bf16[128,4096]{1,0:T(8,128)(2,1)}, bf16[128,4096]{1,0:T(8,128)(2,1)}) fusion(bf16[128,1024]{1,0:T(8,128)(2,1)S(1)} %reshape.236, bf16[128,1024]{1,0:T(8,128)(2,1)S(1)} %reshape.234, bf16[128,1024]{1,0:T(8,128)(2,1)S(1)} %reshape.232, bf16[128,1024]{1,0:T(8,128)(2,1)S(1)} %reshape.230, bf16[128,1024]{1,0:T(8,128)(2,1)S(1)} %reshape.244, ...), kind=kLoop, calls=%fused_computation.81 | loop fusion | flops 8388608 | bytes 4194304 | tf_op jit(solution)/shard_map/concatenate | solution.py:147
  131.9 1.1 collective-permute-done.5
  133.1 1.0 fusion.61
  134.8 46.2 %reduce-scatter.4.cloned.1.call-done = f32[8,1024]{1,0:T(8,128)} async-done(((f32[128,1024]{1,0:T(8,128)}), f32[8,1024]{1,0:T(8,128)}) %reduce-scatter.4.cloned.1.call-update) | async-done | bytes 32784
  181.0 1.3 fusion.104
  (130 shorter events, 23.2 us)
Async XLA Ops:
  7.2 173.9 %reduce-scatter.4.cloned.1.call-start = ((), (), s32[]{:S(2)}) async-start(), calls=%async_computation.1 | async-start | bytes 557056
  7.2 55.0 %collective-permute-start = (bf16[128,512]{1,0:T(8,128)(2,1)}, bf16[128,512]{1,0:T(8,128)(2,1)S(1)}, u32[]{:S(2)}, u32[]{:S(2)}) collective-permute-start(bf16[128,512]{1,0:T(8,128)(2,1)} %param.9), channel_id=1, source_target_pairs={{0,1},{1,2},{2,3},{3,4},{4,5},{5,6},{6,7},{7,8},{8,9},{9,10},{10,1... | collective-permute-start | bytes 393224 | tf_op jit(solution)/shard_map/ppermute | solution.py:15
  9.6 55.0 %collective-permute-start.2 = (bf16[128,512]{1,0:T(8,128)(2,1)}, bf16[128,512]{1,0:T(8,128)(2,1)S(1)}, u32[]{:S(2)}, u32[]{:S(2)}) collective-permute-start(bf16[128,512]{1,0:T(8,128)(2,1)} %param.10), channel_id=1, source_target_pairs={{0,1},{1,2},{2,3},{3,4},{4,5},{5,6},{6,7},{7,8},{8,9},{9,10},{10,1... | collective-permute-start | bytes 393224 | tf_op jit(solution)/shard_map/ppermute | solution.py:15
  36.9 1.7 copy-start.2
  40.5 3.9 %copy-start.23 = (bf16[8,512]{1,0:T(8,128)(2,1)S(1)}, bf16[8,512]{1,0:T(8,128)(2,1)}, u32[]{:S(2)}) copy-start(bf16[8,512]{1,0:T(8,128)(2,1)} %param.11) | copy-start | bytes 24580
  42.2 25.9 %copy-start.17 = (bf16[128,512]{1,0:T(8,128)(2,1)S(1)}, bf16[128,512]{1,0:T(8,128)(2,1)}, u32[]{:S(2)}) copy-start(bf16[128,512]{1,0:T(8,128)(2,1)} %param.9) | copy-start | bytes 393220
  62.2 5.8 %collective-permute-start.1 = (bf16[128,512]{1,0:T(8,128)(2,1)S(1)}, bf16[128,512]{1,0:T(8,128)(2,1)S(1)}, u32[]{:S(2)}, u32[]{:S(2)}) collective-permute-start(bf16[128,512]{1,0:T(8,128)(2,1)S(1)} %collective-permute-done), channel_id=1, source_target_pairs={{0,1},{1,2},{2,3},{3,4},{4,5},{5,6},{6,7},{7,8},{8,9},{9,10},{10,1... | collective-permute-start | bytes 393224 | tf_op jit(solution)/shard_map/ppermute | solution.py:15
  64.5 5.3 %collective-permute-start.3 = (bf16[128,512]{1,0:T(8,128)(2,1)S(1)}, bf16[128,512]{1,0:T(8,128)(2,1)S(1)}, u32[]{:S(2)}, u32[]{:S(2)}) collective-permute-start(bf16[128,512]{1,0:T(8,128)(2,1)S(1)} %collective-permute-done.2), channel_id=1, source_target_pairs={{0,1},{1,2},{2,3},{3,4},{4,5},{5,6},{6,7},{7,8},{8,9},{9,10},{10,1... | collective-permute-start | bytes 393224 | tf_op jit(solution)/shard_map/ppermute | solution.py:15
  69.4 0.9 copy-start.18
  69.5 1.4 copy-start.16
  69.5 1.4 copy-start.22
  76.8 1.4 copy-start.15
  76.8 1.4 copy-start.21
  84.1 1.4 copy-start.14
  84.1 1.4 copy-start.20
  91.5 1.4 copy-start.10
  91.5 1.4 copy-start.19
  96.0 6.4 %copy-start = (f32[1024,128]{1,0:T(8,128)S(1)}, f32[1024,128]{1,0:T(8,128)}, u32[]{:S(2)}) copy-start(f32[1024,128]{1,0:T(8,128)} %fusion.22) | copy-start | bytes 1572868
  101.3 4.2 %copy-start.1 = (f32[1024,128]{1,0:T(8,128)S(1)}, f32[1024,128]{1,0:T(8,128)}, u32[]{:S(2)}) copy-start(f32[1024,128]{1,0:T(8,128)} %fusion.14) | copy-start | bytes 1572868
  103.5 3.9 %copy-start.4 = (f32[384,128]{0,1:T(8,128)S(1)}, f32[384,128]{0,1:T(8,128)}, u32[]{:S(2)}) copy-start(f32[384,128]{0,1:T(8,128)} %fusion.44) | copy-start | bytes 589828
  103.5 3.9 %copy-start.6 = (f32[384,128]{0,1:T(8,128)S(1)}, f32[384,128]{0,1:T(8,128)}, u32[]{:S(2)}) copy-start(f32[384,128]{0,1:T(8,128)} %fusion.48) | copy-start | bytes 589828
  103.5 3.9 %copy-start.8 = (f32[384,128]{0,1:T(8,128)S(1)}, f32[384,128]{0,1:T(8,128)}, u32[]{:S(2)}) copy-start(f32[384,128]{0,1:T(8,128)} %fusion.50) | copy-start | bytes 589828
  105.5 4.1 %copy-start.3 = (f32[384,128]{0,1:T(8,128)S(1)}, f32[384,128]{0,1:T(8,128)}, u32[]{:S(2)}) copy-start(f32[384,128]{0,1:T(8,128)} %convolution_multiply_fusion.9) | copy-start | bytes 589828
  105.5 4.1 %copy-start.5 = (f32[384,128]{0,1:T(8,128)S(1)}, f32[384,128]{0,1:T(8,128)}, u32[]{:S(2)}) copy-start(f32[384,128]{0,1:T(8,128)} %convolution_multiply_fusion.8) | copy-start | bytes 589828
  105.5 4.1 %copy-start.7 = (f32[384,128]{0,1:T(8,128)S(1)}, f32[384,128]{0,1:T(8,128)}, u32[]{:S(2)}) copy-start(f32[384,128]{0,1:T(8,128)} %convolution_multiply_fusion.10) | copy-start | bytes 589828
  105.5 4.1 %copy-start.9 = (f32[384,128]{0,1:T(8,128)S(1)}, f32[384,128]{0,1:T(8,128)}, u32[]{:S(2)}) copy-start(f32[384,128]{0,1:T(8,128)} %convolution_multiply_fusion.11) | copy-start | bytes 589828
  107.4 5.2 %copy-start.11 = (bf16[1024,128]{0,1:T(8,128)(2,1)S(1)}, bf16[1024,128]{0,1:T(8,128)(2,1)}, u32[]{:S(2)}) copy-start(bf16[1024,128]{0,1:T(8,128)(2,1)} %get-tuple-element.67) | copy-start | bytes 786436
  108.1 4.8 %copy-start.12 = (bf16[1024,128]{1,0:T(8,128)(2,1)S(1)}, bf16[1024,128]{1,0:T(8,128)(2,1)}, u32[]{:S(2)}) copy-start(bf16[1024,128]{1,0:T(8,128)(2,1)} %fusion.30) | copy-start | bytes 786436
  108.1 4.9 %copy-start.13 = (bf16[1024,128]{0,1:T(8,128)(2,1)S(1)}, bf16[1024,128]{0,1:T(8,128)(2,1)}, u32[]{:S(2)}) copy-start(bf16[1024,128]{0,1:T(8,128)(2,1)} %get-tuple-element.65) | copy-start | bytes 786436
  108.2 15.3 %collective-permute-start.6 = (f32[128,512]{0,1:T(8,128)}, f32[128,512]{0,1:T(8,128)}, u32[]{:S(2)}, u32[]{:S(2)}) collective-permute-start(f32[128,512]{0,1:T(8,128)} %slice.229), channel_id=1, source_target_pairs={{1,0},{2,1},{3,2},{4,3},{5,4},{6,5},{7,6},{8,7},{9,8},{10,9},{11,1... | collective-permute-start | bytes 786440 | tf_op jit(solution)/shard_map/ppermute | solution.py:15
  110.4 15.3 %collective-permute-start.4 = (f32[128,512]{0,1:T(8,128)}, f32[128,512]{0,1:T(8,128)}, u32[]{:S(2)}, u32[]{:S(2)}) collective-permute-start(f32[128,512]{0,1:T(8,128)} %slice.222), channel_id=1, source_target_pairs={{1,0},{2,1},{3,2},{4,3},{5,4},{6,5},{7,6},{8,7},{9,8},{10,9},{11,1... | collective-permute-start | bytes 786440 | tf_op jit(solution)/shard_map/ppermute | solution.py:15
  124.4 6.7 %collective-permute-start.7 = (f32[128,512]{0,1:T(8,128)S(1)}, f32[128,512]{0,1:T(8,128)S(1)}, u32[]{:S(2)}, u32[]{:S(2)}) collective-permute-start(f32[128,512]{0,1:T(8,128)S(1)} %slice_add_fusion), channel_id=1, source_target_pairs={{1,0},{2,1},{3,2},{4,3},{5,4},{6,5},{7,6},{8,7},{9,8},{10,9},{11,1... | collective-permute-start | bytes 786440 | tf_op jit(solution)/shard_map/ppermute | solution.py:15
  127.4 5.6 %collective-permute-start.5 = (f32[128,512]{0,1:T(8,128)}, f32[128,512]{0,1:T(8,128)}, u32[]{:S(2)}, u32[]{:S(2)}) collective-permute-start(f32[128,512]{0,1:T(8,128)} %slice_add_fusion.2), channel_id=1, source_target_pairs={{1,0},{2,1},{3,2},{4,3},{5,4},{6,5},{7,6},{8,7},{9,8},{10,9},{11,1... | collective-permute-start | bytes 786440 | tf_op jit(solution)/shard_map/ppermute | solution.py:15
Sparse Core Ops, SparseCore 0:
  123.5 57.4 reduce-scatter.3
where the time goes:
time: 190 us; the launch traced here: 189 us
  waiting for transfers between devices  47.4 us (25%)
  blocking collectives  38.4 us (20%)
  matrix products  36.5 us (19%)
  local copies, waits for them, and re-layouts  22.6 us (12%)
  starting transfers between devices  18 us (9%)
  between operations  14.7 us (8%)
  other arithmetic  11.6 us (6%)
    unnamed x2, waiting for transfers between devices  46.2 us
    all_gather x1, blocking collectives, per_device(): lax.all_gather(prompt_values, 'row', axis=0, tiled=True)  20.6 us
    dot_general x16, matrix products, transposed_times(): lax.dot_general(former, latter, (((0,), (0,)), ((), ())), preferred_eleme...  19 us
    ppermute x8, starting transfers between devices, shifted(): return lax.ppermute(x, axis, pairs)  17.9 us
    all_gather x1, blocking collectives, per_device(): lax.all_gather(prompt_keys, 'row', axis=0, tiled=True)  17.8 us
    dot_general x12, matrix products, times_transposed(): lax.dot_general(former, latter, (((1,), (1,)), ((), ())), preferred_eleme...  8.16 us
    dot_general x4, matrix products, per_device(): jnp.dot(head_score_grad, key_rows, preferred_element_type=jnp.float32)  4.85 us
    dot_general x4, matrix products, per_device(): jnp.dot(chances.astype(jnp.bfloat16), value_rows, preferred_element_type=...  4.52 us
  transfers between devices with their start and end apart: 9, of which 2 were waited for; matrix products, arithmetic and copies ran while one was open for 17% of the time, Pallas kernels for 0%

commit v1 on v0

v1 whole, which is shorter than its diff:
```python
import functools
import math

import jax
import jax.numpy as jnp
from jax import lax
from jax.experimental import pallas as pl
from jax.experimental.pallas import tpu as pltpu
from jax.sharding import PartitionSpec as P

HEAD_DIM = 128
MASKED = -1e30
BF16 = jnp.bfloat16
F32 = jnp.float32


def shifted(x, axis, by):
    length = lax.axis_size(axis)
    pairs = [(i, i + by) for i in range(length) if 0 <= i + by < length]
    return lax.ppermute(x, axis, pairs)


def dot_nt(former, latter):
    return lax.dot_general(former, latter, (((1,), (1,)), ((), ())), preferred_element_type=F32)


def dot_nn(former, latter):
    return lax.dot_general(former, latter, (((1,), (0,)), ((), ())), preferred_element_type=F32)


def window_bias(lengths_row, height, heads):
    answers = lengths_row.shape[1]
    before = lax.broadcasted_iota(jnp.int32, (answers, answers), 1) < lax.broadcasted_iota(
        jnp.int32, (answers, answers), 0
    )
    spread = jnp.broadcast_to(lengths_row.astype(F32), (answers, answers))
    starts = jnp.sum(jnp.where(before, spread, 0.0), axis=1, keepdims=True)
    first = lax.axis_index("row") * height
    own = (lax.broadcasted_iota(jnp.int32, (answers, height), 1) + first).astype(F32)
    begin = jnp.max(jnp.where(starts <= own, starts, 0.0), axis=0, keepdims=True)
    shape = (3 * height, height)
    key = (lax.broadcasted_iota(jnp.int32, shape, 0) + (first - 2 * height)).astype(F32)
    row = (lax.broadcasted_iota(jnp.int32, shape, 1) + first).astype(F32)
    bias = jnp.where((key <= row) & (key >= begin), 0.0, MASKED)
    return jnp.concatenate([bias] * heads, axis=1)


def attention_kernel(
    lengths_ref, weights_ref, q_ref, do_ref, pk_ref, pv_ref, fk_ref, fv_ref, nk_ref, nv_ref, ok_ref, ov_ref,
    out_ref, dq_ref, dpk_ref, dpv_ref, far_k_ref, far_v_ref, near_k_ref, near_v_ref, own_k_ref, own_v_ref,
    bias_ref, spread_ref,
):
    height = q_ref.shape[0]
    heads = q_ref.shape[1] // HEAD_DIM
    prompt = pk_ref.shape[0]
    factor = HEAD_DIM**-0.5
    pair = 2

    @pl.when(pl.program_id(0) == 0)
    def _():
        bias_ref[...] = window_bias(lengths_ref[...], height, pair)
        spread_ref[...] = jnp.broadcast_to(weights_ref[...], (HEAD_DIM, height)).T

    keys = jnp.concatenate([pk_ref[...], fk_ref[...], nk_ref[...], ok_ref[...]], axis=0)
    values = jnp.concatenate([pv_ref[...], fv_ref[...], nv_ref[...], ov_ref[...]], axis=0)
    keys_t = keys.astype(F32).T.astype(BF16)
    values_t = values.astype(F32).T.astype(BF16)
    spread = spread_ref[...]
    dk = dv = None
    for h in range(0, heads, pair):
        cols = [slice((h + i) * HEAD_DIM, (h + i + 1) * HEAD_DIM) for i in range(pair)]
        q = jnp.concatenate([q_ref[:, c] for c in cols], axis=0)
        cot = jnp.concatenate([(do_ref[:, c].astype(F32) * spread).astype(BF16) for c in cols], axis=0)
        scores = dot_nt(keys, q)
        scores = jnp.concatenate([scores[:prompt], scores[prompt:] + bias_ref[...]], axis=0)
        highest = jnp.max(scores, axis=0, keepdims=True)
        powers = jnp.exp2((scores - highest) * (factor * math.log2(math.e)))
        total = jnp.sum(powers, axis=0, keepdims=True)
        chances = powers * (1.0 / total)
        rounded = chances.astype(BF16)
        slopes = dot_nt(values, cot)
        delta = jnp.sum(chances * slopes, axis=0, keepdims=True)
        grad = (chances * (slopes - delta)).astype(BF16)
        out = dot_nn(values_t, rounded).T.astype(BF16)
        dq = (dot_nn(keys_t, grad) * factor).T.astype(BF16)
        for i, c in enumerate(cols):
            out_ref[:, c] = out[i * height : (i + 1) * height]
            dq_ref[:, c] = dq[i * height : (i + 1) * height]
        dk_part, dv_part = dot_nn(grad, q), dot_nn(rounded, cot)
        dk, dv = (dk_part, dv_part) if dk is None else (dk + dk_part, dv + dv_part)
    dk = dk * factor
    at = 0
    for k_ref, v_ref in ((dpk_ref, dpv_ref), (far_k_ref, far_v_ref), (near_k_ref, near_v_ref), (own_k_ref, own_v_ref)):
        size = k_ref.shape[0]
        k_ref[...] = dk[at : at + size].astype(k_ref.dtype)
        v_ref[...] = dv[at : at + size].astype(v_ref.dtype)
        at += size


def per_device(
    queries, answer_keys, answer_values, prompt_keys, prompt_values, out_grad, weights, lengths
):
    height = queries.shape[0]
    columns = answer_keys.shape[1]
    kv_heads = columns // HEAD_DIM
    span = queries.shape[1] // kv_heads
    size = lax.axis_size("row")
    own_prompt = prompt_keys.shape[0]
    prompt = own_prompt * size

    own = jnp.concatenate([answer_keys, answer_values], axis=1)
    near, far = shifted(own, "row", 1), shifted(own, "row", 2)
    pair = jnp.concatenate([prompt_keys, prompt_values], axis=1)
    shared = lax.all_to_all(
        jnp.broadcast_to(pair[None], (size, own_prompt, 2 * columns)), "row", 0, 0, tiled=True
    ).reshape(prompt, 2 * columns)

    def key_cols(rows):
        return pl.BlockSpec((rows, HEAD_DIM), lambda g: (0, g))

    def value_cols(rows):
        return pl.BlockSpec((rows, HEAD_DIM), lambda g: (0, g + kv_heads))

    wide = pl.BlockSpec((height, span), lambda g: (0, g))

    def grads(rows, dtype):
        return jax.ShapeDtypeStruct((rows, columns), dtype)

    whole = jax.ShapeDtypeStruct(queries.shape, BF16)
    out, dq, dpk, dpv, fk, fv, nk, nv, ok, ov = pl.pallas_call(
        attention_kernel,
        grid=(kv_heads,),
        in_specs=[
            pl.BlockSpec((1, lengths.shape[0]), lambda g: (0, 0)),
            pl.BlockSpec((1, height), lambda g: (0, 0)),
            wide, wide,
            key_cols(prompt), value_cols(prompt),
            key_cols(height), value_cols(height),
            key_cols(height), value_cols(height),
            key_cols(height), value_cols(height),
        ],
        out_specs=[wide, wide, key_cols(prompt), key_cols(prompt)] + [key_cols(height)] * 6,
        out_shape=[whole, whole] + [grads(prompt, BF16)] * 2 + [grads(height, BF16)] * 4 + [grads(height, F32)] * 2,
        scratch_shapes=[
            pltpu.VMEM((3 * height, 2 * height), F32),
            pltpu.VMEM((height, HEAD_DIM), F32),
        ],
        compiler_params=pltpu.CompilerParams(vmem_limit_bytes=48 * 2**20),
        cost_estimate=pl.CostEstimate(flops=3_200_000_000, bytes_accessed=6_000_000, transcendentals=2_000_000),
    )(
        lengths.reshape(1, -1), weights.reshape(1, -1), queries, out_grad,
        shared, shared, far, far, near, near, own, own,
    )
    terms = jnp.concatenate([dpk, dpv], axis=1).reshape(size, own_prompt, 2 * columns)
    summed = jnp.sum(lax.all_to_all(terms, "row", 0, 0, tiled=True).astype(F32), axis=0)
    from_near = shifted(jnp.concatenate([nk, nv], axis=1), "row", -1).astype(F32)
    from_far = shifted(jnp.concatenate([fk, fv], axis=1), "row", -2).astype(F32)
    dk = (ok + from_near[:, :columns] + from_far[:, :columns]).astype(BF16)
    dv = (ov + from_near[:, columns:] + from_far[:, columns:]).astype(BF16)
    return out, dq, dk, dv, summed[:, :columns], summed[:, columns:]


def solution(mesh):
    rows = P(("grp", "row"), None)
    return jax.shard_map(
        per_device,
        mesh=mesh,
        in_specs=(rows,) * 6 + (P(("grp", "row")), P("grp")),
        out_specs=(rows,) * 6,
        check_vma=False,
    )
```

time: 190 us -> 63.6 us (0.33)
  blocking collectives: 38.4 us -> 0 us
  matrix products: 36.5 us -> 0 us
  waiting for transfers between devices: 47.4 us -> 15.8 us
  local copies, waits for them, and re-layouts: 22.6 us -> 5.07 us
  between operations: 14.7 us -> 0.76 us
  Pallas kernels: 0 us -> 13.3 us
  other arithmetic: 11.6 us -> 2.51 us
  starting transfers between devices: 18 us -> 25.6 us
    unnamed x2 -> x0, waiting for transfers between devices: 46.2 us -> none
    all_gather x2 -> x0, blocking collectives: 38.4 us -> none  [the longest x1 20.6 us: per_device(): lax.all_gather(prompt_values, 'row', axis=0, tiled=True)]
    dot_general x36 -> x0, matrix products: 36.5 us -> none  [the longest x16 19 us: transposed_times(): lax.dot_general(former, latter, (((0,), (0,)), ((), ())), preferred_eleme...]
    all_to_all x0 -> x2, starting transfers between devices: none -> 17.1 us  [the longest x1 9.74 us: per_device(): lax.all_to_all(terms, 'row', 0, 0, tiled=True).astype(F32)]
    pallas_call x0 -> x1, Pallas kernels: none -> 13.3 us  [per_device(): pl.pallas_call(attention_kernel, grid=(kv_heads,), in_specs=[pl.BlockSpec...]
    reshape x20 -> x0, local copies, waits for them, and re-layouts: 9.82 us -> none  [the longest x4 4.04 us: per_device(): record[0].reshape(height, span_cols)]
    ppermute x8 -> x4, starting transfers between devices: 17.9 us -> 8.48 us  [shifted(): return lax.ppermute(x, axis, pairs)]
    all_to_all x0 -> x2, waiting for transfers between devices: none -> 9.11 us  [the longest x1 9.11 us: per_device(): lax.all_to_all(terms, 'row', 0, 0, tiled=True).astype(F32)]
  transfers between devices with their start and end apart: 9 -> 6, of which waited for: 2 -> 2; matrix products, arithmetic and copies ran while one was open for 17% -> 6% of each run, Pallas kernels for 0% -> 0%
where the time goes in v1:
time: 63.6 us; the launch traced here: 63.1 us
  starting transfers between devices  25.6 us (40%)
  waiting for transfers between devices  15.8 us (25%)
  Pallas kernels  13.3 us (21%)
  local copies, waits for them, and re-layouts  5.07 us (8%)
  other arithmetic  2.51 us (4%)
  between operations  0.76 us (1%)
    pallas_call x1, Pallas kernels, per_device(): pl.pallas_call(attention_kernel, grid=(kv_heads,), in_specs=[pl.BlockSpec...  13.3 us
    all_to_all x1, starting transfers between devices, per_device(): lax.all_to_all(terms, 'row', 0, 0, tiled=True).astype(F32)  9.74 us
    all_to_all x1, waiting for transfers between devices, per_device(): lax.all_to_all(terms, 'row', 0, 0, tiled=True).astype(F32)  9.11 us
    ppermute x4, starting transfers between devices, shifted(): return lax.ppermute(x, axis, pairs)  8.48 us
    all_to_all x1, starting transfers between devices, per_device(): lax.all_to_all(jnp.broadcast_to(pair[None], (size, own_prompt, 2 * column...  7.36 us
    ppermute x4, waiting for transfers between devices, shifted(): return lax.ppermute(x, axis, pairs)  6.72 us
    unnamed x9, local copies, waits for them, and re-layouts  2.81 us
  transfers between devices with their start and end apart: 6, of which 2 were waited for; matrix products, arithmetic and copies ran while one was open for 6% of the time, Pallas kernels for 0%

profile of v1, /device:TPU:0, one launch (start us, length us, event | category | flops | bytes accessed | tf_op | source)
XLA Modules:
  0.0 63.1 jit_solution(5109210271141566452)
XLA Ops:
  0.6 0.0 copy-start
  0.6 0.8 %pad_maximum_fusion.2 = bf16[8,1024]{1,0:T(8,128)(2,1)S(1)} fusion(bf16[8,512]{1,0:T(8,128)(2,1)} %param.12, bf16[8,512]{1,0:T(8,128)(2,1)} %param.11), kind=kLoop, calls=%fused_computation.10 | loop fusion | flops 32768 | bytes 32768 | tf_op jit(solution)/shard_map/concatenate | solution.py:113
  1.4 0.7 %broadcast_in_dim.2 = bf16[16,8,1024]{2,1,0:T(8,128)(2,1)} broadcast(bf16[8,1024]{1,0:T(8,128)(2,1)S(1)} %pad_maximum_fusion.2), dimensions={1,2} | broadcast | bytes 278528 | tf_op jit(solution)/shard_map/broadcast_in_dim | solution.py:115
  2.2 7.4 %all-to-all-start = ((bf16[16,8,1024]{2,1,0:T(8,128)(2,1)}), bf16[16,8,1024]{2,1,0:T(8,128)(2,1)S(1)}, u32[]{:S(2)}, u32[]{:S(2)}) async-start(bf16[16,8,1024]{2,1,0:T(8,128)(2,1)} %broadcast_in_dim.2), calls=%async_computation | async-start | bytes 524288 | tf_op jit(solution)/shard_map/all_to_all | solution.py:114
  9.5 0.9 %constant_dynamic-update-slice_fusion.1 = bf16[128,1024]{1,0:T(8,128)(2,1)S(1)} fusion(bf16[128,512]{1,0:T(8,128)(2,1)} %param.9), kind=kLoop, calls=%fused_computation.12 | loop fusion | bytes 262144
  10.5 0.9 %constant_dynamic-update-slice_fusion.ok_ref.ov_ref = bf16[128,1024]{1,0:T(8,128)(2,1)S(1)} fusion(bf16[128,1024]{1,0:T(8,128)(2,1)S(1)} %constant_dynamic-update-slice_fusion.1, bf16[128,512]{1,0:T(8,128)(2,1)} %param.10), kind=kLoop, calls=%fused_computation.11 | loop fusion | bytes 262144 | tf_op jit(solution)/shard_map/concatenate | solution.py:111
  11.4 2.3 %collective-permute-start.1 = (bf16[128,1024]{1,0:T(8,128)(2,1)S(1)}, bf16[128,1024]{1,0:T(8,128)(2,1)S(1)}, u32[]{:S(2)}, u32[]{:S(2)}) collective-permute-start(bf16[128,1024]{1,0:T(8,128)(2,1)S(1)} %constant_dynamic-update-slice_fusion.ok_ref.ov_ref), channel_id=1, source_target_pairs={{0,1},{1,2},{2,3},{3,4},{4,5},{5,6},{6,7},{7,8},{8,9},{9,10},{10,1... | collective-permute-start | bytes 786440 | tf_op jit(solution)/shard_map/ppermute | solution.py:20
  13.7 3.6 %collective-permute-start = (bf16[128,1024]{1,0:T(8,128)(2,1)S(1)}, bf16[128,1024]{1,0:T(8,128)(2,1)S(1)}, u32[]{:S(2)}, u32[]{:S(2)}) collective-permute-start(bf16[128,1024]{1,0:T(8,128)(2,1)S(1)} %constant_dynamic-update-slice_fusion.ok_ref.ov_ref), channel_id=1, source_target_pairs={{0,2},{1,3},{2,4},{3,5},{4,6},{5,7},{6,8},{7,9},{8,10},{9,11},{10,... | collective-permute-start | bytes 786440 | tf_op jit(solution)/shard_map/ppermute | solution.py:20
  17.3 0.0 collective-permute-done.1.nk_ref.nv_ref
  17.3 6.7 %collective-permute-done.fk_ref.fv_ref = bf16[128,1024]{1,0:T(8,128)(2,1)S(1)} collective-permute-done((bf16[128,1024]{1,0:T(8,128)(2,1)S(1)}, bf16[128,1024]{1,0:T(8,128)(2,1)S(1)}, u32[]{:S(2)}, u32[]{:S(2)}) %collective-permute-start) | collective-permute-done | bytes 262176 | tf_op jit(solution)/shard_map/ppermute | solution.py:20
  24.0 0.0 all-to-all-done
  24.0 0.0 copy-start.2
  24.0 0.0 copy-start.3
  24.0 0.0 copy-done
  24.0 0.6 %copy-done.2 = s32[32]{0:T(128)S(1)} copy-done((s32[32]{0:T(128)S(1)}, s32[32]{0:T(128)}, u32[]{:S(2)}) %copy-start.2) | copy-done | bytes 152
  24.7 0.0 copy-done.3
  24.7 0.0 copy-start.1
  24.7 1.2 %copy-done.1 = bf16[128,4096]{1,0:T(8,128)(2,1)S(1)} copy-done((bf16[128,4096]{1,0:T(8,128)(2,1)S(1)}, bf16[128,4096]{1,0:T(8,128)(2,1)}, u32[]{:S(2)}) %copy-start.1) | copy-done | bytes 1048600
  25.9 13.3 %shard_map.127 = (bf16[128,4096]{1,0:T(8,128)(2,1)}, bf16[128,4096]{1,0:T(8,128)(2,1)}, bf16[128,512]{1,0:T(8,128)(2,1)S(1)}, bf16[128,512]{1,0:T(8,128)(2,1)S(1...) custom-call(s32[1,32]{1,0:T(1,128)S(1)} %bitcast.7, ...), custom_call_target="tpu_custom_call" | custom-call | flops 3200000000 | bytes 6000000 | tf_op jit(solution)/shard_map/pallas_call | solution.py:130
  39.3 1.3 %collective-permute-start.3 = (bf16[128,1024]{1,0:T(8,128)(2,1)S(1)}, bf16[128,1024]{1,0:T(8,128)(2,1)S(1)}, u32[]{:S(2)}, u32[]{:S(2)}) collective-permute-start(bf16[128,1024]{1,0:T(8,128)(2,1)S(1)} %pad_maximum_fusion.1), channel_id=1, source_target_pairs={{2,0},{3,1},{4,2},{5,3},{6,4},{7,5},{8,6},{9,7},{10,8},{11,9},{12,... | collective-permute-start | bytes 786440 | tf_op jit(solution)/shard_map/ppermute | solution.py:20
  40.6 1.3 %collective-permute-start.2 = (bf16[128,1024]{1,0:T(8,128)(2,1)S(1)}, bf16[128,1024]{1,0:T(8,128)(2,1)S(1)}, u32[]{:S(2)}, u32[]{:S(2)}) collective-permute-start(bf16[128,1024]{1,0:T(8,128)(2,1)S(1)} %pad_maximum_fusion), channel_id=1, source_target_pairs={{1,0},{2,1},{3,2},{4,3},{5,4},{6,5},{7,6},{8,7},{9,8},{10,9},{11,1... | collective-permute-start | bytes 786440 | tf_op jit(solution)/shard_map/ppermute | solution.py:20
  41.9 0.7 %maximum_bitcast_fusion = bf16[16,8,1024]{2,1,0:T(8,128)(2,1)} fusion(bf16[128,512]{1,0:T(8,128)(2,1)S(1)} %get-tuple-element.25, bf16[128,512]{1,0:T(8,128)(2,1)S(1)} %get-tuple-element.24), kind=kLoop, calls=%fused_computation.9 | loop fusion | flops 524288 | bytes 524288 | tf_op jit(solution)/shard_map/reshape | solution.py:154
  42.6 9.7 %all-to-all-start.1 = ((bf16[16,8,1024]{2,1,0:T(8,128)(2,1)}), bf16[16,8,1024]{2,1,0:T(8,128)(2,1)S(1)}, u32[]{:S(2)}, u32[]{:S(2)}) async-start(bf16[16,8,1024]{2,1,0:T(8,128)(2,1)} %maximum_bitcast_fusion), calls=%async_computation.1 | async-start | bytes 524288 | tf_op jit(solution)/shard_map/all_to_all | solution.py:155
  52.4 0.0 collective-permute-done.3
  52.4 0.0 collective-permute-done.2
  52.5 0.8 %fusion = (bf16[128,512]{1,0:T(8,128)(2,1)}, bf16[128,512]{1,0:T(8,128)(2,1)}) fusion(f32[128,1024]{1,0:T(8,128)S(1)} %convert_element_type.16, f32[128,512]{1,0:T(8,128)S(1)} %get-tuple-element.23, f32[128,1024]{1,0:T(8,128)S(1)} %convert_element_type.15, f32[128,512]{1,0:T(8,128)S(1)} %get-tuple-element.18), kind=kLoop, calls=%fused_computation.2 | loop fusion | flops 393216 | bytes 1835008 | tf_op jit(solution)/shard_map/convert_element_type | solution.py:159
  53.3 9.1 %all-to-all-done.1 = bf16[16,8,1024]{2,1,0:T(8,128)(2,1)S(1)} async-done(((bf16[16,8,1024]{2,1,0:T(8,128)(2,1)}), bf16[16,8,1024]{2,1,0:T(8,128)(2,1)S(1)}, u32[]{:S(2)}, u32[]{:S(2)}) %all-to-all-start.1) | async-done | bytes 262176 | tf_op jit(solution)/shard_map/all_to_all | solution.py:155
  62.4 0.6 fusion.2
  (5 shorter events, 0.2 us)
Async XLA Ops:
  0.6 23.4 %copy-start = (bf16[128,4096]{1,0:T(8,128)(2,1)S(1)}, bf16[128,4096]{1,0:T(8,128)(2,1)}, u32[]{:S(2)}) copy-start(bf16[128,4096]{1,0:T(8,128)(2,1)} %q_ref.1) | copy-start | bytes 3145732
  2.2 21.8 %all-to-all-start = ((bf16[16,8,1024]{2,1,0:T(8,128)(2,1)}), bf16[16,8,1024]{2,1,0:T(8,128)(2,1)S(1)}, u32[]{:S(2)}, u32[]{:S(2)}) async-start(bf16[16,8,1024]{2,1,0:T(8,128)(2,1)} %broadcast_in_dim.2), calls=%async_computation | async-start | bytes 524288 | tf_op jit(solution)/shard_map/all_to_all | solution.py:114
  11.4 5.9 %collective-permute-start.1 = (bf16[128,1024]{1,0:T(8,128)(2,1)S(1)}, bf16[128,1024]{1,0:T(8,128)(2,1)S(1)}, u32[]{:S(2)}, u32[]{:S(2)}) collective-permute-start(bf16[128,1024]{1,0:T(8,128)(2,1)S(1)} %constant_dynamic-update-slice_fusion.ok_ref.ov_ref), channel_id=1, source_target_pairs={{0,1},{1,2},{2,3},{3,4},{4,5},{5,6},{6,7},{7,8},{8,9},{9,10},{10,1... | collective-permute-start | bytes 786440 | tf_op jit(solution)/shard_map/ppermute | solution.py:20
  13.7 10.3 %collective-permute-start = (bf16[128,1024]{1,0:T(8,128)(2,1)S(1)}, bf16[128,1024]{1,0:T(8,128)(2,1)S(1)}, u32[]{:S(2)}, u32[]{:S(2)}) collective-permute-start(bf16[128,1024]{1,0:T(8,128)(2,1)S(1)} %constant_dynamic-update-slice_fusion.ok_ref.ov_ref), channel_id=1, source_target_pairs={{0,2},{1,3},{2,4},{3,5},{4,6},{5,7},{6,8},{7,9},{8,10},{9,11},{10,... | collective-permute-start | bytes 786440 | tf_op jit(solution)/shard_map/ppermute | solution.py:20
  24.0 0.7 %copy-start.2 = (s32[32]{0:T(128)S(1)}, s32[32]{0:T(128)}, u32[]{:S(2)}) copy-start(s32[32]{0:T(128)} %param.15) | copy-start | bytes 388
  24.0 0.7 %copy-start.3 = (f32[128]{0:T(128)S(1)}, f32[128]{0:T(128)}, u32[]{:S(2)}) copy-start(f32[128]{0:T(128)} %param.14) | copy-start | bytes 1540
  24.7 1.2 %copy-start.1 = (bf16[128,4096]{1,0:T(8,128)(2,1)S(1)}, bf16[128,4096]{1,0:T(8,128)(2,1)}, u32[]{:S(2)}) copy-start(bf16[128,4096]{1,0:T(8,128)(2,1)} %do_ref.1) | copy-start | bytes 3145732
  39.3 13.1 %collective-permute-start.3 = (bf16[128,1024]{1,0:T(8,128)(2,1)S(1)}, bf16[128,1024]{1,0:T(8,128)(2,1)S(1)}, u32[]{:S(2)}, u32[]{:S(2)}) collective-permute-start(bf16[128,1024]{1,0:T(8,128)(2,1)S(1)} %pad_maximum_fusion.1), channel_id=1, source_target_pairs={{2,0},{3,1},{4,2},{5,3},{6,4},{7,5},{8,6},{9,7},{10,8},{11,9},{12,... | collective-permute-start | bytes 786440 | tf_op jit(solution)/shard_map/ppermute | solution.py:20
  40.6 11.8 %collective-permute-start.2 = (bf16[128,1024]{1,0:T(8,128)(2,1)S(1)}, bf16[128,1024]{1,0:T(8,128)(2,1)S(1)}, u32[]{:S(2)}, u32[]{:S(2)}) collective-permute-start(bf16[128,1024]{1,0:T(8,128)(2,1)S(1)} %pad_maximum_fusion), channel_id=1, source_target_pairs={{1,0},{2,1},{3,2},{4,3},{5,4},{6,5},{7,6},{8,7},{9,8},{10,9},{11,1... | collective-permute-start | bytes 786440 | tf_op jit(solution)/shard_map/ppermute | solution.py:20
  42.6 19.8 %all-to-all-start.1 = ((bf16[16,8,1024]{2,1,0:T(8,128)(2,1)}), bf16[16,8,1024]{2,1,0:T(8,128)(2,1)S(1)}, u32[]{:S(2)}, u32[]{:S(2)}) async-start(bf16[16,8,1024]{2,1,0:T(8,128)(2,1)} %maximum_bitcast_fusion), calls=%async_computation.1 | async-start | bytes 524288 | tf_op jit(solution)/shard_map/all_to_all | solution.py:155

commit v2 on v1

v2 whole, which is shorter than its diff:
```python
import math

import jax
import jax.numpy as jnp
from jax import lax
from jax.experimental import pallas as pl
from jax.experimental.pallas import tpu as pltpu
from jax.sharding import PartitionSpec as P

HEAD_DIM = 128
PARTS = 4
FACTOR = HEAD_DIM**-0.5
EXPONENT = FACTOR * math.log2(math.e)
MASKED = -1e30
BF16 = jnp.bfloat16
F32 = jnp.float32
VMEM_LIMIT = 60 * 2**20


def shifted(x, by):
    length = lax.axis_size("row")
    pairs = [(i, i + by) for i in range(length) if 0 <= i + by < length]
    return lax.ppermute(x, "row", pairs)


def dot_nt(former, latter):
    return lax.dot_general(former, latter, (((1,), (1,)), ((), ())), preferred_element_type=F32)


def dot_nn(former, latter):
    return lax.dot_general(former, latter, (((1,), (0,)), ((), ())), preferred_element_type=F32)


def transposed(x):
    return x.astype(F32).T.astype(BF16)


def window_bias(lengths_row, height, heads, part):
    answers = lengths_row.shape[1]
    rows = height // PARTS
    before = lax.broadcasted_iota(jnp.int32, (answers, answers), 1) < lax.broadcasted_iota(
        jnp.int32, (answers, answers), 0
    )
    spread = jnp.broadcast_to(lengths_row.astype(F32), (answers, answers))
    starts = jnp.sum(jnp.where(before, spread, 0.0), axis=1, keepdims=True)
    first = lax.axis_index("row") * height + part * rows
    lane = lax.broadcasted_iota(jnp.int32, (1, heads * rows), 1)
    own = (lax.rem(lane, rows) + first).astype(F32)
    begin = jnp.max(jnp.where(starts <= own, starts, 0.0), axis=0, keepdims=True)
    shape = (2 * height + rows, heads * rows)
    key = (lax.broadcasted_iota(jnp.int32, shape, 0) + (first - 2 * height)).astype(F32)
    return jnp.where((key <= own) & (key >= begin), 0.0, MASKED)


def flat_part(ref, part):
    rows = ref.shape[0] // PARTS
    heads = ref.shape[1] // HEAD_DIM
    return jnp.concatenate(
        [ref[part * rows : (part + 1) * rows, h * HEAD_DIM : (h + 1) * HEAD_DIM] for h in range(heads)], axis=0
    )


def store_part(ref, part, value):
    rows = ref.shape[0] // PARTS
    for h in range(ref.shape[1] // HEAD_DIM):
        ref[part * rows : (part + 1) * rows, h * HEAD_DIM : (h + 1) * HEAD_DIM] = value[h * rows : (h + 1) * rows]


def staged(*stages):
    held = {}
    for step in range(PARTS + len(stages) - 1):
        for place, stage in enumerate(stages):
            part = step - place
            if 0 <= part < PARTS:
                held[part] = stage(part, held.get(part))


def pack_kernel(k_ref, v_ref, pk_ref, pv_ref, own_ref, spread_ref):
    own_ref[...] = jnp.concatenate([k_ref[...], v_ref[...]], axis=1)
    pair = jnp.concatenate([pk_ref[...], pv_ref[...]], axis=1)
    spread_ref[...] = jnp.broadcast_to(pair[None], spread_ref.shape)


def attention_kernel(n_near, *refs):
    lengths_ref, weights_ref, q_ref, do_ref, pk_ref, pv_ref, fk_ref, fv_ref, *rest = refs
    near, rest = rest[: 2 * n_near], rest[2 * n_near :]
    ok_ref, ov_ref, out_ref, dq_ref, terms_ref, far_ref, near_ref, own_ref, bias_ref, spread_ref, dk_ref, dv_ref = rest
    height = q_ref.shape[0]
    heads = q_ref.shape[1] // HEAD_DIM
    prompt = pk_ref.shape[0]
    rows = height // PARTS
    window = 2 * height + rows
    kv_heads = own_ref.shape[1] // (2 * HEAD_DIM)

    @pl.when(pl.program_id(0) == 0)
    def _():
        for part in range(PARTS):
            bias_ref[part] = window_bias(lengths_ref[...], height, heads, part)
        spread_ref[...] = jnp.broadcast_to(weights_ref[...], (HEAD_DIM, height)).T

    nk, nv = near[0][...], near[1][...]
    for i in range(1, n_near):
        nk, nv = nk + near[2 * i][...], nv + near[2 * i + 1][...]
    keys = jnp.concatenate([pk_ref[...], fk_ref[...], nk, ok_ref[...]], axis=0)
    values = jnp.concatenate([pv_ref[...], fv_ref[...], nv, ov_ref[...]], axis=0)
    keys_t, values_t = transposed(keys), transposed(values)
    dk_ref[...] = jnp.zeros_like(dk_ref)
    dv_ref[...] = jnp.zeros_like(dv_ref)

    def reachable(x, part):
        begin = prompt + part * rows
        return jnp.concatenate([x[:prompt], x[begin : begin + window]], axis=0)

    def everywhere(x, part):
        before, after = part * rows, height - (part + 1) * rows
        pieces = [x[:prompt], jnp.zeros((before, x.shape[1]), x.dtype), x[prompt:], jnp.zeros((after, x.shape[1]), x.dtype)]
        return jnp.concatenate([piece for piece in pieces if piece.shape[0]], axis=0)

    def score(part, _):
        q, cot = flat_part(q_ref, part), flat_part(do_ref, part)
        spread = jnp.concatenate([spread_ref[part * rows : (part + 1) * rows]] * heads, axis=0)
        cot = (cot.astype(F32) * spread).astype(BF16)
        return q, cot, dot_nt(reachable(keys, part), q), dot_nt(reachable(values, part), cot)

    def weigh(part, held):
        q, cot, scores, slopes = held
        scores = jnp.concatenate([scores[:prompt], scores[prompt:] + bias_ref[part]], axis=0)
        highest = jnp.max(scores, axis=0, keepdims=True)
        powers = jnp.exp2((scores - highest) * EXPONENT)
        chances = powers * (1.0 / jnp.sum(powers, axis=0, keepdims=True))
        delta = jnp.sum(chances * slopes, axis=0, keepdims=True)
        return q, cot, chances.astype(BF16), (chances * (slopes - delta)).astype(BF16)

    def gather(part, held):
        q, cot, chances, grad = held
        store_part(out_ref, part, dot_nn(values_t, everywhere(chances, part)).T.astype(BF16))
        store_part(dq_ref, part, (dot_nn(keys_t, everywhere(grad, part)) * FACTOR).T.astype(BF16))
        begin = prompt + part * rows
        for ref, terms in ((dk_ref, dot_nn(grad, q)), (dv_ref, dot_nn(chances, cot))):
            ref[:prompt] += terms[:prompt]
            ref[begin : begin + window] += terms[prompt:]

    staged(score, weigh, gather)
    g = pl.program_id(0)
    at = 0
    for ref in (terms_ref, far_ref, near_ref, own_ref):
        end = at + ref.shape[0]
        ref[:, pl.ds(pl.multiple_of(g * HEAD_DIM, HEAD_DIM), HEAD_DIM)] = (dk_ref[at:end] * FACTOR).astype(ref.dtype)
        ref[:, pl.ds(pl.multiple_of((g + kv_heads) * HEAD_DIM, HEAD_DIM), HEAD_DIM)] = dv_ref[at:end].astype(ref.dtype)
        at = end


def per_device(
    queries, answer_keys, answer_values, prompt_keys, prompt_values, out_grad, weights, lengths
):
    height = queries.shape[0]
    columns = answer_keys.shape[1]
    kv_heads = columns // HEAD_DIM
    span = queries.shape[1] // kv_heads
    flat = height * queries.shape[1] // HEAD_DIM
    size = lax.axis_size("row")
    own_prompt = prompt_keys.shape[0]
    prompt = own_prompt * size
    window = 2 * height + height // PARTS

    def shape(rows, cols, dtype=BF16):
        return jax.ShapeDtypeStruct((rows, cols), dtype)

    def key_cols(rows):
        return pl.BlockSpec((rows, HEAD_DIM), lambda g: (0, g))

    def value_cols(rows):
        return pl.BlockSpec((rows, HEAD_DIM), lambda g: (0, g + kv_heads))

    def fixed(rows, cols):
        return pl.BlockSpec((rows, cols), lambda g: (0, 0))

    wide = pl.BlockSpec((height, span), lambda g: (0, g))

    own, spread = pl.pallas_call(
        pack_kernel,
        out_shape=[shape(height, 2 * columns), jax.ShapeDtypeStruct((size, own_prompt, 2 * columns), BF16)],
    )(answer_keys, answer_values, prompt_keys, prompt_values)
    far = shifted(own, 2)
    if size % 2 == 0:
        near = [
            lax.ppermute(own, "row", [(i, i + 1) for i in range(0, size, 2)]),
            lax.ppermute(far, "row", [(i + 1, i) for i in range(0, size, 2)]),
        ]
    else:
        near = [shifted(own, 1)]
    shared = lax.all_to_all(spread, "row", 0, 0, tiled=True).reshape(prompt, 2 * columns)

    k_block, v_block = key_cols(height), value_cols(height)
    near_ins = [pair for part in near for pair in ((k_block, part), (v_block, part))]
    ins = [
        (fixed(1, lengths.shape[0]), lengths.reshape(1, -1)),
        (fixed(1, height), weights.reshape(1, -1)),
        (wide, queries), (wide, out_grad), (key_cols(prompt), shared), (value_cols(prompt), shared),
        (k_block, far), (v_block, far), *near_ins, (k_block, own), (v_block, own),
    ]
    outs = [
        (wide, shape(*queries.shape)),
        (wide, shape(*queries.shape)),
        (fixed(prompt, 2 * columns), shape(prompt, 2 * columns)),
        (fixed(height, 2 * columns), shape(height, 2 * columns)),
        (fixed(height, 2 * columns), shape(height, 2 * columns)),
        (fixed(height, 2 * columns), shape(height, 2 * columns, F32)),
    ]
    attn_out, q_grad, terms, far_terms, near_terms, own_terms = pl.pallas_call(
        lambda *refs: attention_kernel(len(near), *refs),
        grid=(kv_heads,),
        in_specs=[spec for spec, _ in ins],
        out_specs=[spec for spec, _ in outs],
        out_shape=[kind for _, kind in outs],
        scratch_shapes=[
            pltpu.VMEM((PARTS, window, flat // kv_heads // PARTS), F32),
            pltpu.VMEM((height, HEAD_DIM), F32),
            pltpu.VMEM((prompt + 3 * height, HEAD_DIM), F32),
            pltpu.VMEM((prompt + 3 * height, HEAD_DIM), F32),
        ],
        compiler_params=pltpu.CompilerParams(vmem_limit_bytes=VMEM_LIMIT),
        cost_estimate=pl.CostEstimate(
            flops=12 * flat * (prompt + window) * HEAD_DIM, bytes_accessed=6_000_000, transcendentals=2_000_000
        ),
    )(*[array for _, array in ins])
    arrived = lax.all_to_all(terms.reshape(size, own_prompt, 2 * columns), "row", 0, 0, tiled=True)
    from_far, from_near = shifted(far_terms, -2), shifted(near_terms, -1)
    window_grad = (own_terms + from_near.astype(F32) + from_far.astype(F32)).astype(BF16)
    summed = jnp.sum(arrived.astype(F32), axis=0)
    return (
        attn_out, q_grad, window_grad[:, :columns], window_grad[:, columns:], summed[:, :columns], summed[:, columns:],
    )


def solution(mesh):
    rows = P(("grp", "row"), None)
    return jax.shard_map(
        per_device,
        mesh=mesh,
        in_specs=(rows,) * 6 + (P(("grp", "row")), P("grp")),
        out_specs=(rows,) * 6,
        check_vma=False,
    )
```

time: 63.6 us -> 53 us (0.83)
  starting transfers between devices: 25.6 us -> 22.3 us
  local copies, waits for them, and re-layouts: 5.07 us -> 2.14 us
  other arithmetic: 2.51 us -> 0.14 us
  Pallas kernels: 13.3 us -> 11.5 us
    all_to_all x2, starting transfers between devices: 17.1 us -> 11.1 us  [the longest x1 6.04 us: per_device(): lax.all_to_all(terms.reshape(size, own_prompt, 2 * columns), 'row', 0, 0,...]
    ppermute x4 -> x5, starting transfers between devices: 8.48 us -> 11.2 us  [the longest x3 7.56 us: shifted(): return lax.ppermute(x, 'row', pairs)]
    unnamed x9 -> x12, local copies, waits for them, and re-layouts: 2.81 us -> 0.81 us
    pallas_call x1 -> x2, Pallas kernels: 13.3 us -> 11.5 us  [the longest x1 9.74 us: per_device(): pl.pallas_call(lambda *refs: attention_kernel(len(near), *refs), grid=(kv...]
    concatenate x1 -> x0, local copies, waits for them, and re-layouts: 0.92 us -> none  [per_device(): own = jnp.concatenate([answer_keys, answer_values], axis=1)]
    concatenate x3 -> x0, other arithmetic: 0.84 us -> none  [the longest x1 0.8 us: per_device(): pair = jnp.concatenate([prompt_keys, prompt_values], axis=1)]
    convert_element_type x3 -> x1, other arithmetic: 0.9 us -> 0.1 us  [per_device(): (own_terms + from_near.astype(F32) + from_far.astype(F32)).astype(BF16)]
    reshape x1 -> x0, other arithmetic: 0.73 us -> none  [per_device(): jnp.concatenate([dpk, dpv], axis=1).reshape(size, own_prompt, 2 * columns)]
  transfers between devices with their start and end apart: 6 -> 7, of which waited for: 2 -> 3; matrix products, arithmetic and copies ran while one was open for 6% -> 2% of each run, Pallas kernels for 0% -> 0%
where the time goes in v2:
time: 53 us; the launch traced here: 52.5 us
  starting transfers between devices  22.3 us (42%)
  waiting for transfers between devices  15.6 us (29%)
  Pallas kernels  11.5 us (22%)
  local copies, waits for them, and re-layouts  2.14 us (4%)
  between operations  0.78 us (1%)
    pallas_call x1, Pallas kernels, per_device(): pl.pallas_call(lambda *refs: attention_kernel(len(near), *refs), grid=(kv...  9.74 us
    ppermute x3, starting transfers between devices, shifted(): return lax.ppermute(x, 'row', pairs)  7.56 us
    all_to_all x1, waiting for transfers between devices, per_device(): lax.all_to_all(spread, 'row', 0, 0, tiled=True).reshape(prompt, 2 * columns)  6.36 us
    ppermute x3, waiting for transfers between devices, shifted(): return lax.ppermute(x, 'row', pairs)  6.35 us
    all_to_all x1, starting transfers between devices, per_device(): lax.all_to_all(terms.reshape(size, own_prompt, 2 * columns), 'row', 0, 0,...  6.04 us
    all_to_all x1, starting transfers between devices, per_device(): lax.all_to_all(spread, 'row', 0, 0, tiled=True).reshape(prompt, 2 * columns)  5.11 us
    all_to_all x1, waiting for transfers between devices, per_device(): lax.all_to_all(terms.reshape(size, own_prompt, 2 * columns), 'row', 0, 0,...  2.86 us
    ppermute x1, starting transfers between devices, per_device(): lax.ppermute(own, 'row', [(i, i + 1) for i in range(0, size, 2)])  2.33 us
  transfers between devices with their start and end apart: 7, of which 3 were waited for; matrix products, arithmetic and copies ran while one was open for 2% of the time, Pallas kernels for 0%

profile of v2, /device:TPU:0, one launch (start us, length us, event | category | flops | bytes accessed | tf_op | source)
XLA Modules:
  0.0 52.5 jit_solution(10103097550747480169)
XLA Ops:
  0.6 1.8 %shard_map.127 = (bf16[128,1024]{1,0:T(8,128)(2,1)}, bf16[16,8,1024]{2,1,0:T(8,128)(2,1)}) custom-call(bf16[128,512]{1,0:T(8,128)(2,1)} %k_ref.1, bf16[128,512]{1,0:T(8,128)(2,1)} %v_ref.1, bf16[8,512]{1,0:T(8,128)(2,1)} %pk_ref.1, bf16[8,512]{1,0:T(8,128)(2,1)} %pv_ref.1), custom_call_target="tpu_custom_call" | custom-call | tf_op jit(solution)/shard_map/pallas_call | solution.py:180
  2.4 4.8 %collective-permute-start = (bf16[128,1024]{1,0:T(8,128)(2,1)}, bf16[128,1024]{1,0:T(8,128)(2,1)S(1)}, u32[]{:S(2)}, u32[]{:S(2)}) collective-permute-start(bf16[128,1024]{1,0:T(8,128)(2,1)} %get-tuple-element.15.refs_12_.refs_13_), channel_id=1, source_target_pairs={{0,2},{1,3},{2,4},{3,5},{4,6},{5,7},{6,8},{7,9},{8,10},{9,11},{10,... | collective-permute-start | bytes 786440 | tf_op jit(solution)/shard_map/ppermute | solution.py:23
  7.3 0.0 copy-start.2
  7.3 5.1 %all-to-all-start = ((bf16[16,8,1024]{2,1,0:T(8,128)(2,1)}), bf16[16,8,1024]{2,1,0:T(8,128)(2,1)S(1)}, u32[]{:S(2)}, u32[]{:S(2)}) async-start(bf16[16,8,1024]{2,1,0:T(8,128)(2,1)} %get-tuple-element.14), calls=%async_computation | async-start | bytes 524288 | tf_op jit(solution)/shard_map/all_to_all | solution.py:192
  12.4 0.0 copy-done.2
  12.4 2.3 %collective-permute-start.1 = (bf16[128,1024]{1,0:T(8,128)(2,1)S(1)}, bf16[128,1024]{1,0:T(8,128)(2,1)S(1)}, u32[]{:S(2)}, u32[]{:S(2)}) collective-permute-start(bf16[128,1024]{1,0:T(8,128)(2,1)S(1)} %copy-done.2), channel_id=1, source_target_pairs={{0,1},{2,3},{4,5},{6,7},{8,9},{10,11},{12,13},{14,15},{16,17},{18,... | collective-permute-start | bytes 786440 | tf_op jit(solution)/shard_map/ppermute | solution.py:187
  14.7 0.0 collective-permute-done.refs_6_.refs_7_
  14.8 0.0 copy-start.3
  14.8 1.3 %collective-permute-start.2 = (bf16[128,1024]{1,0:T(8,128)(2,1)S(1)}, bf16[128,1024]{1,0:T(8,128)(2,1)S(1)}, u32[]{:S(2)}, u32[]{:S(2)}) collective-permute-start(bf16[128,1024]{1,0:T(8,128)(2,1)S(1)} %collective-permute-done.refs_6_.refs_7_), channel_id=1, source_target_pairs={{1,0},{3,2},{5,4},{7,6},{9,8},{11,10},{13,12},{15,14},{17,16},{19,... | collective-permute-start | bytes 786440 | tf_op jit(solution)/shard_map/ppermute | solution.py:188
  16.1 0.0 collective-permute-done.1.refs_8_.refs_9_
  16.1 0.0 copy-start.4
  16.1 6.4 %all-to-all-done = bf16[16,8,1024]{2,1,0:T(8,128)(2,1)S(1)} async-done(((bf16[16,8,1024]{2,1,0:T(8,128)(2,1)}), bf16[16,8,1024]{2,1,0:T(8,128)(2,1)S(1)}, u32[]{:S(2)}, u32[]{:S(2)}) %all-to-all-start) | async-done | bytes 262176 | tf_op jit(solution)/shard_map/all_to_all | solution.py:192
  22.4 0.0 copy-start.1
  22.4 0.0 collective-permute-done.2.refs_10_.refs_11_
  22.5 0.0 copy-start.5
  22.5 0.0 copy-done.3
  22.5 0.0 copy-done.4
  22.5 0.7 %copy-done.1 = bf16[16,8,1024]{2,1,0:T(8,128)(2,1)} copy-done((bf16[16,8,1024]{2,1,0:T(8,128)(2,1)}, bf16[16,8,1024]{2,1,0:T(8,128)(2,1)S(1)}, u32[]{:S(2)}) %copy-start.1) | copy-done | bytes 262168
  23.2 0.1 copy-done.5
  23.3 9.7 %shard_map.128 = (bf16[128,4096]{1,0:T(8,128)(2,1)}, bf16[128,4096]{1,0:T(8,128)(2,1)}, bf16[128,1024]{1,0:T(8,128)(2,1)}, bf16[128,1024]{1,0:T(8,128)(2,1)}, bf...) custom-call(s32[1,32]{1,0:T(1,128)} %bitcast.7, f32[1,128]{1,0:T(1,128)} %bitcast.8, bf16[128,4096]{1,0:T(8,128)(2,1)} %refs_2_.1, ...), custom_call_target="tpu_custom_call" | custom-call | flops 2617245696 | bytes 6000000 | tf_op jit(solution)/shard_map/pallas_call | solution.py:210
  33.0 0.0 copy-start
  33.0 1.4 %collective-permute-start.3 = (bf16[128,1024]{1,0:T(8,128)(2,1)}, bf16[128,1024]{1,0:T(8,128)(2,1)S(1)}, u32[]{:S(2)}, u32[]{:S(2)}) collective-permute-start(bf16[128,1024]{1,0:T(8,128)(2,1)} %get-tuple-element.19), channel_id=1, source_target_pairs={{1,0},{2,1},{3,2},{4,3},{5,4},{6,5},{7,6},{8,7},{9,8},{10,9},{11,1... | collective-permute-start | bytes 786440 | tf_op jit(solution)/shard_map/ppermute | solution.py:23
  34.4 1.3 %collective-permute-start.4 = (bf16[128,1024]{1,0:T(8,128)(2,1)}, bf16[128,1024]{1,0:T(8,128)(2,1)S(1)}, u32[]{:S(2)}, u32[]{:S(2)}) collective-permute-start(bf16[128,1024]{1,0:T(8,128)(2,1)} %get-tuple-element.20), channel_id=1, source_target_pairs={{2,0},{3,1},{4,2},{5,3},{6,4},{7,5},{8,6},{9,7},{10,8},{11,9},{12,... | collective-permute-start | bytes 786440 | tf_op jit(solution)/shard_map/ppermute | solution.py:23
  35.7 6.0 %all-to-all-start.1 = ((bf16[16,8,1024]{2,1,0:T(8,128)(2,1)}), bf16[16,8,1024]{2,1,0:T(8,128)(2,1)S(1)}, u32[]{:S(2)}, u32[]{:S(2)}) async-start(bf16[16,8,1024]{2,1,0:T(8,128)(2,1)} %bitcast.4), calls=%async_computation.1 | async-start | bytes 524288 | tf_op jit(solution)/shard_map/all_to_all | solution.py:227
  41.8 0.0 collective-permute-done.3
  41.8 6.3 %collective-permute-done.4 = bf16[128,1024]{1,0:T(8,128)(2,1)S(1)} collective-permute-done((bf16[128,1024]{1,0:T(8,128)(2,1)}, bf16[128,1024]{1,0:T(8,128)(2,1)S(1)}, u32[]{:S(2)}, u32[]{:S(2)}) %collective-permute-start.4) | collective-permute-done | bytes 262176 | tf_op jit(solution)/shard_map/ppermute | solution.py:23
  48.2 0.0 copy-done
  48.2 0.1 add_convert_fusion
  48.3 0.7 %fusion = (bf16[128,512]{1,0:T(8,128)(2,1)}, bf16[128,512]{1,0:T(8,128)(2,1)}) fusion(bf16[128,1024]{1,0:T(8,128)(2,1)S(1)} %add_convert_fusion), kind=kLoop, calls=%fused_computation.2 | loop fusion | bytes 524288 | tf_op jit(solution)/shard_map/slice | solution.py:232
  49.0 2.9 %all-to-all-done.1 = bf16[16,8,1024]{2,1,0:T(8,128)(2,1)S(1)} async-done(((bf16[16,8,1024]{2,1,0:T(8,128)(2,1)}), bf16[16,8,1024]{2,1,0:T(8,128)(2,1)S(1)}, u32[]{:S(2)}, u32[]{:S(2)}) %all-to-all-start.1) | async-done | bytes 262176 | tf_op jit(solution)/shard_map/all_to_all | solution.py:227
  51.9 0.6 %fusion.1 = (f32[8,512]{1,0:T(8,128)}, f32[8,512]{1,0:T(8,128)}) fusion(f32[8,1024]{1,0:T(8,128)S(1)} %convert_reduce_fusion), kind=kLoop, calls=%fused_computation.3 | loop fusion | bytes 65536 | tf_op jit(solution)/shard_map/slice | solution.py:232
  (1 shorter events, 0.0 us)
Async XLA Ops:
  2.4 12.3 %collective-permute-start = (bf16[128,1024]{1,0:T(8,128)(2,1)}, bf16[128,1024]{1,0:T(8,128)(2,1)S(1)}, u32[]{:S(2)}, u32[]{:S(2)}) collective-permute-start(bf16[128,1024]{1,0:T(8,128)(2,1)} %get-tuple-element.15.refs_12_.refs_13_), channel_id=1, source_target_pairs={{0,2},{1,3},{2,4},{3,5},{4,6},{5,7},{6,8},{7,9},{8,10},{9,11},{10,... | collective-permute-start | bytes 786440 | tf_op jit(solution)/shard_map/ppermute | solution.py:23
  7.3 5.1 %copy-start.2 = (bf16[128,1024]{1,0:T(8,128)(2,1)S(1)}, bf16[128,1024]{1,0:T(8,128)(2,1)}, u32[]{:S(2)}) copy-start(bf16[128,1024]{1,0:T(8,128)(2,1)} %get-tuple-element.15.refs_12_.refs_13_) | copy-start | bytes 786436
  7.3 15.2 %all-to-all-start = ((bf16[16,8,1024]{2,1,0:T(8,128)(2,1)}), bf16[16,8,1024]{2,1,0:T(8,128)(2,1)S(1)}, u32[]{:S(2)}, u32[]{:S(2)}) async-start(bf16[16,8,1024]{2,1,0:T(8,128)(2,1)} %get-tuple-element.14), calls=%async_computation | async-start | bytes 524288 | tf_op jit(solution)/shard_map/all_to_all | solution.py:192
  12.4 3.7 %collective-permute-start.1 = (bf16[128,1024]{1,0:T(8,128)(2,1)S(1)}, bf16[128,1024]{1,0:T(8,128)(2,1)S(1)}, u32[]{:S(2)}, u32[]{:S(2)}) collective-permute-start(bf16[128,1024]{1,0:T(8,128)(2,1)S(1)} %copy-done.2), channel_id=1, source_target_pairs={{0,1},{2,3},{4,5},{6,7},{8,9},{10,11},{12,13},{14,15},{16,17},{18,... | collective-permute-start | bytes 786440 | tf_op jit(solution)/shard_map/ppermute | solution.py:187
  14.8 7.7 %copy-start.3 = (bf16[128,1024]{1,0:T(8,128)(2,1)}, bf16[128,1024]{1,0:T(8,128)(2,1)S(1)}, u32[]{:S(2)}) copy-start(bf16[128,1024]{1,0:T(8,128)(2,1)S(1)} %collective-permute-done.refs_6_.refs_7_) | copy-start | bytes 786436
  14.8 7.7 %collective-permute-start.2 = (bf16[128,1024]{1,0:T(8,128)(2,1)S(1)}, bf16[128,1024]{1,0:T(8,128)(2,1)S(1)}, u32[]{:S(2)}, u32[]{:S(2)}) collective-permute-start(bf16[128,1024]{1,0:T(8,128)(2,1)S(1)} %collective-permute-done.refs_6_.refs_7_), channel_id=1, source_target_pairs={{1,0},{3,2},{5,4},{7,6},{9,8},{11,10},{13,12},{15,14},{17,16},{19,... | collective-permute-start | bytes 786440 | tf_op jit(solution)/shard_map/ppermute | solution.py:188
  16.1 6.4 %copy-start.4 = (bf16[128,1024]{1,0:T(8,128)(2,1)}, bf16[128,1024]{1,0:T(8,128)(2,1)S(1)}, u32[]{:S(2)}) copy-start(bf16[128,1024]{1,0:T(8,128)(2,1)S(1)} %collective-permute-done.1.refs_8_.refs_9_) | copy-start | bytes 786436
  22.4 0.7 %copy-start.1 = (bf16[16,8,1024]{2,1,0:T(8,128)(2,1)}, bf16[16,8,1024]{2,1,0:T(8,128)(2,1)S(1)}, u32[]{:S(2)}) copy-start(bf16[16,8,1024]{2,1,0:T(8,128)(2,1)S(1)} %all-to-all-done) | copy-start | bytes 786436
  22.5 0.8 %copy-start.5 = (bf16[128,1024]{1,0:T(8,128)(2,1)}, bf16[128,1024]{1,0:T(8,128)(2,1)S(1)}, u32[]{:S(2)}) copy-start(bf16[128,1024]{1,0:T(8,128)(2,1)S(1)} %collective-permute-done.2.refs_10_.refs_11_) | copy-start | bytes 786436
  33.0 15.1 %copy-start = (f32[128,1024]{1,0:T(8,128)S(1)}, f32[128,1024]{1,0:T(8,128)}, u32[]{:S(2)}) copy-start(f32[128,1024]{1,0:T(8,128)} %get-tuple-element.18) | copy-start | bytes 1572868
  33.0 8.8 %collective-permute-start.3 = (bf16[128,1024]{1,0:T(8,128)(2,1)}, bf16[128,1024]{1,0:T(8,128)(2,1)S(1)}, u32[]{:S(2)}, u32[]{:S(2)}) collective-permute-start(bf16[128,1024]{1,0:T(8,128)(2,1)} %get-tuple-element.19), channel_id=1, source_target_pairs={{1,0},{2,1},{3,2},{4,3},{5,4},{6,5},{7,6},{8,7},{9,8},{10,9},{11,1... | collective-permute-start | bytes 786440 | tf_op jit(solution)/shard_map/ppermute | solution.py:23
  34.4 13.7 %collective-permute-start.4 = (bf16[128,1024]{1,0:T(8,128)(2,1)}, bf16[128,1024]{1,0:T(8,128)(2,1)S(1)}, u32[]{:S(2)}, u32[]{:S(2)}) collective-permute-start(bf16[128,1024]{1,0:T(8,128)(2,1)} %get-tuple-element.20), channel_id=1, source_target_pairs={{2,0},{3,1},{4,2},{5,3},{6,4},{7,5},{8,6},{9,7},{10,8},{11,9},{12,... | collective-permute-start | bytes 786440 | tf_op jit(solution)/shard_map/ppermute | solution.py:23
  35.7 16.1 %all-to-all-start.1 = ((bf16[16,8,1024]{2,1,0:T(8,128)(2,1)}), bf16[16,8,1024]{2,1,0:T(8,128)(2,1)S(1)}, u32[]{:S(2)}, u32[]{:S(2)}) async-start(bf16[16,8,1024]{2,1,0:T(8,128)(2,1)} %bitcast.4), calls=%async_computation.1 | async-start | bytes 524288 | tf_op jit(solution)/shard_map/all_to_all | solution.py:227

commit v3 on v2

v3 whole, which is shorter than its diff:
```python
import math

import jax
import jax.numpy as jnp
from jax import lax
from jax.experimental import pallas as pl
from jax.experimental.pallas import tpu as pltpu
from jax.sharding import PartitionSpec as P

HEAD_DIM = 128
PARTS = 4
FACTOR = HEAD_DIM**-0.5
EXPONENT = FACTOR * math.log2(math.e)
MASKED = -1e30
BF16 = jnp.bfloat16
F32 = jnp.float32
VMEM_LIMIT = 32 * 2**20
LAYOUT_GFLOP = 3
OUTPUTS_GFLOP = 5


def shifted(x, by):
    length = lax.axis_size("row")
    pairs = [(i, i + by) for i in range(length) if 0 <= i + by < length]
    return lax.ppermute(x, "row", pairs)


def from_other_core(x):
    return lax.ppermute(x, "row", [(i, i ^ 1) for i in range(lax.axis_size("row"))])


def across_chips(x):
    size = lax.axis_size("row")
    groups = [list(range(core, size, 2)) for core in range(2)]
    return lax.all_to_all(x, "row", 0, 0, tiled=True, axis_index_groups=groups)


def dot_nt(former, latter):
    return lax.dot_general(former, latter, (((1,), (1,)), ((), ())), preferred_element_type=F32)


def dot_nn(former, latter):
    return lax.dot_general(former, latter, (((1,), (0,)), ((), ())), preferred_element_type=F32)


def transposed(x):
    return x.astype(F32).T.astype(BF16)


def answer_starts(lengths_row, height, lanes):
    answers = lengths_row.shape[1]
    rows = height // PARTS
    before = lax.broadcasted_iota(jnp.int32, (answers, answers), 1) < lax.broadcasted_iota(
        jnp.int32, (answers, answers), 0
    )
    spread = jnp.broadcast_to(lengths_row.astype(F32), (answers, answers))
    starts = jnp.sum(jnp.where(before, spread, 0.0), axis=1, keepdims=True)
    first = lax.axis_index("row") * height
    lane = lax.rem(lax.broadcasted_iota(jnp.int32, (1, lanes), 1), rows)
    found = []
    for part in range(PARTS):
        own = (lane + (first + part * rows)).astype(F32)
        begin = jnp.max(jnp.where(starts <= own, starts, 0.0), axis=0, keepdims=True)
        found.append(begin - (first + part * rows).astype(F32))
    return found


def window_bias(begin, window, rows):
    shape = (window, begin.shape[1])
    key = (lax.broadcasted_iota(jnp.int32, shape, 0) - (window - rows)).astype(F32)
    own = lax.rem(lax.broadcasted_iota(jnp.int32, (1, begin.shape[1]), 1), rows).astype(F32)
    return jnp.where((key <= own) & (key >= begin), 0.0, MASKED)


def staged(*stages):
    held = {}
    for step in range(PARTS + len(stages) - 1):
        for place, stage in enumerate(stages):
            part = step - place
            if 0 <= part < PARTS:
                held[part] = stage(part, held.get(part))


def for_heads(count, body):
    def step(g, carry):
        body(g)
        return carry

    lax.fori_loop(0, count, step, 0)


def columns_of(g, width=HEAD_DIM):
    return pl.ds(pl.multiple_of(g * width, width), width)


def stack(refs, cols):
    return jnp.concatenate([ref[:, cols] for ref in refs], axis=0)


def pack_kernel(k_ref, v_ref, pk_ref, pv_ref, own_ref, spread_ref):
    own_ref[...] = jnp.concatenate([k_ref[...], v_ref[...]], axis=1)
    pair = jnp.concatenate([pk_ref[...], pv_ref[...]], axis=1)
    spread_ref[...] = jnp.broadcast_to(pair[None], spread_ref.shape)


def layout_kernel(
    lengths_hbm, weights_hbm, q_hbm, do_hbm, qf_ref, cot_hbm, begin_ref,
    lengths_ref, weights_ref, q_ref, do_ref, cot_ref, small_sems, in_sems, out_sems,
):
    height = q_ref.shape[1]
    kv_heads = q_ref.shape[0]
    heads = q_ref.shape[2] // HEAD_DIM
    rows = height // PARTS
    small = [
        pltpu.make_async_copy(lengths_hbm, lengths_ref, small_sems.at[0]),
        pltpu.make_async_copy(weights_hbm, weights_ref, small_sems.at[1]),
    ]
    arriving = []
    for g in range(kv_heads):
        cols = pl.ds(g * heads * HEAD_DIM, heads * HEAD_DIM)
        arriving.append(pltpu.make_async_copy(do_hbm.at[:, cols], do_ref.at[g], in_sems.at[1, g]))
        arriving.append(pltpu.make_async_copy(q_hbm.at[:, cols], q_ref.at[g], in_sems.at[0, g]))
    for copy in small + arriving:
        copy.start()
    for copy in small:
        copy.wait()
    for part, begin in enumerate(answer_starts(lengths_ref[...], height, heads * rows)):
        begin_ref[part, 0:1] = begin
    spread = jnp.broadcast_to(weights_ref[...], (HEAD_DIM, height)).T
    leaving = []
    for g in range(kv_heads):
        arriving[2 * g].wait()
        arriving[2 * g + 1].wait()
        for part in range(PARTS):
            at = slice(part * rows, (part + 1) * rows)
            for h in range(heads):
                cols = slice(h * HEAD_DIM, (h + 1) * HEAD_DIM)
                to = slice(h * rows, (h + 1) * rows)
                cot_ref[g, part, to] = (do_ref[g, at, cols].astype(F32) * spread[at]).astype(BF16)
                qf_ref[g, part, to] = q_ref[g, at, cols]
        leaving.append(pltpu.make_async_copy(cot_ref.at[g], cot_hbm.at[g], out_sems.at[g]))
        leaving[-1].start()
    for copy in leaving:
        copy.wait()


def window_kernel(
    qf_ref, cot_hbm, begin_ref, far_ref, near_ref, own_ref,
    cot_ref, powers_ref, slopes_ref, stats_ref, bias_ref, sems,
):
    kv_heads = qf_ref.shape[0]
    window = powers_ref.shape[2]
    rows = far_ref.shape[0] // PARTS

    def arrival(g):
        return pltpu.make_async_copy(cot_hbm.at[g], cot_ref.at[g], sems.at[g])

    for g in range(kv_heads):
        arrival(g).start()
    for part in range(PARTS):
        bias_ref[part] = window_bias(begin_ref[part, 0:1], window, rows)

    def head(g):
        arrival(g).wait()
        keys = stack((far_ref, near_ref, own_ref), columns_of(g))
        values = stack((far_ref, near_ref, own_ref), columns_of(g + kv_heads))

        def score(part, _):
            at = slice(part * rows, part * rows + window)
            return dot_nt(keys[at], qf_ref[g, part]), dot_nt(values[at], cot_ref[g, part])

        def weigh(part, held):
            scores, slopes = held
            scores = scores + bias_ref[part]
            highest = jnp.max(scores, axis=0, keepdims=True)
            powers = jnp.exp2((scores - highest) * EXPONENT)
            powers_ref[g, part] = powers
            slopes_ref[g, part] = slopes
            stats_ref[g, part, 0:1] = highest
            stats_ref[g, part, 1:2] = jnp.sum(powers, axis=0, keepdims=True)
            stats_ref[g, part, 2:3] = jnp.sum(powers * slopes, axis=0, keepdims=True)

        staged(score, weigh)

    for_heads(kv_heads, head)


def terms_kernel(
    qf_ref, cot_ref, powers_ref, slopes_ref, stats_ref, same_ref, other_ref,
    keep_ref, pass_ref, far_ref, own_ref, chances_hbm, grad_hbm, chances_ref, grad_ref, dk_ref, dv_ref, sems,
):
    kv_heads = qf_ref.shape[0]
    window = powers_ref.shape[2]
    half = same_ref.shape[0]
    prompt = 2 * half
    height = far_ref.shape[0]
    rows = height // PARTS

    def copies(g, part):
        return (
            pltpu.make_async_copy(chances_ref.at[g, part], chances_hbm.at[g, part], sems.at[0, g, part]),
            pltpu.make_async_copy(grad_ref.at[g, part], grad_hbm.at[g, part], sems.at[1, g, part]),
        )

    def head(g):
        keys = stack((same_ref, other_ref), columns_of(g))
        values = stack((same_ref, other_ref), columns_of(g + kv_heads))
        dk_ref[...] = jnp.zeros_like(dk_ref)
        dv_ref[...] = jnp.zeros_like(dv_ref)

        def score(part, _):
            return dot_nt(keys, qf_ref[g, part]), dot_nt(values, cot_ref[g, part])

        def weigh(part, held):
            scores, slopes = held
            window_high, window_sum, window_delta = (stats_ref[g, part, i : i + 1] for i in range(3))
            highest = jnp.maximum(jnp.max(scores, axis=0, keepdims=True), window_high)
            powers = jnp.exp2((scores - highest) * EXPONENT)
            fade = jnp.exp2((window_high - highest) * EXPONENT)
            inverse = 1.0 / (jnp.sum(powers, axis=0, keepdims=True) + fade * window_sum)
            scale = fade * inverse
            chances = powers * inverse
            delta = jnp.sum(chances * slopes, axis=0, keepdims=True) + scale * window_delta
            chances_ref[g, part, :prompt] = chances.astype(BF16)
            grad_ref[g, part, :prompt] = (chances * (slopes - delta)).astype(BF16)
            chances = powers_ref[g, part] * scale
            chances_ref[g, part, prompt:] = chances.astype(BF16)
            grad_ref[g, part, prompt:] = (chances * (slopes_ref[g, part] - delta)).astype(BF16)

        def gather(part, _):
            for copy in copies(g, part):
                copy.start()
            begin = prompt + part * rows
            for ref, former, latter in ((dk_ref, grad_ref, qf_ref), (dv_ref, chances_ref, cot_ref)):
                terms = dot_nn(former[g, part], latter[g, part])
                ref[:prompt] += terms[:prompt]
                ref[begin : begin + window] += terms[prompt:]

        staged(score, weigh, gather)
        far, near, own = (slice(prompt + i * height, prompt + (i + 1) * height) for i in range(3))
        for ref, into, source in (
            (keep_ref, slice(0, half), slice(0, half)),
            (pass_ref, slice(0, half), slice(half, prompt)),
            (pass_ref, slice(half, half + height), near),
            (far_ref, slice(0, height), far),
            (own_ref, slice(0, height), own),
        ):
            ref[into, columns_of(g)] = (dk_ref[source] * FACTOR).astype(ref.dtype)
            ref[into, columns_of(g + kv_heads)] = dv_ref[source].astype(ref.dtype)

    for_heads(kv_heads, head)
    for g in range(kv_heads):
        for part in range(PARTS):
            for copy in copies(g, part):
                copy.wait()


def outputs_kernel(
    chances_hbm, grad_hbm, same_ref, other_ref, far_ref, near_ref, own_ref, out_hbm, dq_hbm,
    out_ref, dq_ref, chances_ref, grad_ref, sems, in_sems,
):
    kv_heads = chances_hbm.shape[0]
    height = far_ref.shape[0]
    prompt = 2 * same_ref.shape[0]
    rows = height // PARTS
    heads = out_ref.shape[2] // HEAD_DIM
    refs = (same_ref, other_ref, far_ref, near_ref, own_ref)

    def everywhere(x, part):
        before, after = part * rows, height - (part + 1) * rows
        pieces = [x[:prompt], jnp.zeros((before, x.shape[1]), x.dtype), x[prompt:], jnp.zeros((after, x.shape[1]), x.dtype)]
        return jnp.concatenate([piece for piece in pieces if piece.shape[0]], axis=0)

    def copies(g):
        cols = columns_of(g, heads * HEAD_DIM)
        return (
            pltpu.make_async_copy(out_ref.at[g], out_hbm.at[:, cols], sems.at[0, g]),
            pltpu.make_async_copy(dq_ref.at[g], dq_hbm.at[:, cols], sems.at[1, g]),
        )

    def arrivals(g):
        return (
            pltpu.make_async_copy(chances_hbm.at[g], chances_ref.at[g], in_sems.at[0, g]),
            pltpu.make_async_copy(grad_hbm.at[g], grad_ref.at[g], in_sems.at[1, g]),
        )

    for g in range(kv_heads):
        for copy in arrivals(g):
            copy.start()

    def head(g):
        for copy in arrivals(g):
            copy.wait()
        keys_t = transposed(stack(refs, columns_of(g)))
        values_t = transposed(stack(refs, columns_of(g + kv_heads)))

        def multiply(part, _):
            out = dot_nn(values_t, everywhere(chances_ref[g, part], part))
            return out, dot_nn(keys_t, everywhere(grad_ref[g, part], part)) * FACTOR

        def turn(part, held):
            for ref, value in zip((out_ref, dq_ref), held):
                value = value.T.astype(BF16)
                for h in range(heads):
                    at = slice(part * rows, (part + 1) * rows)
                    ref[g, at, h * HEAD_DIM : (h + 1) * HEAD_DIM] = value[h * rows : (h + 1) * rows]

        staged(multiply, turn)
        for copy in copies(g):
            copy.start()

    for_heads(kv_heads, head)
    for g in range(kv_heads):
        for copy in copies(g):
            copy.wait()


def sums_kernel(
    own_ref, passed_ref, far_ref, arrived_ref, ak_hbm, av_hbm, pk_hbm, pv_hbm, ak_ref, av_ref, pk_ref, pv_ref, sems
):
    height, columns = ak_ref.shape
    total = arrived_ref[0].astype(F32)
    for chip in range(1, arrived_ref.shape[0]):
        total += arrived_ref[chip].astype(F32)
    pk_ref[...] = total[:, :columns]
    pv_ref[...] = total[:, columns:]
    copies = [pltpu.make_async_copy(pk_ref, pk_hbm, sems.at[0]), pltpu.make_async_copy(pv_ref, pv_hbm, sems.at[1])]
    for copy in copies:
        copy.start()
    even = 1.0 - lax.rem(lax.axis_index("row"), 2).astype(F32)
    near = passed_ref[passed_ref.shape[0] - height :].astype(F32) * even
    answers = (own_ref[...] + near + far_ref[...].astype(F32)).astype(BF16)
    ak_ref[...] = answers[:, :columns]
    av_ref[...] = answers[:, columns:]
    copies += [pltpu.make_async_copy(ak_ref, ak_hbm, sems.at[2]), pltpu.make_async_copy(av_ref, av_hbm, sems.at[3])]
    for copy in copies[2:]:
        copy.start()
    for copy in copies:
        copy.wait()


def per_device(
    queries, answer_keys, answer_values, prompt_keys, prompt_values, out_grad, weights, lengths
):
    height = queries.shape[0]
    columns = answer_keys.shape[1]
    kv_heads = columns // HEAD_DIM
    span = queries.shape[1] // kv_heads
    size = lax.axis_size("row")
    own_prompt = prompt_keys.shape[0]
    half = own_prompt * size // 2
    prompt = 2 * half
    window = 2 * height + height // PARTS
    lanes = span // HEAD_DIM * height // PARTS
    parts = (kv_heads, PARTS)

    def call(kernel, outs, gflop, arrays, in_specs=None, out_specs=None, scratch=()):
        given = {} if in_specs is None else {"in_specs": in_specs}
        if out_specs is not None:
            given["out_specs"] = out_specs
        return pl.pallas_call(
            kernel,
            out_shape=outs,
            scratch_shapes=list(scratch),
            compiler_params=pltpu.CompilerParams(vmem_limit_bytes=VMEM_LIMIT),
            cost_estimate=pl.CostEstimate(flops=int(gflop * 1e9), bytes_accessed=1_000_000, transcendentals=500_000),
            **given,
        )(*arrays)

    anywhere = pl.BlockSpec(memory_space=pl.ANY)
    vmem = pl.BlockSpec(memory_space=pltpu.VMEM)

    own, spread = pl.pallas_call(
        pack_kernel,
        out_shape=[
            jax.ShapeDtypeStruct((height, 2 * columns), BF16),
            jax.ShapeDtypeStruct((size // 2, own_prompt, 2 * columns), BF16),
        ],
    )(answer_keys, answer_values, prompt_keys, prompt_values)
    far = shifted(own, 2)
    odd = lax.rem(lax.axis_index("row"), 2) == 1
    near = from_other_core(jnp.where(odd, far, own))
    same = across_chips(spread).reshape(half, 2 * columns)
    near, same = lax.optimization_barrier((near, same))
    other = from_other_core(same)

    def in_hbm(*arrays):
        return [pltpu.with_memory_space_constraint(array, pltpu.HBM) for array in arrays]

    flat_queries, cotangent, begin = call(
        layout_kernel,
        [
            pltpu.VMEM((*parts, lanes, HEAD_DIM), BF16),
            pltpu.HBM((*parts, lanes, HEAD_DIM), BF16),
            pltpu.VMEM((PARTS, 8, lanes), F32),
        ],
        LAYOUT_GFLOP,
        in_hbm(lengths.reshape(1, -1), weights.reshape(1, -1), queries, out_grad),
        in_specs=[anywhere] * 4,
        out_specs=[vmem, anywhere, vmem],
        scratch=[
            pltpu.VMEM((1, lengths.shape[0]), jnp.int32),
            pltpu.VMEM((1, height), F32),
            pltpu.VMEM((kv_heads, height, span), BF16),
            pltpu.VMEM((kv_heads, height, span), BF16),
            pltpu.VMEM((*parts, lanes, HEAD_DIM), BF16),
            pltpu.SemaphoreType.DMA((2,)),
            pltpu.SemaphoreType.DMA((2, kv_heads)),
            pltpu.SemaphoreType.DMA((kv_heads,)),
        ],
    )
    cotangent, powers, slopes, stats = call(
        window_kernel,
        [
            pltpu.VMEM((*parts, lanes, HEAD_DIM), BF16),
            pltpu.VMEM((*parts, window, lanes), F32),
            pltpu.VMEM((*parts, window, lanes), F32),
            pltpu.VMEM((*parts, 8, lanes), F32),
        ],
        3,
        [flat_queries, *in_hbm(cotangent), begin, far, near, own],
        in_specs=[vmem, anywhere] + [vmem] * 4,
        scratch=[pltpu.VMEM((PARTS, window, lanes), F32), pltpu.SemaphoreType.DMA((kv_heads,))],
    )
    keep, passed, far_terms, own_terms, chances, score_grad = call(
        terms_kernel,
        [
            pltpu.VMEM((half, 2 * columns), F32),
            pltpu.VMEM((half + height, 2 * columns), BF16),
            pltpu.VMEM((height, 2 * columns), BF16),
            pltpu.VMEM((height, 2 * columns), F32),
            pltpu.HBM((*parts, prompt + window, lanes), BF16),
            pltpu.HBM((*parts, prompt + window, lanes), BF16),
        ],
        4,
        [flat_queries, cotangent, powers, slopes, stats, same, other],
        out_specs=[vmem] * 4 + [anywhere] * 2,
        scratch=[pltpu.VMEM((*parts, prompt + window, lanes), BF16)] * 2
        + [pltpu.VMEM((prompt + 3 * height, HEAD_DIM), F32)] * 2
        + [pltpu.SemaphoreType.DMA((2, *parts))],
    )
    whole = jax.ShapeDtypeStruct(queries.shape, BF16)
    attn_out, q_grad = call(
        outputs_kernel,
        [whole, whole],
        OUTPUTS_GFLOP,
        [*in_hbm(chances, score_grad), same, other, far, near, own],
        in_specs=[anywhere] * 2 + [vmem] * 5,
        out_specs=[anywhere, anywhere],
        scratch=[pltpu.VMEM((kv_heads, height, span), BF16)] * 2
        + [pltpu.VMEM((*parts, prompt + window, lanes), BF16)] * 2
        + [pltpu.SemaphoreType.DMA((2, kv_heads))] * 2,
    )
    passed = from_other_core(passed)
    both = (keep + passed[:half].astype(F32)).astype(BF16)
    far_terms = (far_terms.astype(F32) + jnp.where(odd, passed[half:].astype(F32), 0.0)).astype(BF16)
    both, far_terms = lax.optimization_barrier((both, far_terms))
    from_far = shifted(far_terms, -2)
    arrived = across_chips(both.reshape(size // 2, own_prompt, 2 * columns))
    answer_grad = jax.ShapeDtypeStruct((height, columns), BF16)
    prompt_grad = jax.ShapeDtypeStruct((own_prompt, columns), F32)
    dk, dv, dpk, dpv = call(
        sums_kernel,
        [answer_grad, answer_grad, prompt_grad, prompt_grad],
        0.1,
        [own_terms, passed, from_far, arrived],
        out_specs=[anywhere] * 4,
        scratch=[pltpu.VMEM((height, columns), BF16)] * 2
        + [pltpu.VMEM((own_prompt, columns), F32)] * 2
        + [pltpu.SemaphoreType.DMA((4,))],
    )
    return attn_out, q_grad, dk, dv, dpk, dpv


def solution(mesh):
    rows = P(("grp", "row"), None)
    return jax.shard_map(
        per_device,
        mesh=mesh,
        in_specs=(rows,) * 6 + (P(("grp", "row")), P("grp")),
        out_specs=(rows,) * 6,
        check_vma=False,
    )
```

time: 53 us -> 49.2 us (0.928)
  Pallas kernels: 11.5 us -> 19.3 us
  waiting for transfers between devices: 15.6 us -> 9.91 us
  starting transfers between devices: 22.3 us -> 17.1 us
  local copies, waits for them, and re-layouts: 2.14 us -> 0.01 us
  other arithmetic: 0.14 us -> 1.74 us
    pallas_call x2 -> x6, Pallas kernels: 11.5 us -> 19.3 us  [the longest x5 17.5 us: call(): pl.pallas_call(kernel, out_shape=outs, scratch_shapes=list(scratch), comp...]
    all_to_all x2, waiting for transfers between devices: 9.23 us -> 4.02 us  [across_chips(): return lax.all_to_all(x, 'row', 0, 0, tiled=True, axis_index_groups=groups)]
    ppermute x2 -> x3, starting transfers between devices: 3.62 us -> 0.64 us  [from_other_core(): lax.ppermute(x, 'row', [(i, i ^ 1) for i in range(lax.axis_size('row'))])]
    ppermute x3 -> x2, waiting for transfers between devices: 6.35 us -> 4.53 us  [shifted(): return lax.ppermute(x, 'row', pairs)]
    ppermute x3 -> x2, starting transfers between devices: 7.56 us -> 6.13 us  [shifted(): return lax.ppermute(x, 'row', pairs)]
    ppermute x2 -> x3, waiting for transfers between devices: 0.01 us -> 1.35 us  [from_other_core(): lax.ppermute(x, 'row', [(i, i ^ 1) for i in range(lax.axis_size('row'))])]
    slice x2 -> x0, local copies, waits for them, and re-layouts: 1.33 us -> none  [the longest x1 0.72 us: per_device(): window_grad[:, columns:]]
    select_n x0 -> x1, other arithmetic: none -> 0.98 us  [per_device(): near = from_other_core(jnp.where(odd, far, own))]
  transfers between devices with their start and end apart: 7 -> 7, of which waited for: 3 -> 5; matrix products, arithmetic and copies ran while one was open for 2% -> 2% of each run, Pallas kernels for 0% -> 23%
where the time goes in v3:
time: 49.2 us; the launch traced here: 48.8 us
  Pallas kernels  19.3 us (39%)
  starting transfers between devices  17.1 us (35%)
  waiting for transfers between devices  9.91 us (20%)
  other arithmetic  1.74 us (4%)
  between operations  0.72 us (1%)
    pallas_call x5, Pallas kernels, call(): pl.pallas_call(kernel, out_shape=outs, scratch_shapes=list(scratch), comp...  17.5 us
    all_to_all x2, starting transfers between devices, across_chips(): return lax.all_to_all(x, 'row', 0, 0, tiled=True, axis_index_groups=groups)  10.3 us
    ppermute x2, starting transfers between devices, shifted(): return lax.ppermute(x, 'row', pairs)  6.13 us
    ppermute x2, waiting for transfers between devices, shifted(): return lax.ppermute(x, 'row', pairs)  4.53 us
    all_to_all x2, waiting for transfers between devices, across_chips(): return lax.all_to_all(x, 'row', 0, 0, tiled=True, axis_index_groups=groups)  4.02 us
    pallas_call x1, Pallas kernels, per_device(): pl.pallas_call(pack_kernel, out_shape=[jax.ShapeDtypeStruct((height, 2 *...  1.73 us
    ppermute x3, waiting for transfers between devices, from_other_core(): lax.ppermute(x, 'row', [(i, i ^ 1) for i in range(lax.axis_size('row'))])  1.35 us
  transfers between devices with their start and end apart: 7, of which 5 were waited for; matrix products, arithmetic and copies ran while one was open for 2% of the time, Pallas kernels for 23%

profile of v3, /device:TPU:0, one launch (start us, length us, event | category | flops | bytes accessed | tf_op | source)
XLA Modules:
  0.0 48.8 jit_solution(17101713312914548724)
XLA Ops:
  0.6 1.7 %shard_map.128 = (bf16[128,1024]{1,0:T(8,128)(2,1)}, bf16[8,8,1024]{2,1,0:T(8,128)(2,1)}) custom-call(bf16[128,512]{1,0:T(8,128)(2,1)} %k_ref.1, bf16[128,512]{1,0:T(8,128)(2,1)} %v_ref.1, bf16[8,512]{1,0:T(8,128)(2,1)} %pk_ref.1, bf16[8,512]{1,0:T(8,128)(2,1)} %pv_ref.1), custom_call_target="tpu_custom_call" | custom-call | tf_op jit(solution)/shard_map/pallas_call | solution.py:373
  2.4 4.8 %collective-permute-start = (bf16[128,1024]{1,0:T(8,128)(2,1)}, bf16[128,1024]{1,0:T(8,128)(2,1)S(1)}, u32[]{:S(2)}, u32[]{:S(2)}) collective-permute-start(bf16[128,1024]{1,0:T(8,128)(2,1)} %get-tuple-element.34.own_ref), channel_id=1, source_target_pairs={{0,2},{1,3},{2,4},{3,5},{4,6},{5,7},{6,8},{7,9},{8,10},{9,11},{10,... | collective-permute-start | bytes 786440 | tf_op jit(solution)/shard_map/ppermute | solution.py:25
  7.2 4.9 %all-to-all-start = ((bf16[8,8,1024]{2,1,0:T(8,128)(2,1)}), bf16[8,8,1024]{2,1,0:T(8,128)(2,1)S(1)}, u32[]{:S(2)}, u32[]{:S(2)}) async-start(bf16[8,8,1024]{2,1,0:T(8,128)(2,1)} %get-tuple-element.35), calls=%async_computation | async-start | bytes 262144 | tf_op jit(solution)/shard_map/all_to_all | solution.py:35
  12.1 1.1 %collective-permute-done.far_ref = bf16[128,1024]{1,0:T(8,128)(2,1)S(1)} collective-permute-done((bf16[128,1024]{1,0:T(8,128)(2,1)}, bf16[128,1024]{1,0:T(8,128)(2,1)S(1)}, u32[]{:S(2)}, u32[]{:S(2)}) %collective-permute-start) | collective-permute-done | bytes 262176 | tf_op jit(solution)/shard_map/ppermute | solution.py:25
  13.2 1.0 %broadcast_select_fusion = bf16[128,1024]{1,0:T(8,128)(2,1)S(1)} fusion(bf16[128,1024]{1,0:T(8,128)(2,1)S(1)} %collective-permute-done.far_ref, bf16[128,1024]{1,0:T(8,128)(2,1)} %get-tuple-element.34.own_ref, pred[]{:T(512)S(6)} %eq.3), kind=kLoop, calls=%fused_computation.2 | loop fusion | flops 131072 | bytes 786433 | tf_op jit(solution)/shard_map/jit(_where)/select_n | solution.py:382
  14.2 0.1 collective-permute-start.1
  14.3 0.0 copy-start
  14.3 2.6 %shard_map.127 = (bf16[4,4,256,128]{3,2,1,0:T(8,128)(2,1)S(1)}, bf16[4,4,256,128]{3,2,1,0:T(8,128)(2,1)}, f32[4,8,256]{2,1,0:T(8,128)S(1)}) custom-call(s32[1,32]{1,0:T(1,128)} %bitcast.7, f32[1,128]{1,0:T(1,128)} %bitcast.8, bf16[128,4096]{1,0:T(8,128)(2,1)} %q_hbm.1, bf16[128,4096]{1,0:T(8,128)(2,1)} %do_hbm.1), custom_call_target="tpu_custom_call" | custom-call | flops 3000000000 | bytes 1000000 | tf_op jit(solution)/shard_map/pallas_call | solution.py:361
  16.9 2.6 %all-to-all-done = bf16[8,8,1024]{2,1,0:T(8,128)(2,1)S(1)} async-done(((bf16[8,8,1024]{2,1,0:T(8,128)(2,1)}), bf16[8,8,1024]{2,1,0:T(8,128)(2,1)S(1)}, u32[]{:S(2)}, u32[]{:S(2)}) %all-to-all-start) | async-done | bytes 131104 | tf_op jit(solution)/shard_map/all_to_all | solution.py:35
  19.4 0.0 collective-permute-done.1.near_ref
  19.4 0.0 collective-permute-start.2
  19.4 0.0 copy-done
  19.5 3.9 %shard_map.129 = (bf16[4,4,256,128]{3,2,1,0:T(8,128)(2,1)S(1)}, f32[4,4,288,256]{3,2,1,0:T(8,128)S(1)}, f32[4,4,288,256]{3,2,1,0:T(8,128)S(1)}, f32[4,4,8,256]{3,2,1,0:T(8,128)S(1)}) custom-call(bf16[4,4,256,128]{3,2,1,0:T(8,128)(2,1)S(1)} %get-tuple-element.31.qf_ref, bf16[4,4,256,128]{3,2,1,0:T(8,128)(2,1)} %get-tuple-element.32.cot_hbm, ...), custom_call_target="tpu_custom_call" | custom-call | flops 3000000000 | bytes 1000000 | tf_op jit(solution)/shard_map/pallas_call | solution.py:361
  23.4 0.0 collective-permute-done.2.other_ref
  23.4 5.6 %shard_map.130 = (f32[64,1024]{1,0:T(8,128)S(1)}, bf16[192,1024]{1,0:T(8,128)(2,1)S(1)}, bf16[128,1024]{1,0:T(8,128)(2,1)S(1)}, f32[128,1024]{1,0:T(8,128)S(1)},...) custom-call(bf16[4,4,256,128]{3,2,1,0:T(8,128)(2,1)S(1)} %get-tuple-element.31.qf_ref, ...), custom_call_target="tpu_custom_call" | custom-call | flops 4000000000 | bytes 1000000 | tf_op jit(solution)/shard_map/pallas_call | solution.py:361
  29.0 0.6 %collective-permute-start.3 = (bf16[192,1024]{1,0:T(8,128)(2,1)S(1)}, bf16[192,1024]{1,0:T(8,128)(2,1)S(1)}, u32[]{:S(2)}, u32[]{:S(2)}) collective-permute-start(bf16[192,1024]{1,0:T(8,128)(2,1)S(1)} %get-tuple-element.47), channel_id=1, source_target_pairs={{0,1},{1,0},{2,3},{3,2},{4,5},{5,4},{6,7},{7,6},{8,9},{9,8},{10,11... | collective-permute-start | bytes 1179656 | tf_op jit(solution)/shard_map/ppermute | solution.py:29
  29.5 1.3 %collective-permute-done.3.passed_ref = bf16[192,1024]{1,0:T(8,128)(2,1)S(1)} collective-permute-done((bf16[192,1024]{1,0:T(8,128)(2,1)S(1)}, bf16[192,1024]{1,0:T(8,128)(2,1)S(1)}, u32[]{:S(2)}, u32[]{:S(2)}) %collective-permute-start.3) | collective-permute-done | bytes 393248 | tf_op jit(solution)/shard_map/ppermute | solution.py:29
  30.9 0.7 %add_convert_fusion.1 = bf16[64,1024]{1,0:T(8,128)(2,1)} fusion(f32[64,1024]{1,0:T(8,128)S(1)} %get-tuple-element.48, bf16[192,1024]{1,0:T(8,128)(2,1)S(1)} %collective-permute-done.3.passed_ref), kind=kLoop, calls=%fused_computation.1 | loop fusion | flops 196608 | bytes 524288 | tf_op jit(solution)/shard_map/convert_element_type | solution.py:455
  31.6 0.1 add_convert_fusion
  31.7 5.5 %all-to-all-start.1 = ((bf16[8,8,1024]{2,1,0:T(8,128)(2,1)}), bf16[8,8,1024]{2,1,0:T(8,128)(2,1)S(1)}, u32[]{:S(2)}, u32[]{:S(2)}) async-start(bf16[8,8,1024]{2,1,0:T(8,128)(2,1)} %bitcast.3), calls=%async_computation.1 | async-start | bytes 262144 | tf_op jit(solution)/shard_map/all_to_all | solution.py:35
  37.1 1.3 %collective-permute-start.4 = (bf16[128,1024]{1,0:T(8,128)(2,1)S(1)}, bf16[128,1024]{1,0:T(8,128)(2,1)S(1)}, u32[]{:S(2)}, u32[]{:S(2)}) collective-permute-start(bf16[128,1024]{1,0:T(8,128)(2,1)S(1)} %add_convert_fusion), channel_id=1, source_target_pairs={{2,0},{3,1},{4,2},{5,3},{6,4},{7,5},{8,6},{9,7},{10,8},{11,9},{12,... | collective-permute-start | bytes 786440 | tf_op jit(solution)/shard_map/ppermute | solution.py:25
  38.4 4.7 %shard_map.131 = (bf16[128,4096]{1,0:T(8,128)(2,1)}, bf16[128,4096]{1,0:T(8,128)(2,1)}) custom-call(bf16[4,4,416,256]{3,2,1,0:T(8,128)(2,1)} %get-tuple-element.42.chances_hbm, bf16[4,4,416,256]{3,2,1,0:T(8,128)(2,1)} %get-tuple-element.43.grad_hbm, bf16[64,1024]{1,0:T(8,128)(2,1)S(1)} %bitcast.6, bf16[64,1024]{1,0:T(8,128)(2,1)S(1)} %collective-permute-done.2.other_ref, ...), custom_call_target="tpu_custom_call" | custom-call | flops 5000000000 | bytes 1000000 | tf_op jit(solution)/shard_map/pallas_call | solution.py:361
  43.1 1.5 %all-to-all-done.1.arrived_ref = bf16[8,8,1024]{2,1,0:T(8,128)(2,1)S(1)} async-done(((bf16[8,8,1024]{2,1,0:T(8,128)(2,1)}), bf16[8,8,1024]{2,1,0:T(8,128)(2,1)S(1)}, u32[]{:S(2)}, u32[]{:S(2)}) %all-to-all-start.1) | async-done | bytes 131104 | tf_op jit(solution)/shard_map/all_to_all | solution.py:35
  44.6 3.4 %collective-permute-done.4.far_ref = bf16[128,1024]{1,0:T(8,128)(2,1)S(1)} collective-permute-done((bf16[128,1024]{1,0:T(8,128)(2,1)S(1)}, bf16[128,1024]{1,0:T(8,128)(2,1)S(1)}, u32[]{:S(2)}, u32[]{:S(2)}) %collective-permute-start.4) | collective-permute-done | bytes 262176 | tf_op jit(solution)/shard_map/ppermute | solution.py:25
  47.9 0.8 %shard_map.132 = (bf16[128,512]{1,0:T(8,128)(2,1)}, bf16[128,512]{1,0:T(8,128)(2,1)}, f32[8,512]{1,0:T(8,128)}, f32[8,512]{1,0:T(8,128)}) custom-call(f32[128,1024]{1,0:T(8,128)S(1)} %get-tuple-element.46.own_ref, bf16[192,1024]{1,0:T(8,128)(2,1)S(1)} %collective-permute-done.3.passed_ref, bf16[128,1024]{1,0:T(8,128)(2,1)S(1)} %collective-permute-done.4.far_ref, ...), custom_call_target="tpu_custom_call" | custom-call | flops 100000000 | bytes 1000000 | tf_op jit(solution)/shard_map/pallas_call | solution.py:361
Async XLA Ops:
  2.4 10.9 %collective-permute-start = (bf16[128,1024]{1,0:T(8,128)(2,1)}, bf16[128,1024]{1,0:T(8,128)(2,1)S(1)}, u32[]{:S(2)}, u32[]{:S(2)}) collective-permute-start(bf16[128,1024]{1,0:T(8,128)(2,1)} %get-tuple-element.34.own_ref), channel_id=1, source_target_pairs={{0,2},{1,3},{2,4},{3,5},{4,6},{5,7},{6,8},{7,9},{8,10},{9,11},{10,... | collective-permute-start | bytes 786440 | tf_op jit(solution)/shard_map/ppermute | solution.py:25
  7.2 12.2 %all-to-all-start = ((bf16[8,8,1024]{2,1,0:T(8,128)(2,1)}), bf16[8,8,1024]{2,1,0:T(8,128)(2,1)S(1)}, u32[]{:S(2)}, u32[]{:S(2)}) async-start(bf16[8,8,1024]{2,1,0:T(8,128)(2,1)} %get-tuple-element.35), calls=%async_computation | async-start | bytes 262144 | tf_op jit(solution)/shard_map/all_to_all | solution.py:35
  14.2 5.2 %collective-permute-start.1 = (bf16[128,1024]{1,0:T(8,128)(2,1)S(1)}, bf16[128,1024]{1,0:T(8,128)(2,1)S(1)}, u32[]{:S(2)}, u32[]{:S(2)}) collective-permute-start(bf16[128,1024]{1,0:T(8,128)(2,1)S(1)} %broadcast_select_fusion), channel_id=1, source_target_pairs={{0,1},{1,0},{2,3},{3,2},{4,5},{5,4},{6,7},{7,6},{8,9},{9,8},{10,11... | collective-permute-start | bytes 786440 | tf_op jit(solution)/shard_map/ppermute | solution.py:29
  14.3 5.1 %copy-start = (bf16[128,1024]{1,0:T(8,128)(2,1)S(1)}, bf16[128,1024]{1,0:T(8,128)(2,1)}, u32[]{:S(2)}) copy-start(bf16[128,1024]{1,0:T(8,128)(2,1)} %get-tuple-element.34.own_ref) | copy-start | bytes 786436
  19.4 4.0 %collective-permute-start.2 = (bf16[64,1024]{1,0:T(8,128)(2,1)S(1)}, bf16[64,1024]{1,0:T(8,128)(2,1)S(1)}, u32[]{:S(2)}, u32[]{:S(2)}) collective-permute-start(bf16[64,1024]{1,0:T(8,128)(2,1)S(1)} %bitcast.4), channel_id=1, source_target_pairs={{0,1},{1,0},{2,3},{3,2},{4,5},{5,4},{6,7},{7,6},{8,9},{9,8},{10,11... | collective-permute-start | bytes 393224 | tf_op jit(solution)/shard_map/ppermute | solution.py:29
  29.0 1.9 %collective-permute-start.3 = (bf16[192,1024]{1,0:T(8,128)(2,1)S(1)}, bf16[192,1024]{1,0:T(8,128)(2,1)S(1)}, u32[]{:S(2)}, u32[]{:S(2)}) collective-permute-start(bf16[192,1024]{1,0:T(8,128)(2,1)S(1)} %get-tuple-element.47), channel_id=1, source_target_pairs={{0,1},{1,0},{2,3},{3,2},{4,5},{5,4},{6,7},{7,6},{8,9},{9,8},{10,11... | collective-permute-start | bytes 1179656 | tf_op jit(solution)/shard_map/ppermute | solution.py:29
  31.7 12.9 %all-to-all-start.1 = ((bf16[8,8,1024]{2,1,0:T(8,128)(2,1)}), bf16[8,8,1024]{2,1,0:T(8,128)(2,1)S(1)}, u32[]{:S(2)}, u32[]{:S(2)}) async-start(bf16[8,8,1024]{2,1,0:T(8,128)(2,1)} %bitcast.3), calls=%async_computation.1 | async-start | bytes 262144 | tf_op jit(solution)/shard_map/all_to_all | solution.py:35
  37.1 10.8 %collective-permute-start.4 = (bf16[128,1024]{1,0:T(8,128)(2,1)S(1)}, bf16[128,1024]{1,0:T(8,128)(2,1)S(1)}, u32[]{:S(2)}, u32[]{:S(2)}) collective-permute-start(bf16[128,1024]{1,0:T(8,128)(2,1)S(1)} %add_convert_fusion), channel_id=1, source_target_pairs={{2,0},{3,1},{4,2},{5,3},{6,4},{7,5},{8,6},{9,7},{10,8},{11,9},{12,... | collective-permute-start | bytes 786440 | tf_op jit(solution)/shard_map/ppermute | solution.py:25

commit v4 on v3

--- a/solution.py
+++ b/solution.py
@@ -187,7 +187,7 @@
 
 def terms_kernel(
     qf_ref, cot_ref, powers_ref, slopes_ref, stats_ref, same_ref, other_ref,
-    keep_ref, pass_ref, far_ref, own_ref, chances_hbm, grad_hbm, chances_ref, grad_ref, dk_ref, dv_ref, sems,
+    keep_ref, pass_ref, near_ref, far_ref, own_ref, chances_hbm, grad_hbm, chances_ref, grad_ref, dk_ref, dv_ref, sems,
 ):
     kv_heads = qf_ref.shape[0]
     window = powers_ref.shape[2]
@@ -196,10 +196,10 @@
     height = far_ref.shape[0]
     rows = height // PARTS
 
-    def copies(g, part):
+    def copies(g):
         return (
-            pltpu.make_async_copy(chances_ref.at[g, part], chances_hbm.at[g, part], sems.at[0, g, part]),
-            pltpu.make_async_copy(grad_ref.at[g, part], grad_hbm.at[g, part], sems.at[1, g, part]),
+            pltpu.make_async_copy(chances_ref.at[g], chances_hbm.at[g], sems.at[0, g]),
+            pltpu.make_async_copy(grad_ref.at[g], grad_hbm.at[g], sems.at[1, g]),
         )
 
     def head(g):
@@ -228,8 +228,6 @@
             grad_ref[g, part, prompt:] = (chances * (slopes_ref[g, part] - delta)).astype(BF16)
 
         def gather(part, _):
-            for copy in copies(g, part):
-                copy.start()
             begin = prompt + part * rows
             for ref, former, latter in ((dk_ref, grad_ref, qf_ref), (dv_ref, chances_ref, cot_ref)):
                 terms = dot_nn(former[g, part], latter[g, part])
@@ -237,11 +235,13 @@
                 ref[begin : begin + window] += terms[prompt:]
 
         staged(score, weigh, gather)
+        for copy in copies(g):
+            copy.start()
         far, near, own = (slice(prompt + i * height, prompt + (i + 1) * height) for i in range(3))
         for ref, into, source in (
             (keep_ref, slice(0, half), slice(0, half)),
             (pass_ref, slice(0, half), slice(half, prompt)),
-            (pass_ref, slice(half, half + height), near),
+            (near_ref, slice(0, height), near),
             (far_ref, slice(0, height), far),
             (own_ref, slice(0, height), own),
         ):
@@ -250,9 +250,8 @@
 
     for_heads(kv_heads, head)
     for g in range(kv_heads):
-        for part in range(PARTS):
-            for copy in copies(g, part):
-                copy.wait()
+        for copy in copies(g):
+            copy.wait()
 
 
 def outputs_kernel(
@@ -316,7 +315,7 @@
 
 
 def sums_kernel(
-    own_ref, passed_ref, far_ref, arrived_ref, ak_hbm, av_hbm, pk_hbm, pv_hbm, ak_ref, av_ref, pk_ref, pv_ref, sems
+    own_ref, near_ref, far_ref, arrived_ref, ak_hbm, av_hbm, pk_hbm, pv_hbm, ak_ref, av_ref, pk_ref, pv_ref, sems
 ):
     height, columns = ak_ref.shape
     total = arrived_ref[0].astype(F32)
@@ -328,7 +327,7 @@
     for copy in copies:
         copy.start()
     even = 1.0 - lax.rem(lax.axis_index("row"), 2).astype(F32)
-    near = passed_ref[passed_ref.shape[0] - height :].astype(F32) * even
+    near = near_ref[...].astype(F32) * even
     answers = (own_ref[...] + near + far_ref[...].astype(F32)).astype(BF16)
     ak_ref[...] = answers[:, :columns]
     av_ref[...] = answers[:, columns:]
@@ -373,7 +372,7 @@
     own, spread = pl.pallas_call(
         pack_kernel,
         out_shape=[
-            jax.ShapeDtypeStruct((height, 2 * columns), BF16),
+            pltpu.VMEM((height, 2 * columns), BF16),
             jax.ShapeDtypeStruct((size // 2, own_prompt, 2 * columns), BF16),
         ],
     )(answer_keys, answer_values, prompt_keys, prompt_values)
@@ -422,11 +421,12 @@
         in_specs=[vmem, anywhere] + [vmem] * 4,
         scratch=[pltpu.VMEM((PARTS, window, lanes), F32), pltpu.SemaphoreType.DMA((kv_heads,))],
     )
-    keep, passed, far_terms, own_terms, chances, score_grad = call(
+    keep, passed, near_terms, far_terms, own_terms, chances, score_grad = call(
         terms_kernel,
         [
             pltpu.VMEM((half, 2 * columns), F32),
-            pltpu.VMEM((half + height, 2 * columns), BF16),
+            pltpu.VMEM((half, 2 * columns), BF16),
+            pltpu.VMEM((height, 2 * columns), BF16),
             pltpu.VMEM((height, 2 * columns), BF16),
             pltpu.VMEM((height, 2 * columns), F32),
             pltpu.HBM((*parts, prompt + window, lanes), BF16),
@@ -434,10 +434,10 @@
         ],
         4,
         [flat_queries, cotangent, powers, slopes, stats, same, other],
-        out_specs=[vmem] * 4 + [anywhere] * 2,
+        out_specs=[vmem] * 5 + [anywhere] * 2,
         scratch=[pltpu.VMEM((*parts, prompt + window, lanes), BF16)] * 2
         + [pltpu.VMEM((prompt + 3 * height, HEAD_DIM), F32)] * 2
-        + [pltpu.SemaphoreType.DMA((2, *parts))],
+        + [pltpu.SemaphoreType.DMA((2, kv_heads))],
     )
     whole = jax.ShapeDtypeStruct(queries.shape, BF16)
     attn_out, q_grad = call(
@@ -451,10 +451,10 @@
         + [pltpu.VMEM((*parts, prompt + window, lanes), BF16)] * 2
         + [pltpu.SemaphoreType.DMA((2, kv_heads))] * 2,
     )
-    passed = from_other_core(passed)
-    both = (keep + passed[:half].astype(F32)).astype(BF16)
-    far_terms = (far_terms.astype(F32) + jnp.where(odd, passed[half:].astype(F32), 0.0)).astype(BF16)
-    both, far_terms = lax.optimization_barrier((both, far_terms))
+    near_terms = from_other_core(near_terms)
+    far_terms = (far_terms.astype(F32) + jnp.where(odd, near_terms.astype(F32), 0.0)).astype(BF16)
+    passed, far_terms = lax.optimization_barrier((passed, far_terms))
+    both = (keep + from_other_core(passed).astype(F32)).astype(BF16)
     from_far = shifted(far_terms, -2)
     arrived = across_chips(both.reshape(size // 2, own_prompt, 2 * columns))
     answer_grad = jax.ShapeDtypeStruct((height, columns), BF16)
@@ -463,7 +463,7 @@
         sums_kernel,
         [answer_grad, answer_grad, prompt_grad, prompt_grad],
         0.1,
-        [own_terms, passed, from_far, arrived],
+        [own_terms, near_terms, from_far, arrived],
         out_specs=[anywhere] * 4,
         scratch=[pltpu.VMEM((height, columns), BF16)] * 2
         + [pltpu.VMEM((own_prompt, columns), F32)] * 2

time: 49.2 us -> 47.2 us (0.959)
  waiting for transfers between devices: 9.91 us -> 8.52 us
  other arithmetic: 1.74 us -> 0.8 us
  starting transfers between devices: 17.1 us -> 18 us
  Pallas kernels: 19.3 us -> 18.8 us
    ppermute x2, waiting for transfers between devices: 4.53 us -> 0.83 us  [shifted(): return lax.ppermute(x, 'row', pairs)]
    all_to_all x2, waiting for transfers between devices: 4.02 us -> 6.52 us  [across_chips(): return lax.all_to_all(x, 'row', 0, 0, tiled=True, axis_index_groups=groups)]
    select_n x1, other arithmetic: 0.98 us -> 0.03 us  [per_device(): near = from_other_core(jnp.where(odd, far, own))]
    reshape x0 -> x1, other arithmetic: none -> 0.69 us  [per_device(): arrived = across_chips(both.reshape(size // 2, own_prompt, 2 * columns))]
    convert_element_type x2 -> x1, other arithmetic: 0.77 us -> 0.08 us  [per_device(): (far_terms.astype(F32) + jnp.where(odd, near_terms.astype(F32), 0.0)).ast...]
    ppermute x3 -> x4, starting transfers between devices: 0.64 us -> 1.09 us  [from_other_core(): lax.ppermute(x, 'row', [(i, i ^ 1) for i in range(lax.axis_size('row'))])]
    ppermute x3 -> x4, waiting for transfers between devices: 1.35 us -> 1.17 us  [from_other_core(): lax.ppermute(x, 'row', [(i, i ^ 1) for i in range(lax.axis_size('row'))])]
  transfers between devices with their start and end apart: 7 -> 8, of which waited for: 5 -> 4; matrix products, arithmetic and copies ran while one was open for 2% -> 2% of each run, Pallas kernels for 23% -> 24%
where the time goes in v4:
time: 47.2 us; the launch traced here: 46.8 us
  Pallas kernels  18.8 us (40%)
  starting transfers between devices  18 us (38%)
  waiting for transfers between devices  8.52 us (18%)
  other arithmetic  0.8 us (2%)
  between operations  0.73 us (2%)
    pallas_call x5, Pallas kernels, call(): pl.pallas_call(kernel, out_shape=outs, scratch_shapes=list(scratch), comp...  17.2 us
    all_to_all x2, starting transfers between devices, across_chips(): return lax.all_to_all(x, 'row', 0, 0, tiled=True, axis_index_groups=groups)  10.8 us
    all_to_all x2, waiting for transfers between devices, across_chips(): return lax.all_to_all(x, 'row', 0, 0, tiled=True, axis_index_groups=groups)  6.52 us
    ppermute x2, starting transfers between devices, shifted(): return lax.ppermute(x, 'row', pairs)  6.13 us
    pallas_call x1, Pallas kernels, per_device(): pl.pallas_call(pack_kernel, out_shape=[pltpu.VMEM((height, 2 * columns),...  1.64 us
    ppermute x4, waiting for transfers between devices, from_other_core(): lax.ppermute(x, 'row', [(i, i ^ 1) for i in range(lax.axis_size('row'))])  1.17 us
    ppermute x4, starting transfers between devices, from_other_core(): lax.ppermute(x, 'row', [(i, i ^ 1) for i in range(lax.axis_size('row'))])  1.09 us
  transfers between devices with their start and end apart: 8, of which 4 were waited for; matrix products, arithmetic and copies ran while one was open for 2% of the time, Pallas kernels for 24%

profile of v4, /device:TPU:0, one launch (start us, length us, event | category | flops | bytes accessed | tf_op | source)
XLA Modules:
  0.0 46.8 jit_solution(9803452801159713637)
XLA Ops:
  0.6 1.6 %shard_map.128 = (bf16[128,1024]{1,0:T(8,128)(2,1)S(1)}, bf16[8,8,1024]{2,1,0:T(8,128)(2,1)}) custom-call(bf16[128,512]{1,0:T(8,128)(2,1)} %k_ref.1, bf16[128,512]{1,0:T(8,128)(2,1)} %v_ref.1, bf16[8,512]{1,0:T(8,128)(2,1)} %pk_ref.1, bf16[8,512]{1,0:T(8,128)(2,1)} %pv_ref.1), custom_call_target="tpu_custom_call" | custom-call | tf_op jit(solution)/shard_map/pallas_call | solution.py:372
  2.3 4.8 %collective-permute-start = (bf16[128,1024]{1,0:T(8,128)(2,1)S(1)}, bf16[128,1024]{1,0:T(8,128)(2,1)S(1)}, u32[]{:S(2)}, u32[]{:S(2)}) collective-permute-start(bf16[128,1024]{1,0:T(8,128)(2,1)S(1)} %get-tuple-element.35.own_ref), channel_id=1, source_target_pairs={{0,2},{1,3},{2,4},{3,5},{4,6},{5,7},{6,8},{7,9},{8,10},{9,11},{10,... | collective-permute-start | bytes 786440 | tf_op jit(solution)/shard_map/ppermute | solution.py:25
  7.1 4.9 %all-to-all-start = ((bf16[8,8,1024]{2,1,0:T(8,128)(2,1)}), bf16[8,8,1024]{2,1,0:T(8,128)(2,1)S(1)}, u32[]{:S(2)}, u32[]{:S(2)}) async-start(bf16[8,8,1024]{2,1,0:T(8,128)(2,1)} %get-tuple-element.36), calls=%async_computation | async-start | bytes 262144 | tf_op jit(solution)/shard_map/all_to_all | solution.py:35
  12.0 0.8 %collective-permute-done.far_ref = bf16[128,1024]{1,0:T(8,128)(2,1)S(1)} collective-permute-done((bf16[128,1024]{1,0:T(8,128)(2,1)S(1)}, bf16[128,1024]{1,0:T(8,128)(2,1)S(1)}, u32[]{:S(2)}, u32[]{:S(2)}) %collective-permute-start) | collective-permute-done | bytes 262176 | tf_op jit(solution)/shard_map/ppermute | solution.py:25
  12.9 0.1 collective-permute-start.1
  12.9 2.5 %shard_map.127 = (bf16[4,4,256,128]{3,2,1,0:T(8,128)(2,1)S(1)}, bf16[4,4,256,128]{3,2,1,0:T(8,128)(2,1)}, f32[4,8,256]{2,1,0:T(8,128)S(1)}) custom-call(s32[1,32]{1,0:T(1,128)} %bitcast.8, f32[1,128]{1,0:T(1,128)} %bitcast.9, bf16[128,4096]{1,0:T(8,128)(2,1)} %q_hbm.1, bf16[128,4096]{1,0:T(8,128)(2,1)} %do_hbm.1), custom_call_target="tpu_custom_call" | custom-call | flops 3000000000 | bytes 1000000 | tf_op jit(solution)/shard_map/pallas_call | solution.py:360
  15.5 3.9 %all-to-all-done = bf16[8,8,1024]{2,1,0:T(8,128)(2,1)S(1)} async-done(((bf16[8,8,1024]{2,1,0:T(8,128)(2,1)}), bf16[8,8,1024]{2,1,0:T(8,128)(2,1)S(1)}, u32[]{:S(2)}, u32[]{:S(2)}) %all-to-all-start) | async-done | bytes 131104 | tf_op jit(solution)/shard_map/all_to_all | solution.py:35
  19.3 0.0 collective-permute-done.1.near_ref
  19.4 0.0 collective-permute-start.2
  19.4 3.9 %shard_map.129 = (bf16[4,4,256,128]{3,2,1,0:T(8,128)(2,1)S(1)}, f32[4,4,288,256]{3,2,1,0:T(8,128)S(1)}, f32[4,4,288,256]{3,2,1,0:T(8,128)S(1)}, f32[4,4,8,256]{3,2,1,0:T(8,128)S(1)}) custom-call(bf16[4,4,256,128]{3,2,1,0:T(8,128)(2,1)S(1)} %get-tuple-element.32.qf_ref, bf16[4,4,256,128]{3,2,1,0:T(8,128)(2,1)} %get-tuple-element.33.cot_hbm, ...), custom_call_target="tpu_custom_call" | custom-call | flops 3000000000 | bytes 1000000 | tf_op jit(solution)/shard_map/pallas_call | solution.py:360
  23.3 0.0 collective-permute-done.2.other_ref
  23.3 5.2 %shard_map.130 = (f32[64,1024]{1,0:T(8,128)S(1)}, bf16[64,1024]{1,0:T(8,128)(2,1)S(1)}, bf16[128,1024]{1,0:T(8,128)(2,1)S(1)}, bf16[128,1024]{1,0:T(8,128)(2,1)S...) custom-call(bf16[4,4,256,128]{3,2,1,0:T(8,128)(2,1)S(1)} %get-tuple-element.32.qf_r, ...), custom_call_target="tpu_custom_call" | custom-call | flops 4000000000 | bytes 1000000 | tf_op jit(solution)/shard_map/pallas_call | solution.py:360
  28.5 0.6 %collective-permute-start.3 = (bf16[128,1024]{1,0:T(8,128)(2,1)S(1)}, bf16[128,1024]{1,0:T(8,128)(2,1)S(1)}, u32[]{:S(2)}, u32[]{:S(2)}) collective-permute-start(bf16[128,1024]{1,0:T(8,128)(2,1)S(1)} %get-tuple-element.48), channel_id=1, source_target_pairs={{0,1},{1,0},{2,3},{3,2},{4,5},{5,4},{6,7},{7,6},{8,9},{9,8},{10,11... | collective-permute-start | bytes 786440 | tf_op jit(solution)/shard_map/ppermute | solution.py:29
  29.1 1.2 %collective-permute-done.3.near_ref = bf16[128,1024]{1,0:T(8,128)(2,1)S(1)} collective-permute-done((bf16[128,1024]{1,0:T(8,128)(2,1)S(1)}, bf16[128,1024]{1,0:T(8,128)(2,1)S(1)}, u32[]{:S(2)}, u32[]{:S(2)}) %collective-permute-start.3) | collective-permute-done | bytes 262176 | tf_op jit(solution)/shard_map/ppermute | solution.py:29
  30.3 0.1 add_convert_fusion
  30.4 0.4 collective-permute-start.5
  30.8 1.3 %collective-permute-start.4 = (bf16[128,1024]{1,0:T(8,128)(2,1)S(1)}, bf16[128,1024]{1,0:T(8,128)(2,1)S(1)}, u32[]{:S(2)}, u32[]{:S(2)}) collective-permute-start(bf16[128,1024]{1,0:T(8,128)(2,1)S(1)} %add_convert_fusion), channel_id=1, source_target_pairs={{2,0},{3,1},{4,2},{5,3},{6,4},{7,5},{8,6},{9,7},{10,8},{11,9},{12,... | collective-permute-start | bytes 786440 | tf_op jit(solution)/shard_map/ppermute | solution.py:25
  32.1 0.0 collective-permute-done.5
  32.1 0.7 %fusion = bf16[8,8,1024]{2,1,0:T(8,128)(2,1)} fusion(f32[64,1024]{1,0:T(8,128)S(1)} %get-tuple-element.52, bf16[64,1024]{1,0:T(8,128)(2,1)S(1)} %collective-permute-done.5), kind=kLoop, calls=%fused_computation.3 | loop fusion | flops 196608 | bytes 524288 | tf_op jit(solution)/shard_map/reshape | solution.py:459
  32.8 5.9 %all-to-all-start.1 = ((bf16[8,8,1024]{2,1,0:T(8,128)(2,1)}), bf16[8,8,1024]{2,1,0:T(8,128)(2,1)S(1)}, u32[]{:S(2)}, u32[]{:S(2)}) async-start(bf16[8,8,1024]{2,1,0:T(8,128)(2,1)} %fusion), calls=%async_computation.1 | async-start | bytes 262144 | tf_op jit(solution)/shard_map/all_to_all | solution.py:35
  38.7 4.7 %shard_map.131 = (bf16[128,4096]{1,0:T(8,128)(2,1)}, bf16[128,4096]{1,0:T(8,128)(2,1)}) custom-call(bf16[4,4,416,256]{3,2,1,0:T(8,128)(2,1)} %get-tuple-element.43.chances_hbm, bf16[4,4,416,256]{3,2,1,0:T(8,128)(2,1)} %get-tuple-element.44.grad_hbm, bf16[64,1024]{1,0:T(8,128)(2,1)S(1)} %bitcast.7, bf16[64,1024]{1,0:T(8,128)(2,1)S(1)} %collective-permute-done.2.other_ref, ...), custom_call_target="tpu_custom_call" | custom-call | flops 5000000000 | bytes 1000000 | tf_op jit(solution)/shard_map/pallas_call | solution.py:360
  43.4 0.0 collective-permute-done.4.far_ref
  43.4 2.6 %all-to-all-done.1.arrived_ref = bf16[8,8,1024]{2,1,0:T(8,128)(2,1)S(1)} async-done(((bf16[8,8,1024]{2,1,0:T(8,128)(2,1)}), bf16[8,8,1024]{2,1,0:T(8,128)(2,1)S(1)}, u32[]{:S(2)}, u32[]{:S(2)}) %all-to-all-start.1) | async-done | bytes 131104 | tf_op jit(solution)/shard_map/all_to_all | solution.py:35
  46.0 0.8 %shard_map.132 = (bf16[128,512]{1,0:T(8,128)(2,1)}, bf16[128,512]{1,0:T(8,128)(2,1)}, f32[8,512]{1,0:T(8,128)}, f32[8,512]{1,0:T(8,128)}) custom-call(f32[128,1024]{1,0:T(8,128)S(1)} %get-tuple-element.47.own_ref, bf16[128,1024]{1,0:T(8,128)(2,1)S(1)} %collective-permute-done.3.near_ref, bf16[128,1024]{1,0:T(8,128)(2,1)S(1)} %collective-permute-done.4.far_ref, ...), custom_call_target="tpu_custom_call" | custom-call | flops 100000000 | bytes 1000000 | tf_op jit(solution)/shard_map/pallas_call | solution.py:360
  (1 shorter events, 0.0 us)
Async XLA Ops:
  2.3 10.6 %collective-permute-start = (bf16[128,1024]{1,0:T(8,128)(2,1)S(1)}, bf16[128,1024]{1,0:T(8,128)(2,1)S(1)}, u32[]{:S(2)}, u32[]{:S(2)}) collective-permute-start(bf16[128,1024]{1,0:T(8,128)(2,1)S(1)} %get-tuple-element.35.own_ref), channel_id=1, source_target_pairs={{0,2},{1,3},{2,4},{3,5},{4,6},{5,7},{6,8},{7,9},{8,10},{9,11},{10,... | collective-permute-start | bytes 786440 | tf_op jit(solution)/shard_map/ppermute | solution.py:25
  7.1 12.2 %all-to-all-start = ((bf16[8,8,1024]{2,1,0:T(8,128)(2,1)}), bf16[8,8,1024]{2,1,0:T(8,128)(2,1)S(1)}, u32[]{:S(2)}, u32[]{:S(2)}) async-start(bf16[8,8,1024]{2,1,0:T(8,128)(2,1)} %get-tuple-element.36), calls=%async_computation | async-start | bytes 262144 | tf_op jit(solution)/shard_map/all_to_all | solution.py:35
  12.9 6.5 %collective-permute-start.1 = (bf16[128,1024]{1,0:T(8,128)(2,1)S(1)}, bf16[128,1024]{1,0:T(8,128)(2,1)S(1)}, u32[]{:S(2)}, u32[]{:S(2)}) collective-permute-start(bf16[128,1024]{1,0:T(8,128)(2,1)S(1)} %broadcast_select_fusion), channel_id=1, source_target_pairs={{0,1},{1,0},{2,3},{3,2},{4,5},{5,4},{6,7},{7,6},{8,9},{9,8},{10,11... | collective-permute-start | bytes 786440 | tf_op jit(solution)/shard_map/ppermute | solution.py:29
  19.4 3.9 %collective-permute-start.2 = (bf16[64,1024]{1,0:T(8,128)(2,1)S(1)}, bf16[64,1024]{1,0:T(8,128)(2,1)S(1)}, u32[]{:S(2)}, u32[]{:S(2)}) collective-permute-start(bf16[64,1024]{1,0:T(8,128)(2,1)S(1)} %bitcast.5), channel_id=1, source_target_pairs={{0,1},{1,0},{2,3},{3,2},{4,5},{5,4},{6,7},{7,6},{8,9},{9,8},{10,11... | collective-permute-start | bytes 393224 | tf_op jit(solution)/shard_map/ppermute | solution.py:29
  28.5 1.7 %collective-permute-start.3 = (bf16[128,1024]{1,0:T(8,128)(2,1)S(1)}, bf16[128,1024]{1,0:T(8,128)(2,1)S(1)}, u32[]{:S(2)}, u32[]{:S(2)}) collective-permute-start(bf16[128,1024]{1,0:T(8,128)(2,1)S(1)} %get-tuple-element.48), channel_id=1, source_target_pairs={{0,1},{1,0},{2,3},{3,2},{4,5},{5,4},{6,7},{7,6},{8,9},{9,8},{10,11... | collective-permute-start | bytes 786440 | tf_op jit(solution)/shard_map/ppermute | solution.py:29
  30.4 1.7 %collective-permute-start.5 = (bf16[64,1024]{1,0:T(8,128)(2,1)S(1)}, bf16[64,1024]{1,0:T(8,128)(2,1)S(1)}, u32[]{:S(2)}, u32[]{:S(2)}) collective-permute-start(bf16[64,1024]{1,0:T(8,128)(2,1)S(1)} %get-tuple-element.53), channel_id=1, source_target_pairs={{0,1},{1,0},{2,3},{3,2},{4,5},{5,4},{6,7},{7,6},{8,9},{9,8},{10,11... | collective-permute-start | bytes 393224 | tf_op jit(solution)/shard_map/ppermute | solution.py:29
  30.8 12.6 %collective-permute-start.4 = (bf16[128,1024]{1,0:T(8,128)(2,1)S(1)}, bf16[128,1024]{1,0:T(8,128)(2,1)S(1)}, u32[]{:S(2)}, u32[]{:S(2)}) collective-permute-start(bf16[128,1024]{1,0:T(8,128)(2,1)S(1)} %add_convert_fusion), channel_id=1, source_target_pairs={{2,0},{3,1},{4,2},{5,3},{6,4},{7,5},{8,6},{9,7},{10,8},{11,9},{12,... | collective-permute-start | bytes 786440 | tf_op jit(solution)/shard_map/ppermute | solution.py:25
  32.8 13.2 %all-to-all-start.1 = ((bf16[8,8,1024]{2,1,0:T(8,128)(2,1)}), bf16[8,8,1024]{2,1,0:T(8,128)(2,1)S(1)}, u32[]{:S(2)}, u32[]{:S(2)}) async-start(bf16[8,8,1024]{2,1,0:T(8,128)(2,1)} %fusion), calls=%async_computation.1 | async-start | bytes 262144 | tf_op jit(solution)/shard_map/all_to_all | solution.py:35

commit v5 on v4

--- a/solution.py
+++ b/solution.py
@@ -17,6 +17,7 @@
 VMEM_LIMIT = 32 * 2**20
 LAYOUT_GFLOP = 3
 OUTPUTS_GFLOP = 5
+STORE_GFLOP = 1
 
 
 def shifted(x, by):
@@ -90,7 +91,8 @@
 
 
 def columns_of(g, width=HEAD_DIM):
-    return pl.ds(pl.multiple_of(g * width, width), width)
+    begin = g * width
+    return pl.ds(begin if isinstance(begin, int) else pl.multiple_of(begin, width), width)
 
 
 def stack(refs, cols):
@@ -160,34 +162,43 @@
     for part in range(PARTS):
         bias_ref[part] = window_bias(begin_ref[part, 0:1], window, rows)
 
-    def head(g):
-        arrival(g).wait()
+    def powers_head(g):
         keys = stack((far_ref, near_ref, own_ref), columns_of(g))
-        values = stack((far_ref, near_ref, own_ref), columns_of(g + kv_heads))
 
         def score(part, _):
-            at = slice(part * rows, part * rows + window)
-            return dot_nt(keys[at], qf_ref[g, part]), dot_nt(values[at], cot_ref[g, part])
-
-        def weigh(part, held):
-            scores, slopes = held
+            return dot_nt(keys[part * rows : part * rows + window], qf_ref[g, part])
+
+        def weigh(part, scores):
             scores = scores + bias_ref[part]
             highest = jnp.max(scores, axis=0, keepdims=True)
             powers = jnp.exp2((scores - highest) * EXPONENT)
             powers_ref[g, part] = powers
-            slopes_ref[g, part] = slopes
             stats_ref[g, part, 0:1] = highest
             stats_ref[g, part, 1:2] = jnp.sum(powers, axis=0, keepdims=True)
-            stats_ref[g, part, 2:3] = jnp.sum(powers * slopes, axis=0, keepdims=True)
 
         staged(score, weigh)
 
-    for_heads(kv_heads, head)
+    def slopes_head(g):
+        arrival(g).wait()
+        values = stack((far_ref, near_ref, own_ref), columns_of(g + kv_heads))
+
+        def slope(part, _):
+            return dot_nt(values[part * rows : part * rows + window], cot_ref[g, part])
+
+        def add(part, slopes):
+            slopes_ref[g, part] = slopes
+            stats_ref[g, part, 2:3] = jnp.sum(powers_ref[g, part] * slopes, axis=0, keepdims=True)
+
+        staged(slope, add)
+
+    for_heads(kv_heads, powers_head)
+    for_heads(kv_heads, slopes_head)
 
 
 def terms_kernel(
     qf_ref, cot_ref, powers_ref, slopes_ref, stats_ref, same_ref, other_ref,
-    keep_ref, pass_ref, near_ref, far_ref, own_ref, chances_hbm, grad_hbm, chances_ref, grad_ref, dk_ref, dv_ref, sems,
+    keep_ref, pass_ref, near_ref, far_ref, own_ref, chances_hbm, grad_hbm, last_chances_ref, last_grad_ref,
+    chances_ref, grad_ref, dk_ref, dv_ref, sems,
 ):
     kv_heads = qf_ref.shape[0]
     window = powers_ref.shape[2]
@@ -202,7 +213,7 @@
             pltpu.make_async_copy(grad_ref.at[g], grad_hbm.at[g], sems.at[1, g]),
         )
 
-    def head(g):
+    def head(g, chances_to, grad_to):
         keys = stack((same_ref, other_ref), columns_of(g))
         values = stack((same_ref, other_ref), columns_of(g + kv_heads))
         dk_ref[...] = jnp.zeros_like(dk_ref)
@@ -221,22 +232,20 @@
             scale = fade * inverse
             chances = powers * inverse
             delta = jnp.sum(chances * slopes, axis=0, keepdims=True) + scale * window_delta
-            chances_ref[g, part, :prompt] = chances.astype(BF16)
-            grad_ref[g, part, :prompt] = (chances * (slopes - delta)).astype(BF16)
+            chances_to[part, :prompt] = chances.astype(BF16)
+            grad_to[part, :prompt] = (chances * (slopes - delta)).astype(BF16)
             chances = powers_ref[g, part] * scale
-            chances_ref[g, part, prompt:] = chances.astype(BF16)
-            grad_ref[g, part, prompt:] = (chances * (slopes_ref[g, part] - delta)).astype(BF16)
+            chances_to[part, prompt:] = chances.astype(BF16)
+            grad_to[part, prompt:] = (chances * (slopes_ref[g, part] - delta)).astype(BF16)
 
         def gather(part, _):
             begin = prompt + part * rows
-            for ref, former, latter in ((dk_ref, grad_ref, qf_ref), (dv_ref, chances_ref, cot_ref)):
-                terms = dot_nn(former[g, part], latter[g, part])
+            for ref, former, latter in ((dk_ref, grad_to, qf_ref), (dv_ref, chances_to, cot_ref)):
+                terms = dot_nn(former[part], latter[g, part])
                 ref[:prompt] += terms[:prompt]
                 ref[begin : begin + window] += terms[prompt:]
 
         staged(score, weigh, gather)
-        for copy in copies(g):
-            copy.start()
         far, near, own = (slice(prompt + i * height, prompt + (i + 1) * height) for i in range(3))
         for ref, into, source in (
             (keep_ref, slice(0, half), slice(0, half)),
@@ -248,17 +257,35 @@
             ref[into, columns_of(g)] = (dk_ref[source] * FACTOR).astype(ref.dtype)
             ref[into, columns_of(g + kv_heads)] = dv_ref[source].astype(ref.dtype)
 
-    for_heads(kv_heads, head)
-    for g in range(kv_heads):
+    def stored_head(g):
+        head(g, chances_ref.at[g], grad_ref.at[g])
+        for copy in copies(g):
+            copy.start()
+
+    for_heads(kv_heads - 1, stored_head)
+    head(kv_heads - 1, last_chances_ref, last_grad_ref)
+    for g in range(kv_heads - 1):
         for copy in copies(g):
             copy.wait()
 
 
+def store_kernel(chances_ref, grad_ref, chances_hbm, grad_hbm, sems):
+    copies = [
+        pltpu.make_async_copy(chances_ref, chances_hbm, sems.at[0]),
+        pltpu.make_async_copy(grad_ref, grad_hbm, sems.at[1]),
+    ]
+    for copy in copies:
+        copy.start()
+    for copy in copies:
+        copy.wait()
+
+
 def outputs_kernel(
-    chances_hbm, grad_hbm, same_ref, other_ref, far_ref, near_ref, own_ref, out_hbm, dq_hbm,
+    chances_hbm, grad_hbm, last_chances_hbm, last_grad_hbm, same_ref, other_ref, far_ref, near_ref, own_ref,
+    out_hbm, dq_hbm,
     out_ref, dq_ref, chances_ref, grad_ref, sems, in_sems,
 ):
-    kv_heads = chances_hbm.shape[0]
+    kv_heads = out_ref.shape[0]
     height = far_ref.shape[0]
     prompt = 2 * same_ref.shape[0]
     rows = height // PARTS
@@ -277,18 +304,24 @@
             pltpu.make_async_copy(dq_ref.at[g], dq_hbm.at[:, cols], sems.at[1, g]),
         )
 
-    def arrivals(g):
+    def arrivals(g, chances_from, grad_from):
         return (
-            pltpu.make_async_copy(chances_hbm.at[g], chances_ref.at[g], in_sems.at[0, g]),
-            pltpu.make_async_copy(grad_hbm.at[g], grad_ref.at[g], in_sems.at[1, g]),
+            pltpu.make_async_copy(chances_from, chances_ref.at[g], in_sems.at[0, g]),
+            pltpu.make_async_copy(grad_from, grad_ref.at[g], in_sems.at[1, g]),
         )
 
-    for g in range(kv_heads):
-        for copy in arrivals(g):
+    def stored(g):
+        return arrivals(g, chances_hbm.at[g], grad_hbm.at[g])
+
+    last = arrivals(kv_heads - 1, last_chances_hbm, last_grad_hbm)
+    for g in range(kv_heads - 1):
+        for copy in stored(g):
             copy.start()
-
-    def head(g):
-        for copy in arrivals(g):
+    for copy in last:
+        copy.start()
+
+    def head(g, arriving):
+        for copy in arriving:
             copy.wait()
         keys_t = transposed(stack(refs, columns_of(g)))
         values_t = transposed(stack(refs, columns_of(g + kv_heads)))
@@ -308,7 +341,8 @@
         for copy in copies(g):
             copy.start()
 
-    for_heads(kv_heads, head)
+    for_heads(kv_heads - 1, lambda g: head(g, stored(g)))
+    head(kv_heads - 1, last)
     for g in range(kv_heads):
         for copy in copies(g):
             copy.wait()
@@ -421,7 +455,7 @@
         in_specs=[vmem, anywhere] + [vmem] * 4,
         scratch=[pltpu.VMEM((PARTS, window, lanes), F32), pltpu.SemaphoreType.DMA((kv_heads,))],
     )
-    keep, passed, near_terms, far_terms, own_terms, chances, score_grad = call(
+    keep, passed, near_terms, far_terms, own_terms, chances, score_grad, last_chances, last_grad = call(
         terms_kernel,
         [
             pltpu.VMEM((half, 2 * columns), F32),
@@ -429,29 +463,40 @@
             pltpu.VMEM((height, 2 * columns), BF16),
             pltpu.VMEM((height, 2 * columns), BF16),
             pltpu.VMEM((height, 2 * columns), F32),
-            pltpu.HBM((*parts, prompt + window, lanes), BF16),
-            pltpu.HBM((*parts, prompt + window, lanes), BF16),
+            pltpu.HBM((kv_heads - 1, PARTS, prompt + window, lanes), BF16),
+            pltpu.HBM((kv_heads - 1, PARTS, prompt + window, lanes), BF16),
+            pltpu.VMEM((PARTS, prompt + window, lanes), BF16),
+            pltpu.VMEM((PARTS, prompt + window, lanes), BF16),
         ],
         4,
         [flat_queries, cotangent, powers, slopes, stats, same, other],
-        out_specs=[vmem] * 5 + [anywhere] * 2,
-        scratch=[pltpu.VMEM((*parts, prompt + window, lanes), BF16)] * 2
+        out_specs=[vmem] * 5 + [anywhere] * 2 + [vmem] * 2,
+        scratch=[pltpu.VMEM((kv_heads - 1, PARTS, prompt + window, lanes), BF16)] * 2
         + [pltpu.VMEM((prompt + 3 * height, HEAD_DIM), F32)] * 2
         + [pltpu.SemaphoreType.DMA((2, kv_heads))],
     )
+    last_chances, last_grad = call(
+        store_kernel,
+        [pltpu.HBM((PARTS, prompt + window, lanes), BF16)] * 2,
+        STORE_GFLOP,
+        [last_chances, last_grad],
+        in_specs=[vmem] * 2,
+        out_specs=[anywhere] * 2,
+        scratch=[pltpu.SemaphoreType.DMA((2,))],
+    )
+    near_terms, last_chances = lax.optimization_barrier((from_other_core(near_terms), last_chances))
     whole = jax.ShapeDtypeStruct(queries.shape, BF16)
     attn_out, q_grad = call(
         outputs_kernel,
         [whole, whole],
         OUTPUTS_GFLOP,
-        [*in_hbm(chances, score_grad), same, other, far, near, own],
-        in_specs=[anywhere] * 2 + [vmem] * 5,
+        [*in_hbm(chances, score_grad, last_chances, last_grad), same, other, far, near, own],
+        in_specs=[anywhere] * 4 + [vmem] * 5,
         out_specs=[anywhere, anywhere],
         scratch=[pltpu.VMEM((kv_heads, height, span), BF16)] * 2
         + [pltpu.VMEM((*parts, prompt + window, lanes), BF16)] * 2
         + [pltpu.SemaphoreType.DMA((2, kv_heads))] * 2,
     )
-    near_terms = from_other_core(near_terms)
     far_terms = (far_terms.astype(F32) + jnp.where(odd, near_terms.astype(F32), 0.0)).astype(BF16)
     passed, far_terms = lax.optimization_barrier((passed, far_terms))
     both = (keep + from_other_core(passed).astype(F32)).astype(BF16)

time: 47.2 us -> 46.1 us (0.977)
  waiting for transfers between devices: 8.52 us -> 7.39 us
    ppermute x4, waiting for transfers between devices: 1.17 us -> 0.01 us  [from_other_core(): lax.ppermute(x, 'row', [(i, i ^ 1) for i in range(lax.axis_size('row'))])]
    pallas_call x5 -> x6, Pallas kernels: 17.2 us -> 17.1 us  [call(): pl.pallas_call(kernel, out_shape=outs, scratch_shapes=list(scratch), comp...]
  transfers between devices with their start and end apart: 8 -> 8, of which waited for: 4 -> 3; matrix products, arithmetic and copies ran while one was open for 2% -> 2% of each run, Pallas kernels for 24% -> 27%
where the time goes in v5:
time: 46.1 us; the launch traced here: 45.6 us
  Pallas kernels  18.7 us (41%)
  starting transfers between devices  18 us (39%)
  waiting for transfers between devices  7.39 us (16%)
  other arithmetic  0.81 us (2%)
  between operations  0.74 us (2%)
    pallas_call x6, Pallas kernels, call(): pl.pallas_call(kernel, out_shape=outs, scratch_shapes=list(scratch), comp...  17.1 us
    all_to_all x2, starting transfers between devices, across_chips(): return lax.all_to_all(x, 'row', 0, 0, tiled=True, axis_index_groups=groups)  10.9 us
    all_to_all x2, waiting for transfers between devices, across_chips(): return lax.all_to_all(x, 'row', 0, 0, tiled=True, axis_index_groups=groups)  6.55 us
    ppermute x2, starting transfers between devices, shifted(): return lax.ppermute(x, 'row', pairs)  6.13 us
    pallas_call x1, Pallas kernels, per_device(): pl.pallas_call(pack_kernel, out_shape=[pltpu.VMEM((height, 2 * columns),...  1.64 us
    ppermute x4, starting transfers between devices, from_other_core(): lax.ppermute(x, 'row', [(i, i ^ 1) for i in range(lax.axis_size('row'))])  0.98 us
  transfers between devices with their start and end apart: 8, of which 3 were waited for; matrix products, arithmetic and copies ran while one was open for 2% of the time, Pallas kernels for 27%

profile of v5, /device:TPU:0, one launch (start us, length us, event | category | flops | bytes accessed | tf_op | source)
XLA Modules:
  0.0 45.6 jit_solution(2964246114490285434)
XLA Ops:
  0.6 1.6 %shard_map.128 = (bf16[128,1024]{1,0:T(8,128)(2,1)S(1)}, bf16[8,8,1024]{2,1,0:T(8,128)(2,1)}) custom-call(bf16[128,512]{1,0:T(8,128)(2,1)} %k_ref.1, bf16[128,512]{1,0:T(8,128)(2,1)} %v_ref.1, bf16[8,512]{1,0:T(8,128)(2,1)} %pk_ref.1, bf16[8,512]{1,0:T(8,128)(2,1)} %pv_ref.1), custom_call_target="tpu_custom_call" | custom-call | tf_op jit(solution)/shard_map/pallas_call | solution.py:406
  2.3 4.8 %collective-permute-start = (bf16[128,1024]{1,0:T(8,128)(2,1)S(1)}, bf16[128,1024]{1,0:T(8,128)(2,1)S(1)}, u32[]{:S(2)}, u32[]{:S(2)}) collective-permute-start(bf16[128,1024]{1,0:T(8,128)(2,1)S(1)} %get-tuple-element.41.own_ref), channel_id=1, source_target_pairs={{0,2},{1,3},{2,4},{3,5},{4,6},{5,7},{6,8},{7,9},{8,10},{9,11},{10,... | collective-permute-start | bytes 786440 | tf_op jit(solution)/shard_map/ppermute | solution.py:26
  7.1 4.9 %all-to-all-start = ((bf16[8,8,1024]{2,1,0:T(8,128)(2,1)}), bf16[8,8,1024]{2,1,0:T(8,128)(2,1)S(1)}, u32[]{:S(2)}, u32[]{:S(2)}) async-start(bf16[8,8,1024]{2,1,0:T(8,128)(2,1)} %get-tuple-element.42), calls=%async_computation | async-start | bytes 262144 | tf_op jit(solution)/shard_map/all_to_all | solution.py:36
  12.0 0.8 %collective-permute-done.far_ref = bf16[128,1024]{1,0:T(8,128)(2,1)S(1)} collective-permute-done((bf16[128,1024]{1,0:T(8,128)(2,1)S(1)}, bf16[128,1024]{1,0:T(8,128)(2,1)S(1)}, u32[]{:S(2)}, u32[]{:S(2)}) %collective-permute-start) | collective-permute-done | bytes 262176 | tf_op jit(solution)/shard_map/ppermute | solution.py:26
  12.9 0.1 collective-permute-start.1
  12.9 2.5 %shard_map.127 = (bf16[4,4,256,128]{3,2,1,0:T(8,128)(2,1)S(1)}, bf16[4,4,256,128]{3,2,1,0:T(8,128)(2,1)}, f32[4,8,256]{2,1,0:T(8,128)S(1)}) custom-call(s32[1,32]{1,0:T(1,128)} %bitcast.8, f32[1,128]{1,0:T(1,128)} %bitcast.9, bf16[128,4096]{1,0:T(8,128)(2,1)} %q_hbm.1, bf16[128,4096]{1,0:T(8,128)(2,1)} %do_hbm.1), custom_call_target="tpu_custom_call" | custom-call | flops 3000000000 | bytes 1000000 | tf_op jit(solution)/shard_map/pallas_call | solution.py:394
  15.5 3.9 %all-to-all-done = bf16[8,8,1024]{2,1,0:T(8,128)(2,1)S(1)} async-done(((bf16[8,8,1024]{2,1,0:T(8,128)(2,1)}), bf16[8,8,1024]{2,1,0:T(8,128)(2,1)S(1)}, u32[]{:S(2)}, u32[]{:S(2)}) %all-to-all-start) | async-done | bytes 131104 | tf_op jit(solution)/shard_map/all_to_all | solution.py:36
  19.3 0.0 collective-permute-done.1.near_ref
  19.4 0.0 collective-permute-start.2
  19.4 3.7 %shard_map.129 = (bf16[4,4,256,128]{3,2,1,0:T(8,128)(2,1)S(1)}, f32[4,4,288,256]{3,2,1,0:T(8,128)S(1)}, f32[4,4,288,256]{3,2,1,0:T(8,128)S(1)}, f32[4,4,8,256]{3,2,1,0:T(8,128)S(1)}) custom-call(bf16[4,4,256,128]{3,2,1,0:T(8,128)(2,1)S(1)} %get-tuple-element.38.qf_ref, bf16[4,4,256,128]{3,2,1,0:T(8,128)(2,1)} %get-tuple-element.39.cot_hbm, ...), custom_call_target="tpu_custom_call" | custom-call | flops 3000000000 | bytes 1000000 | tf_op jit(solution)/shard_map/pallas_call | solution.py:394
  23.0 0.0 collective-permute-done.2.other_ref
  23.0 4.2 %shard_map.130 = (f32[64,1024]{1,0:T(8,128)S(1)}, bf16[64,1024]{1,0:T(8,128)(2,1)S(1)}, bf16[128,1024]{1,0:T(8,128)(2,1)S(1)}, bf16[128,1024]{1,0:T(8,128)(2,1)S...) custom-call(bf16[4,4,256,128]{3,2,1,0:T(8,128)(2,1)S(1)} %get-tuple-, ...), custom_call_target="tpu_custom_call" | custom-call | flops 4000000000 | bytes 1000000 | tf_op jit(solution)/shard_map/pallas_call | solution.py:394
  27.2 0.6 %collective-permute-start.3 = (bf16[128,1024]{1,0:T(8,128)(2,1)S(1)}, bf16[128,1024]{1,0:T(8,128)(2,1)S(1)}, u32[]{:S(2)}, u32[]{:S(2)}) collective-permute-start(bf16[128,1024]{1,0:T(8,128)(2,1)S(1)} %get-tuple-element.51), channel_id=1, source_target_pairs={{0,1},{1,0},{2,3},{3,2},{4,5},{5,4},{6,7},{7,6},{8,9},{9,8},{10,11... | collective-permute-start | bytes 786440 | tf_op jit(solution)/shard_map/ppermute | solution.py:30
  27.8 1.3 %shard_map.131 = (bf16[4,416,256]{2,1,0:T(8,128)(2,1)}, bf16[4,416,256]{2,1,0:T(8,128)(2,1)}) custom-call(bf16[4,416,256]{2,1,0:T(8,128)(2,1)S(1)} %get-tuple-element.52.chances_ref, bf16[4,416,256]{2,1,0:T(8,128)(2,1)S(1)} %get-tuple-element.53.grad_ref), custom_call_target="tpu_custom_call" | custom-call | flops 1000000000 | bytes 1000000 | tf_op jit(solution)/shard_map/pallas_call | solution.py:394
  29.1 0.0 collective-permute-done.3.near_ref
  29.1 0.1 add_convert_fusion
  29.2 0.3 collective-permute-start.5
  29.5 1.3 %collective-permute-start.4 = (bf16[128,1024]{1,0:T(8,128)(2,1)S(1)}, bf16[128,1024]{1,0:T(8,128)(2,1)S(1)}, u32[]{:S(2)}, u32[]{:S(2)}) collective-permute-start(bf16[128,1024]{1,0:T(8,128)(2,1)S(1)} %add_convert_fusion), channel_id=1, source_target_pairs={{2,0},{3,1},{4,2},{5,3},{6,4},{7,5},{8,6},{9,7},{10,8},{11,9},{12,... | collective-permute-start | bytes 786440 | tf_op jit(solution)/shard_map/ppermute | solution.py:26
  30.8 0.0 collective-permute-done.5
  30.8 0.7 %fusion = bf16[8,8,1024]{2,1,0:T(8,128)(2,1)} fusion(f32[64,1024]{1,0:T(8,128)S(1)} %get-tuple-element.64, bf16[64,1024]{1,0:T(8,128)(2,1)S(1)} %collective-permute-done.5), kind=kLoop, calls=%fused_computation.3 | loop fusion | flops 196608 | bytes 524288 | tf_op jit(solution)/shard_map/reshape | solution.py:504
  31.5 6.0 %all-to-all-start.1 = ((bf16[8,8,1024]{2,1,0:T(8,128)(2,1)}), bf16[8,8,1024]{2,1,0:T(8,128)(2,1)S(1)}, u32[]{:S(2)}, u32[]{:S(2)}) async-start(bf16[8,8,1024]{2,1,0:T(8,128)(2,1)} %fusion), calls=%async_computation.1 | async-start | bytes 262144 | tf_op jit(solution)/shard_map/all_to_all | solution.py:36
  37.5 4.7 %shard_map.132 = (bf16[128,4096]{1,0:T(8,128)(2,1)}, bf16[128,4096]{1,0:T(8,128)(2,1)}) custom-call(bf16[3,4,416,256]{3,2,1,0:T(8,128)(2,1)} %get-tuple-element.49.chances_hbm, bf16[3,4,416,256]{3,2,1,0:T(8,128)(2,1)} %get-tuple-element.50.grad_hbm, bf16[4,416,256]{2,1,0:T(8,128)(2,1)} %get-tuple-element.55.last_chances_hbm, ...), custom_call_target="tpu_custom_call" | custom-call | flops 5000000000 | bytes 1000000 | tf_op jit(solution)/shard_map/pallas_call | solution.py:394
  42.1 0.0 collective-permute-done.4.far_ref
  42.2 2.7 %all-to-all-done.1.arrived_ref = bf16[8,8,1024]{2,1,0:T(8,128)(2,1)S(1)} async-done(((bf16[8,8,1024]{2,1,0:T(8,128)(2,1)}), bf16[8,8,1024]{2,1,0:T(8,128)(2,1)S(1)}, u32[]{:S(2)}, u32[]{:S(2)}) %all-to-all-start.1) | async-done | bytes 131104 | tf_op jit(solution)/shard_map/all_to_all | solution.py:36
  44.8 0.8 %shard_map.133 = (bf16[128,512]{1,0:T(8,128)(2,1)}, bf16[128,512]{1,0:T(8,128)(2,1)}, f32[8,512]{1,0:T(8,128)}, f32[8,512]{1,0:T(8,128)}) custom-call(f32[128,1024]{1,0:T(8,128)S(1)} %get-tuple-element.59.own_ref, bf16[128,1024]{1,0:T(8,128)(2,1)S(1)} %collective-permute-done.3.near_ref, bf16[128,1024]{1,0:T(8,128)(2,1)S(1)} %collective-permute-done.4.far_ref, ...), custom_call_target="tpu_custom_call" | custom-call | flops 100000000 | bytes 1000000 | tf_op jit(solution)/shard_map/pallas_call | solution.py:394
  (1 shorter events, 0.0 us)
Async XLA Ops:
  2.3 10.6 %collective-permute-start = (bf16[128,1024]{1,0:T(8,128)(2,1)S(1)}, bf16[128,1024]{1,0:T(8,128)(2,1)S(1)}, u32[]{:S(2)}, u32[]{:S(2)}) collective-permute-start(bf16[128,1024]{1,0:T(8,128)(2,1)S(1)} %get-tuple-element.41.own_ref), channel_id=1, source_target_pairs={{0,2},{1,3},{2,4},{3,5},{4,6},{5,7},{6,8},{7,9},{8,10},{9,11},{10,... | collective-permute-start | bytes 786440 | tf_op jit(solution)/shard_map/ppermute | solution.py:26
  7.1 12.2 %all-to-all-start = ((bf16[8,8,1024]{2,1,0:T(8,128)(2,1)}), bf16[8,8,1024]{2,1,0:T(8,128)(2,1)S(1)}, u32[]{:S(2)}, u32[]{:S(2)}) async-start(bf16[8,8,1024]{2,1,0:T(8,128)(2,1)} %get-tuple-element.42), calls=%async_computation | async-start | bytes 262144 | tf_op jit(solution)/shard_map/all_to_all | solution.py:36
  12.9 6.5 %collective-permute-start.1 = (bf16[128,1024]{1,0:T(8,128)(2,1)S(1)}, bf16[128,1024]{1,0:T(8,128)(2,1)S(1)}, u32[]{:S(2)}, u32[]{:S(2)}) collective-permute-start(bf16[128,1024]{1,0:T(8,128)(2,1)S(1)} %broadcast_select_fusion), channel_id=1, source_target_pairs={{0,1},{1,0},{2,3},{3,2},{4,5},{5,4},{6,7},{7,6},{8,9},{9,8},{10,11... | collective-permute-start | bytes 786440 | tf_op jit(solution)/shard_map/ppermute | solution.py:30
  19.4 3.7 %collective-permute-start.2 = (bf16[64,1024]{1,0:T(8,128)(2,1)S(1)}, bf16[64,1024]{1,0:T(8,128)(2,1)S(1)}, u32[]{:S(2)}, u32[]{:S(2)}) collective-permute-start(bf16[64,1024]{1,0:T(8,128)(2,1)S(1)} %bitcast.5), channel_id=1, source_target_pairs={{0,1},{1,0},{2,3},{3,2},{4,5},{5,4},{6,7},{7,6},{8,9},{9,8},{10,11... | collective-permute-start | bytes 393224 | tf_op jit(solution)/shard_map/ppermute | solution.py:30
  27.2 1.8 %collective-permute-start.3 = (bf16[128,1024]{1,0:T(8,128)(2,1)S(1)}, bf16[128,1024]{1,0:T(8,128)(2,1)S(1)}, u32[]{:S(2)}, u32[]{:S(2)}) collective-permute-start(bf16[128,1024]{1,0:T(8,128)(2,1)S(1)} %get-tuple-element.51), channel_id=1, source_target_pairs={{0,1},{1,0},{2,3},{3,2},{4,5},{5,4},{6,7},{7,6},{8,9},{9,8},{10,11... | collective-permute-start | bytes 786440 | tf_op jit(solution)/shard_map/ppermute | solution.py:30
  29.2 1.6 %collective-permute-start.5 = (bf16[64,1024]{1,0:T(8,128)(2,1)S(1)}, bf16[64,1024]{1,0:T(8,128)(2,1)S(1)}, u32[]{:S(2)}, u32[]{:S(2)}) collective-permute-start(bf16[64,1024]{1,0:T(8,128)(2,1)S(1)} %get-tuple-element.65), channel_id=1, source_target_pairs={{0,1},{1,0},{2,3},{3,2},{4,5},{5,4},{6,7},{7,6},{8,9},{9,8},{10,11... | collective-permute-start | bytes 393224 | tf_op jit(solution)/shard_map/ppermute | solution.py:30
  29.5 12.7 %collective-permute-start.4 = (bf16[128,1024]{1,0:T(8,128)(2,1)S(1)}, bf16[128,1024]{1,0:T(8,128)(2,1)S(1)}, u32[]{:S(2)}, u32[]{:S(2)}) collective-permute-start(bf16[128,1024]{1,0:T(8,128)(2,1)S(1)} %add_convert_fusion), channel_id=1, source_target_pairs={{2,0},{3,1},{4,2},{5,3},{6,4},{7,5},{8,6},{9,7},{10,8},{11,9},{12,... | collective-permute-start | bytes 786440 | tf_op jit(solution)/shard_map/ppermute | solution.py:26
  31.5 13.3 %all-to-all-start.1 = ((bf16[8,8,1024]{2,1,0:T(8,128)(2,1)}), bf16[8,8,1024]{2,1,0:T(8,128)(2,1)S(1)}, u32[]{:S(2)}, u32[]{:S(2)}) async-start(bf16[8,8,1024]{2,1,0:T(8,128)(2,1)} %fusion), calls=%async_computation.1 | async-start | bytes 262144 | tf_op jit(solution)/shard_map/all_to_all | solution.py:36

commit v6 on v5

--- a/solution.py
+++ b/solution.py
@@ -106,8 +106,7 @@
 
 
 def layout_kernel(
-    lengths_hbm, weights_hbm, q_hbm, do_hbm, qf_ref, cot_hbm, begin_ref,
-    lengths_ref, weights_ref, q_ref, do_ref, cot_ref, small_sems, in_sems, out_sems,
+    lengths_hbm, weights_hbm, q_hbm, qf_ref, begin_ref, spread_ref, lengths_ref, weights_ref, q_ref, small_sems, sems
 ):
     height = q_ref.shape[1]
     kv_heads = q_ref.shape[0]
@@ -117,45 +116,39 @@
         pltpu.make_async_copy(lengths_hbm, lengths_ref, small_sems.at[0]),
         pltpu.make_async_copy(weights_hbm, weights_ref, small_sems.at[1]),
     ]
-    arriving = []
-    for g in range(kv_heads):
-        cols = pl.ds(g * heads * HEAD_DIM, heads * HEAD_DIM)
-        arriving.append(pltpu.make_async_copy(do_hbm.at[:, cols], do_ref.at[g], in_sems.at[1, g]))
-        arriving.append(pltpu.make_async_copy(q_hbm.at[:, cols], q_ref.at[g], in_sems.at[0, g]))
+    arriving = [
+        pltpu.make_async_copy(
+            q_hbm.at[:, pl.ds(g * heads * HEAD_DIM, heads * HEAD_DIM)], q_ref.at[g], sems.at[g]
+        )
+        for g in range(kv_heads)
+    ]
     for copy in small + arriving:
         copy.start()
     for copy in small:
         copy.wait()
     for part, begin in enumerate(answer_starts(lengths_ref[...], height, heads * rows)):
         begin_ref[part, 0:1] = begin
-    spread = jnp.broadcast_to(weights_ref[...], (HEAD_DIM, height)).T
-    leaving = []
+    spread_ref[...] = jnp.broadcast_to(weights_ref[...], (HEAD_DIM, height)).T
     for g in range(kv_heads):
-        arriving[2 * g].wait()
-        arriving[2 * g + 1].wait()
+        arriving[g].wait()
         for part in range(PARTS):
             at = slice(part * rows, (part + 1) * rows)
             for h in range(heads):
-                cols = slice(h * HEAD_DIM, (h + 1) * HEAD_DIM)
-                to = slice(h * rows, (h + 1) * rows)
-                cot_ref[g, part, to] = (do_ref[g, at, cols].astype(F32) * spread[at]).astype(BF16)
-                qf_ref[g, part, to] = q_ref[g, at, cols]
-        leaving.append(pltpu.make_async_copy(cot_ref.at[g], cot_hbm.at[g], out_sems.at[g]))
-        leaving[-1].start()
-    for copy in leaving:
-        copy.wait()
+                qf_ref[g, part, h * rows : (h + 1) * rows] = q_ref[g, at, h * HEAD_DIM : (h + 1) * HEAD_DIM]
 
 
 def window_kernel(
-    qf_ref, cot_hbm, begin_ref, far_ref, near_ref, own_ref,
-    cot_ref, powers_ref, slopes_ref, stats_ref, bias_ref, sems,
+    qf_ref, do_hbm, begin_ref, spread_ref, far_ref, near_ref, own_ref,
+    cot_ref, powers_ref, slopes_ref, stats_ref, bias_ref, do_ref, sems,
 ):
     kv_heads = qf_ref.shape[0]
     window = powers_ref.shape[2]
     rows = far_ref.shape[0] // PARTS
 
+    heads = do_ref.shape[2] // HEAD_DIM
+
     def arrival(g):
-        return pltpu.make_async_copy(cot_hbm.at[g], cot_ref.at[g], sems.at[g])
+        return pltpu.make_async_copy(do_hbm.at[:, columns_of(g, heads * HEAD_DIM)], do_ref.at[g], sems.at[g])
 
     for g in range(kv_heads):
         arrival(g).start()
@@ -183,6 +176,10 @@
         values = stack((far_ref, near_ref, own_ref), columns_of(g + kv_heads))
 
         def slope(part, _):
+            at = slice(part * rows, (part + 1) * rows)
+            for h in range(heads):
+                out_grad = do_ref[g, at, h * HEAD_DIM : (h + 1) * HEAD_DIM].astype(F32)
+                cot_ref[g, part, h * rows : (h + 1) * rows] = (out_grad * spread_ref[at]).astype(BF16)
             return dot_nt(values[part * rows : part * rows + window], cot_ref[g, part])
 
         def add(part, slopes):
@@ -420,25 +417,21 @@
     def in_hbm(*arrays):
         return [pltpu.with_memory_space_constraint(array, pltpu.HBM) for array in arrays]
 
-    flat_queries, cotangent, begin = call(
+    flat_queries, begin, weight_columns = call(
         layout_kernel,
         [
             pltpu.VMEM((*parts, lanes, HEAD_DIM), BF16),
-            pltpu.HBM((*parts, lanes, HEAD_DIM), BF16),
             pltpu.VMEM((PARTS, 8, lanes), F32),
+            pltpu.VMEM((height, HEAD_DIM), F32),
         ],
         LAYOUT_GFLOP,
-        in_hbm(lengths.reshape(1, -1), weights.reshape(1, -1), queries, out_grad),
-        in_specs=[anywhere] * 4,
-        out_specs=[vmem, anywhere, vmem],
+        in_hbm(lengths.reshape(1, -1), weights.reshape(1, -1), queries),
+        in_specs=[anywhere] * 3,
         scratch=[
             pltpu.VMEM((1, lengths.shape[0]), jnp.int32),
             pltpu.VMEM((1, height), F32),
             pltpu.VMEM((kv_heads, height, span), BF16),
-            pltpu.VMEM((kv_heads, height, span), BF16),
-            pltpu.VMEM((*parts, lanes, HEAD_DIM), BF16),
             pltpu.SemaphoreType.DMA((2,)),
-            pltpu.SemaphoreType.DMA((2, kv_heads)),
             pltpu.SemaphoreType.DMA((kv_heads,)),
         ],
     )
@@ -451,9 +444,13 @@
             pltpu.VMEM((*parts, 8, lanes), F32),
         ],
         3,
-        [flat_queries, *in_hbm(cotangent), begin, far, near, own],
-        in_specs=[vmem, anywhere] + [vmem] * 4,
-        scratch=[pltpu.VMEM((PARTS, window, lanes), F32), pltpu.SemaphoreType.DMA((kv_heads,))],
+        [flat_queries, *in_hbm(out_grad), begin, weight_columns, far, near, own],
+        in_specs=[vmem, anywhere] + [vmem] * 5,
+        scratch=[
+            pltpu.VMEM((PARTS, window, lanes), F32),
+            pltpu.VMEM((kv_heads, height, span), BF16),
+            pltpu.SemaphoreType.DMA((kv_heads,)),
+        ],
     )
     keep, passed, near_terms, far_terms, own_terms, chances, score_grad, last_chances, last_grad = call(
         terms_kernel,

time: 46.1 us -> 45 us (0.976)
  starting transfers between devices: 18 us -> 16.8 us
  waiting for transfers between devices: 7.39 us -> 8.57 us
  Pallas kernels: 18.7 us -> 17.6 us
    all_to_all x2, waiting for transfers between devices: 6.55 us -> 7.73 us  [across_chips(): return lax.all_to_all(x, 'row', 0, 0, tiled=True, axis_index_groups=groups)]
    all_to_all x2, starting transfers between devices: 10.9 us -> 9.69 us  [across_chips(): return lax.all_to_all(x, 'row', 0, 0, tiled=True, axis_index_groups=groups)]
    pallas_call x6, Pallas kernels: 17.1 us -> 16 us  [call(): pl.pallas_call(kernel, out_shape=outs, scratch_shapes=list(scratch), comp...]
  transfers between devices with their start and end apart: 8 -> 8, of which waited for: 3 -> 3; matrix products, arithmetic and copies ran while one was open for 2% -> 2% of each run, Pallas kernels for 27% -> 25%
where the time goes in v6:
time: 45 us; the launch traced here: 44.5 us
  Pallas kernels  17.6 us (39%)
  starting transfers between devices  16.8 us (37%)
  waiting for transfers between devices  8.57 us (19%)
  other arithmetic  0.81 us (2%)
  between operations  0.74 us (2%)
    pallas_call x6, Pallas kernels, call(): pl.pallas_call(kernel, out_shape=outs, scratch_shapes=list(scratch), comp...  16 us
    all_to_all x2, starting transfers between devices, across_chips(): return lax.all_to_all(x, 'row', 0, 0, tiled=True, axis_index_groups=groups)  9.69 us
    all_to_all x2, waiting for transfers between devices, across_chips(): return lax.all_to_all(x, 'row', 0, 0, tiled=True, axis_index_groups=groups)  7.73 us
    ppermute x2, starting transfers between devices, shifted(): return lax.ppermute(x, 'row', pairs)  6.13 us
    pallas_call x1, Pallas kernels, per_device(): pl.pallas_call(pack_kernel, out_shape=[pltpu.VMEM((height, 2 * columns),...  1.64 us
    ppermute x4, starting transfers between devices, from_other_core(): lax.ppermute(x, 'row', [(i, i ^ 1) for i in range(lax.axis_size('row'))])  0.97 us
  transfers between devices with their start and end apart: 8, of which 3 were waited for; matrix products, arithmetic and copies ran while one was open for 2% of the time, Pallas kernels for 25%

profile of v6, /device:TPU:0, one launch (start us, length us, event | category | flops | bytes accessed | tf_op | source)
XLA Modules:
  0.0 44.5 jit_solution(13170149142428947318)
XLA Ops:
  0.6 1.6 %shard_map.128 = (bf16[128,1024]{1,0:T(8,128)(2,1)S(1)}, bf16[8,8,1024]{2,1,0:T(8,128)(2,1)}) custom-call(bf16[128,512]{1,0:T(8,128)(2,1)} %k_ref.1, bf16[128,512]{1,0:T(8,128)(2,1)} %v_ref.1, bf16[8,512]{1,0:T(8,128)(2,1)} %pk_ref.1, bf16[8,512]{1,0:T(8,128)(2,1)} %pv_ref.1), custom_call_target="tpu_custom_call" | custom-call | tf_op jit(solution)/shard_map/pallas_call | solution.py:403
  2.3 4.8 %collective-permute-start = (bf16[128,1024]{1,0:T(8,128)(2,1)S(1)}, bf16[128,1024]{1,0:T(8,128)(2,1)S(1)}, u32[]{:S(2)}, u32[]{:S(2)}) collective-permute-start(bf16[128,1024]{1,0:T(8,128)(2,1)S(1)} %get-tuple-element.41.own_ref), channel_id=1, source_target_pairs={{0,2},{1,3},{2,4},{3,5},{4,6},{5,7},{6,8},{7,9},{8,10},{9,11},{10,... | collective-permute-start | bytes 786440 | tf_op jit(solution)/shard_map/ppermute | solution.py:26
  7.1 4.9 %all-to-all-start = ((bf16[8,8,1024]{2,1,0:T(8,128)(2,1)}), bf16[8,8,1024]{2,1,0:T(8,128)(2,1)S(1)}, u32[]{:S(2)}, u32[]{:S(2)}) async-start(bf16[8,8,1024]{2,1,0:T(8,128)(2,1)} %get-tuple-element.42), calls=%async_computation | async-start | bytes 262144 | tf_op jit(solution)/shard_map/all_to_all | solution.py:36
  12.0 0.8 %collective-permute-done.far_ref = bf16[128,1024]{1,0:T(8,128)(2,1)S(1)} collective-permute-done((bf16[128,1024]{1,0:T(8,128)(2,1)S(1)}, bf16[128,1024]{1,0:T(8,128)(2,1)S(1)}, u32[]{:S(2)}, u32[]{:S(2)}) %collective-permute-start) | collective-permute-done | bytes 262176 | tf_op jit(solution)/shard_map/ppermute | solution.py:26
  12.9 0.1 collective-permute-start.1
  12.9 1.3 %shard_map.127 = (bf16[4,4,256,128]{3,2,1,0:T(8,128)(2,1)S(1)}, f32[4,8,256]{2,1,0:T(8,128)S(1)}, f32[128,128]{1,0:T(8,128)S(1)}) custom-call(s32[1,32]{1,0:T(1,128)} %bitcast.8, f32[1,128]{1,0:T(1,128)} %bitcast.9, bf16[128,4096]{1,0:T(8,128)(2,1)} %q_hbm.1), custom_call_target="tpu_custom_call" | custom-call | flops 3000000000 | bytes 1000000 | tf_op jit(solution)/shard_map/pallas_call | solution.py:391
  14.3 5.1 %all-to-all-done = bf16[8,8,1024]{2,1,0:T(8,128)(2,1)S(1)} async-done(((bf16[8,8,1024]{2,1,0:T(8,128)(2,1)}), bf16[8,8,1024]{2,1,0:T(8,128)(2,1)S(1)}, u32[]{:S(2)}, u32[]{:S(2)}) %all-to-all-start) | async-done | bytes 131104 | tf_op jit(solution)/shard_map/all_to_all | solution.py:36
  19.3 0.0 collective-permute-done.1.near_ref
  19.4 0.0 collective-permute-start.2
  19.4 3.8 %shard_map.129 = (bf16[4,4,256,128]{3,2,1,0:T(8,128)(2,1)S(1)}, f32[4,4,288,256]{3,2,1,0:T(8,128)S(1)}, f32[4,4,288,256]{3,2,1,0:T(8,128)S(1)}, f32[4,4,8,256]{3,2,1,0:T(8,128)S(1)}) custom-call(bf16[4,4,256,128]{3,2,1,0:T(8,128)(2,1)S(1)} %get-tuple-element.38.qf_ref, bf16[128,4096]{1,0:T(8,128)(2,1)} %do_hbm.1, ...), custom_call_target="tpu_custom_call" | custom-call | flops 3000000000 | bytes 1000000 | tf_op jit(solution)/shard_map/pallas_call | solution.py:391
  23.1 0.0 collective-permute-done.2.other_ref
  23.1 4.2 %shard_map.130 = (f32[64,1024]{1,0:T(8,128)S(1)}, bf16[64,1024]{1,0:T(8,128)(2,1)S(1)}, bf16[128,1024]{1,0:T(8,128)(2,1)S(1)}, bf16[128,1024]{1,0:T(8,128)(2,1)S...) custom-call(bf16[4,4,256,128]{3,2,1,0:T(8,128)(2,1)S(1)} %get-tuple-, ...), custom_call_target="tpu_custom_call" | custom-call | flops 4000000000 | bytes 1000000 | tf_op jit(solution)/shard_map/pallas_call | solution.py:391
  27.3 0.6 %collective-permute-start.3 = (bf16[128,1024]{1,0:T(8,128)(2,1)S(1)}, bf16[128,1024]{1,0:T(8,128)(2,1)S(1)}, u32[]{:S(2)}, u32[]{:S(2)}) collective-permute-start(bf16[128,1024]{1,0:T(8,128)(2,1)S(1)} %get-tuple-element.51), channel_id=1, source_target_pairs={{0,1},{1,0},{2,3},{3,2},{4,5},{5,4},{6,7},{7,6},{8,9},{9,8},{10,11... | collective-permute-start | bytes 786440 | tf_op jit(solution)/shard_map/ppermute | solution.py:30
  27.9 1.3 %shard_map.131 = (bf16[4,416,256]{2,1,0:T(8,128)(2,1)}, bf16[4,416,256]{2,1,0:T(8,128)(2,1)}) custom-call(bf16[4,416,256]{2,1,0:T(8,128)(2,1)S(1)} %get-tuple-element.52.chances_ref, bf16[4,416,256]{2,1,0:T(8,128)(2,1)S(1)} %get-tuple-element.53.grad_ref), custom_call_target="tpu_custom_call" | custom-call | flops 1000000000 | bytes 1000000 | tf_op jit(solution)/shard_map/pallas_call | solution.py:391
  29.1 0.0 collective-permute-done.3.near_ref
  29.2 0.1 add_convert_fusion
  29.3 0.3 collective-permute-start.5
  29.6 1.3 %collective-permute-start.4 = (bf16[128,1024]{1,0:T(8,128)(2,1)S(1)}, bf16[128,1024]{1,0:T(8,128)(2,1)S(1)}, u32[]{:S(2)}, u32[]{:S(2)}) collective-permute-start(bf16[128,1024]{1,0:T(8,128)(2,1)S(1)} %add_convert_fusion), channel_id=1, source_target_pairs={{2,0},{3,1},{4,2},{5,3},{6,4},{7,5},{8,6},{9,7},{10,8},{11,9},{12,... | collective-permute-start | bytes 786440 | tf_op jit(solution)/shard_map/ppermute | solution.py:26
  30.9 0.0 collective-permute-done.5
  30.9 0.7 %fusion = bf16[8,8,1024]{2,1,0:T(8,128)(2,1)} fusion(f32[64,1024]{1,0:T(8,128)S(1)} %get-tuple-element.64, bf16[64,1024]{1,0:T(8,128)(2,1)S(1)} %collective-permute-done.5), kind=kLoop, calls=%fused_computation.3 | loop fusion | flops 196608 | bytes 524288 | tf_op jit(solution)/shard_map/reshape | solution.py:501
  31.6 4.8 %all-to-all-start.1 = ((bf16[8,8,1024]{2,1,0:T(8,128)(2,1)}), bf16[8,8,1024]{2,1,0:T(8,128)(2,1)S(1)}, u32[]{:S(2)}, u32[]{:S(2)}) async-start(bf16[8,8,1024]{2,1,0:T(8,128)(2,1)} %fusion), calls=%async_computation.1 | async-start | bytes 262144 | tf_op jit(solution)/shard_map/all_to_all | solution.py:36
  36.4 4.7 %shard_map.132 = (bf16[128,4096]{1,0:T(8,128)(2,1)}, bf16[128,4096]{1,0:T(8,128)(2,1)}) custom-call(bf16[3,4,416,256]{3,2,1,0:T(8,128)(2,1)} %get-tuple-element.49.chances_hbm, bf16[3,4,416,256]{3,2,1,0:T(8,128)(2,1)} %get-tuple-element.50.grad_hbm, bf16[4,416,256]{2,1,0:T(8,128)(2,1)} %get-tuple-element.55.last_chances_hbm, ...), custom_call_target="tpu_custom_call" | custom-call | flops 5000000000 | bytes 1000000 | tf_op jit(solution)/shard_map/pallas_call | solution.py:391
  41.1 0.0 collective-permute-done.4.far_ref
  41.1 2.7 %all-to-all-done.1.arrived_ref = bf16[8,8,1024]{2,1,0:T(8,128)(2,1)S(1)} async-done(((bf16[8,8,1024]{2,1,0:T(8,128)(2,1)}), bf16[8,8,1024]{2,1,0:T(8,128)(2,1)S(1)}, u32[]{:S(2)}, u32[]{:S(2)}) %all-to-all-start.1) | async-done | bytes 131104 | tf_op jit(solution)/shard_map/all_to_all | solution.py:36
  43.7 0.8 %shard_map.133 = (bf16[128,512]{1,0:T(8,128)(2,1)}, bf16[128,512]{1,0:T(8,128)(2,1)}, f32[8,512]{1,0:T(8,128)}, f32[8,512]{1,0:T(8,128)}) custom-call(f32[128,1024]{1,0:T(8,128)S(1)} %get-tuple-element.59.own_ref, bf16[128,1024]{1,0:T(8,128)(2,1)S(1)} %collective-permute-done.3.near_ref, bf16[128,1024]{1,0:T(8,128)(2,1)S(1)} %collective-permute-done.4.far_ref, ...), custom_call_target="tpu_custom_call" | custom-call | flops 100000000 | bytes 1000000 | tf_op jit(solution)/shard_map/pallas_call | solution.py:391
  (1 shorter events, 0.0 us)
Async XLA Ops:
  2.3 10.6 %collective-permute-start = (bf16[128,1024]{1,0:T(8,128)(2,1)S(1)}, bf16[128,1024]{1,0:T(8,128)(2,1)S(1)}, u32[]{:S(2)}, u32[]{:S(2)}) collective-permute-start(bf16[128,1024]{1,0:T(8,128)(2,1)S(1)} %get-tuple-element.41.own_ref), channel_id=1, source_target_pairs={{0,2},{1,3},{2,4},{3,5},{4,6},{5,7},{6,8},{7,9},{8,10},{9,11},{10,... | collective-permute-start | bytes 786440 | tf_op jit(solution)/shard_map/ppermute | solution.py:26
  7.1 12.2 %all-to-all-start = ((bf16[8,8,1024]{2,1,0:T(8,128)(2,1)}), bf16[8,8,1024]{2,1,0:T(8,128)(2,1)S(1)}, u32[]{:S(2)}, u32[]{:S(2)}) async-start(bf16[8,8,1024]{2,1,0:T(8,128)(2,1)} %get-tuple-element.42), calls=%async_computation | async-start | bytes 262144 | tf_op jit(solution)/shard_map/all_to_all | solution.py:36
  12.9 6.5 %collective-permute-start.1 = (bf16[128,1024]{1,0:T(8,128)(2,1)S(1)}, bf16[128,1024]{1,0:T(8,128)(2,1)S(1)}, u32[]{:S(2)}, u32[]{:S(2)}) collective-permute-start(bf16[128,1024]{1,0:T(8,128)(2,1)S(1)} %broadcast_select_fusion), channel_id=1, source_target_pairs={{0,1},{1,0},{2,3},{3,2},{4,5},{5,4},{6,7},{7,6},{8,9},{9,8},{10,11... | collective-permute-start | bytes 786440 | tf_op jit(solution)/shard_map/ppermute | solution.py:30
  19.4 3.8 %collective-permute-start.2 = (bf16[64,1024]{1,0:T(8,128)(2,1)S(1)}, bf16[64,1024]{1,0:T(8,128)(2,1)S(1)}, u32[]{:S(2)}, u32[]{:S(2)}) collective-permute-start(bf16[64,1024]{1,0:T(8,128)(2,1)S(1)} %bitcast.5), channel_id=1, source_target_pairs={{0,1},{1,0},{2,3},{3,2},{4,5},{5,4},{6,7},{7,6},{8,9},{9,8},{10,11... | collective-permute-start | bytes 393224 | tf_op jit(solution)/shard_map/ppermute | solution.py:30
  27.3 1.8 %collective-permute-start.3 = (bf16[128,1024]{1,0:T(8,128)(2,1)S(1)}, bf16[128,1024]{1,0:T(8,128)(2,1)S(1)}, u32[]{:S(2)}, u32[]{:S(2)}) collective-permute-start(bf16[128,1024]{1,0:T(8,128)(2,1)S(1)} %get-tuple-element.51), channel_id=1, source_target_pairs={{0,1},{1,0},{2,3},{3,2},{4,5},{5,4},{6,7},{7,6},{8,9},{9,8},{10,11... | collective-permute-start | bytes 786440 | tf_op jit(solution)/shard_map/ppermute | solution.py:30
  29.3 1.6 %collective-permute-start.5 = (bf16[64,1024]{1,0:T(8,128)(2,1)S(1)}, bf16[64,1024]{1,0:T(8,128)(2,1)S(1)}, u32[]{:S(2)}, u32[]{:S(2)}) collective-permute-start(bf16[64,1024]{1,0:T(8,128)(2,1)S(1)} %get-tuple-element.65), channel_id=1, source_target_pairs={{0,1},{1,0},{2,3},{3,2},{4,5},{5,4},{6,7},{7,6},{8,9},{9,8},{10,11... | collective-permute-start | bytes 393224 | tf_op jit(solution)/shard_map/ppermute | solution.py:30
  29.6 11.5 %collective-permute-start.4 = (bf16[128,1024]{1,0:T(8,128)(2,1)S(1)}, bf16[128,1024]{1,0:T(8,128)(2,1)S(1)}, u32[]{:S(2)}, u32[]{:S(2)}) collective-permute-start(bf16[128,1024]{1,0:T(8,128)(2,1)S(1)} %add_convert_fusion), channel_id=1, source_target_pairs={{2,0},{3,1},{4,2},{5,3},{6,4},{7,5},{8,6},{9,7},{10,8},{11,9},{12,... | collective-permute-start | bytes 786440 | tf_op jit(solution)/shard_map/ppermute | solution.py:26
  31.6 12.2 %all-to-all-start.1 = ((bf16[8,8,1024]{2,1,0:T(8,128)(2,1)}), bf16[8,8,1024]{2,1,0:T(8,128)(2,1)S(1)}, u32[]{:S(2)}, u32[]{:S(2)}) async-start(bf16[8,8,1024]{2,1,0:T(8,128)(2,1)} %fusion), calls=%async_computation.1 | async-start | bytes 262144 | tf_op jit(solution)/shard_map/all_to_all | solution.py:36

commit v7 on v6

--- a/solution.py
+++ b/solution.py
@@ -188,8 +188,10 @@
 
         staged(slope, add)
 
-    for_heads(kv_heads, powers_head)
-    for_heads(kv_heads, slopes_head)
+    for g in range(kv_heads):
+        powers_head(g)
+    for g in range(kv_heads):
+        slopes_head(g)
 
 
 def terms_kernel(

time: 45 us -> 44.3 us (0.984)
  Pallas kernels: 17.6 us -> 17 us
    pallas_call x6, Pallas kernels: 16 us -> 15.4 us  [call(): pl.pallas_call(kernel, out_shape=outs, scratch_shapes=list(scratch), comp...]
  transfers between devices with their start and end apart: 8 -> 8, of which waited for: 3 -> 3; matrix products, arithmetic and copies ran while one was open for 2% -> 2% of each run, Pallas kernels for 25% -> 24%
where the time goes in v7:
time: 44.3 us; the launch traced here: 43.9 us
  Pallas kernels  17 us (38%)
  starting transfers between devices  16.8 us (38%)
  waiting for transfers between devices  8.57 us (19%)
  other arithmetic  0.81 us (2%)
  between operations  0.74 us (2%)
    pallas_call x6, Pallas kernels, call(): pl.pallas_call(kernel, out_shape=outs, scratch_shapes=list(scratch), comp...  15.4 us
    all_to_all x2, starting transfers between devices, across_chips(): return lax.all_to_all(x, 'row', 0, 0, tiled=True, axis_index_groups=groups)  9.66 us
    all_to_all x2, waiting for transfers between devices, across_chips(): return lax.all_to_all(x, 'row', 0, 0, tiled=True, axis_index_groups=groups)  7.73 us
    ppermute x2, starting transfers between devices, shifted(): return lax.ppermute(x, 'row', pairs)  6.13 us
    pallas_call x1, Pallas kernels, per_device(): pl.pallas_call(pack_kernel, out_shape=[pltpu.VMEM((height, 2 * columns),...  1.64 us
    ppermute x4, starting transfers between devices, from_other_core(): lax.ppermute(x, 'row', [(i, i ^ 1) for i in range(lax.axis_size('row'))])  0.97 us
  transfers between devices with their start and end apart: 8, of which 3 were waited for; matrix products, arithmetic and copies ran while one was open for 2% of the time, Pallas kernels for 24%

profile of v7, /device:TPU:0, one launch (start us, length us, event | category | flops | bytes accessed | tf_op | source)
XLA Modules:
  0.0 43.9 jit_solution(17797967987368919108)
XLA Ops:
  0.6 1.6 %shard_map.128 = (bf16[128,1024]{1,0:T(8,128)(2,1)S(1)}, bf16[8,8,1024]{2,1,0:T(8,128)(2,1)}) custom-call(bf16[128,512]{1,0:T(8,128)(2,1)} %k_ref.1, bf16[128,512]{1,0:T(8,128)(2,1)} %v_ref.1, bf16[8,512]{1,0:T(8,128)(2,1)} %pk_ref.1, bf16[8,512]{1,0:T(8,128)(2,1)} %pv_ref.1), custom_call_target="tpu_custom_call" | custom-call | tf_op jit(solution)/shard_map/pallas_call | solution.py:405
  2.3 4.8 %collective-permute-start = (bf16[128,1024]{1,0:T(8,128)(2,1)S(1)}, bf16[128,1024]{1,0:T(8,128)(2,1)S(1)}, u32[]{:S(2)}, u32[]{:S(2)}) collective-permute-start(bf16[128,1024]{1,0:T(8,128)(2,1)S(1)} %get-tuple-element.41.own_ref), channel_id=1, source_target_pairs={{0,2},{1,3},{2,4},{3,5},{4,6},{5,7},{6,8},{7,9},{8,10},{9,11},{10,... | collective-permute-start | bytes 786440 | tf_op jit(solution)/shard_map/ppermute | solution.py:26
  7.1 4.9 %all-to-all-start = ((bf16[8,8,1024]{2,1,0:T(8,128)(2,1)}), bf16[8,8,1024]{2,1,0:T(8,128)(2,1)S(1)}, u32[]{:S(2)}, u32[]{:S(2)}) async-start(bf16[8,8,1024]{2,1,0:T(8,128)(2,1)} %get-tuple-element.42), calls=%async_computation | async-start | bytes 262144 | tf_op jit(solution)/shard_map/all_to_all | solution.py:36
  12.0 0.8 %collective-permute-done.far_ref = bf16[128,1024]{1,0:T(8,128)(2,1)S(1)} collective-permute-done((bf16[128,1024]{1,0:T(8,128)(2,1)S(1)}, bf16[128,1024]{1,0:T(8,128)(2,1)S(1)}, u32[]{:S(2)}, u32[]{:S(2)}) %collective-permute-start) | collective-permute-done | bytes 262176 | tf_op jit(solution)/shard_map/ppermute | solution.py:26
  12.9 0.1 collective-permute-start.1
  12.9 1.3 %shard_map.127 = (bf16[4,4,256,128]{3,2,1,0:T(8,128)(2,1)S(1)}, f32[4,8,256]{2,1,0:T(8,128)S(1)}, f32[128,128]{1,0:T(8,128)S(1)}) custom-call(s32[1,32]{1,0:T(1,128)} %bitcast.8, f32[1,128]{1,0:T(1,128)} %bitcast.9, bf16[128,4096]{1,0:T(8,128)(2,1)} %q_hbm.1), custom_call_target="tpu_custom_call" | custom-call | flops 3000000000 | bytes 1000000 | tf_op jit(solution)/shard_map/pallas_call | solution.py:393
  14.3 5.1 %all-to-all-done = bf16[8,8,1024]{2,1,0:T(8,128)(2,1)S(1)} async-done(((bf16[8,8,1024]{2,1,0:T(8,128)(2,1)}), bf16[8,8,1024]{2,1,0:T(8,128)(2,1)S(1)}, u32[]{:S(2)}, u32[]{:S(2)}) %all-to-all-start) | async-done | bytes 131104 | tf_op jit(solution)/shard_map/all_to_all | solution.py:36
  19.3 0.0 collective-permute-done.1.near_ref
  19.4 0.0 collective-permute-start.2
  19.4 3.2 %shard_map.129 = (bf16[4,4,256,128]{3,2,1,0:T(8,128)(2,1)S(1)}, f32[4,4,288,256]{3,2,1,0:T(8,128)S(1)}, f32[4,4,288,256]{3,2,1,0:T(8,128)S(1)}, f32[4,4,8,256]{3,2,1,0:T(8,128)S(1)}) custom-call(bf16[4,4,256,128]{3,2,1,0:T(8,128)(2,1)S(1)} %get-tuple-element.38.qf_ref, bf16[128,4096]{1,0:T(8,128)(2,1)} %do_hbm.1, ...), custom_call_target="tpu_custom_call" | custom-call | flops 3000000000 | bytes 1000000 | tf_op jit(solution)/shard_map/pallas_call | solution.py:393
  22.5 0.0 collective-permute-done.2.other_ref
  22.5 4.2 %shard_map.130 = (f32[64,1024]{1,0:T(8,128)S(1)}, bf16[64,1024]{1,0:T(8,128)(2,1)S(1)}, bf16[128,1024]{1,0:T(8,128)(2,1)S(1)}, bf16[128,1024]{1,0:T(8,128)(2,1)S...) custom-call(bf16[4,4,256,128]{3,2,1,0:T(8,128)(2,1)S(1)} %get-tuple-, ...), custom_call_target="tpu_custom_call" | custom-call | flops 4000000000 | bytes 1000000 | tf_op jit(solution)/shard_map/pallas_call | solution.py:393
  26.7 0.6 %collective-permute-start.3 = (bf16[128,1024]{1,0:T(8,128)(2,1)S(1)}, bf16[128,1024]{1,0:T(8,128)(2,1)S(1)}, u32[]{:S(2)}, u32[]{:S(2)}) collective-permute-start(bf16[128,1024]{1,0:T(8,128)(2,1)S(1)} %get-tuple-element.51), channel_id=1, source_target_pairs={{0,1},{1,0},{2,3},{3,2},{4,5},{5,4},{6,7},{7,6},{8,9},{9,8},{10,11... | collective-permute-start | bytes 786440 | tf_op jit(solution)/shard_map/ppermute | solution.py:30
  27.3 1.3 %shard_map.131 = (bf16[4,416,256]{2,1,0:T(8,128)(2,1)}, bf16[4,416,256]{2,1,0:T(8,128)(2,1)}) custom-call(bf16[4,416,256]{2,1,0:T(8,128)(2,1)S(1)} %get-tuple-element.52.chances_ref, bf16[4,416,256]{2,1,0:T(8,128)(2,1)S(1)} %get-tuple-element.53.grad_ref), custom_call_target="tpu_custom_call" | custom-call | flops 1000000000 | bytes 1000000 | tf_op jit(solution)/shard_map/pallas_call | solution.py:393
  28.6 0.0 collective-permute-done.3.near_ref
  28.6 0.1 add_convert_fusion
  28.7 0.3 collective-permute-start.5
  29.0 1.3 %collective-permute-start.4 = (bf16[128,1024]{1,0:T(8,128)(2,1)S(1)}, bf16[128,1024]{1,0:T(8,128)(2,1)S(1)}, u32[]{:S(2)}, u32[]{:S(2)}) collective-permute-start(bf16[128,1024]{1,0:T(8,128)(2,1)S(1)} %add_convert_fusion), channel_id=1, source_target_pairs={{2,0},{3,1},{4,2},{5,3},{6,4},{7,5},{8,6},{9,7},{10,8},{11,9},{12,... | collective-permute-start | bytes 786440 | tf_op jit(solution)/shard_map/ppermute | solution.py:26
  30.3 0.0 collective-permute-done.5
  30.3 0.7 %fusion = bf16[8,8,1024]{2,1,0:T(8,128)(2,1)} fusion(f32[64,1024]{1,0:T(8,128)S(1)} %get-tuple-element.64, bf16[64,1024]{1,0:T(8,128)(2,1)S(1)} %collective-permute-done.5), kind=kLoop, calls=%fused_computation.3 | loop fusion | flops 196608 | bytes 524288 | tf_op jit(solution)/shard_map/reshape | solution.py:503
  31.0 4.8 %all-to-all-start.1 = ((bf16[8,8,1024]{2,1,0:T(8,128)(2,1)}), bf16[8,8,1024]{2,1,0:T(8,128)(2,1)S(1)}, u32[]{:S(2)}, u32[]{:S(2)}) async-start(bf16[8,8,1024]{2,1,0:T(8,128)(2,1)} %fusion), calls=%async_computation.1 | async-start | bytes 262144 | tf_op jit(solution)/shard_map/all_to_all | solution.py:36
  35.7 4.7 %shard_map.132 = (bf16[128,4096]{1,0:T(8,128)(2,1)}, bf16[128,4096]{1,0:T(8,128)(2,1)}) custom-call(bf16[3,4,416,256]{3,2,1,0:T(8,128)(2,1)} %get-tuple-element.49.chances_hbm, bf16[3,4,416,256]{3,2,1,0:T(8,128)(2,1)} %get-tuple-element.50.grad_hbm, bf16[4,416,256]{2,1,0:T(8,128)(2,1)} %get-tuple-element.55.last_chances_hbm, ...), custom_call_target="tpu_custom_call" | custom-call | flops 5000000000 | bytes 1000000 | tf_op jit(solution)/shard_map/pallas_call | solution.py:393
  40.4 0.0 collective-permute-done.4.far_ref
  40.4 2.7 %all-to-all-done.1.arrived_ref = bf16[8,8,1024]{2,1,0:T(8,128)(2,1)S(1)} async-done(((bf16[8,8,1024]{2,1,0:T(8,128)(2,1)}), bf16[8,8,1024]{2,1,0:T(8,128)(2,1)S(1)}, u32[]{:S(2)}, u32[]{:S(2)}) %all-to-all-start.1) | async-done | bytes 131104 | tf_op jit(solution)/shard_map/all_to_all | solution.py:36
  43.1 0.8 %shard_map.133 = (bf16[128,512]{1,0:T(8,128)(2,1)}, bf16[128,512]{1,0:T(8,128)(2,1)}, f32[8,512]{1,0:T(8,128)}, f32[8,512]{1,0:T(8,128)}) custom-call(f32[128,1024]{1,0:T(8,128)S(1)} %get-tuple-element.59.own_ref, bf16[128,1024]{1,0:T(8,128)(2,1)S(1)} %collective-permute-done.3.near_ref, bf16[128,1024]{1,0:T(8,128)(2,1)S(1)} %collective-permute-done.4.far_ref, ...), custom_call_target="tpu_custom_call" | custom-call | flops 100000000 | bytes 1000000 | tf_op jit(solution)/shard_map/pallas_call | solution.py:393
  (1 shorter events, 0.0 us)
Async XLA Ops:
  2.3 10.6 %collective-permute-start = (bf16[128,1024]{1,0:T(8,128)(2,1)S(1)}, bf16[128,1024]{1,0:T(8,128)(2,1)S(1)}, u32[]{:S(2)}, u32[]{:S(2)}) collective-permute-start(bf16[128,1024]{1,0:T(8,128)(2,1)S(1)} %get-tuple-element.41.own_ref), channel_id=1, source_target_pairs={{0,2},{1,3},{2,4},{3,5},{4,6},{5,7},{6,8},{7,9},{8,10},{9,11},{10,... | collective-permute-start | bytes 786440 | tf_op jit(solution)/shard_map/ppermute | solution.py:26
  7.1 12.2 %all-to-all-start = ((bf16[8,8,1024]{2,1,0:T(8,128)(2,1)}), bf16[8,8,1024]{2,1,0:T(8,128)(2,1)S(1)}, u32[]{:S(2)}, u32[]{:S(2)}) async-start(bf16[8,8,1024]{2,1,0:T(8,128)(2,1)} %get-tuple-element.42), calls=%async_computation | async-start | bytes 262144 | tf_op jit(solution)/shard_map/all_to_all | solution.py:36
  12.9 6.5 %collective-permute-start.1 = (bf16[128,1024]{1,0:T(8,128)(2,1)S(1)}, bf16[128,1024]{1,0:T(8,128)(2,1)S(1)}, u32[]{:S(2)}, u32[]{:S(2)}) collective-permute-start(bf16[128,1024]{1,0:T(8,128)(2,1)S(1)} %broadcast_select_fusion), channel_id=1, source_target_pairs={{0,1},{1,0},{2,3},{3,2},{4,5},{5,4},{6,7},{7,6},{8,9},{9,8},{10,11... | collective-permute-start | bytes 786440 | tf_op jit(solution)/shard_map/ppermute | solution.py:30
  19.4 3.2 %collective-permute-start.2 = (bf16[64,1024]{1,0:T(8,128)(2,1)S(1)}, bf16[64,1024]{1,0:T(8,128)(2,1)S(1)}, u32[]{:S(2)}, u32[]{:S(2)}) collective-permute-start(bf16[64,1024]{1,0:T(8,128)(2,1)S(1)} %bitcast.5), channel_id=1, source_target_pairs={{0,1},{1,0},{2,3},{3,2},{4,5},{5,4},{6,7},{7,6},{8,9},{9,8},{10,11... | collective-permute-start | bytes 393224 | tf_op jit(solution)/shard_map/ppermute | solution.py:30
  26.7 1.8 %collective-permute-start.3 = (bf16[128,1024]{1,0:T(8,128)(2,1)S(1)}, bf16[128,1024]{1,0:T(8,128)(2,1)S(1)}, u32[]{:S(2)}, u32[]{:S(2)}) collective-permute-start(bf16[128,1024]{1,0:T(8,128)(2,1)S(1)} %get-tuple-element.51), channel_id=1, source_target_pairs={{0,1},{1,0},{2,3},{3,2},{4,5},{5,4},{6,7},{7,6},{8,9},{9,8},{10,11... | collective-permute-start | bytes 786440 | tf_op jit(solution)/shard_map/ppermute | solution.py:30
  28.7 1.6 %collective-permute-start.5 = (bf16[64,1024]{1,0:T(8,128)(2,1)S(1)}, bf16[64,1024]{1,0:T(8,128)(2,1)S(1)}, u32[]{:S(2)}, u32[]{:S(2)}) collective-permute-start(bf16[64,1024]{1,0:T(8,128)(2,1)S(1)} %get-tuple-element.65), channel_id=1, source_target_pairs={{0,1},{1,0},{2,3},{3,2},{4,5},{5,4},{6,7},{7,6},{8,9},{9,8},{10,11... | collective-permute-start | bytes 393224 | tf_op jit(solution)/shard_map/ppermute | solution.py:30
  29.0 11.4 %collective-permute-start.4 = (bf16[128,1024]{1,0:T(8,128)(2,1)S(1)}, bf16[128,1024]{1,0:T(8,128)(2,1)S(1)}, u32[]{:S(2)}, u32[]{:S(2)}) collective-permute-start(bf16[128,1024]{1,0:T(8,128)(2,1)S(1)} %add_convert_fusion), channel_id=1, source_target_pairs={{2,0},{3,1},{4,2},{5,3},{6,4},{7,5},{8,6},{9,7},{10,8},{11,9},{12,... | collective-permute-start | bytes 786440 | tf_op jit(solution)/shard_map/ppermute | solution.py:26
  31.0 12.1 %all-to-all-start.1 = ((bf16[8,8,1024]{2,1,0:T(8,128)(2,1)}), bf16[8,8,1024]{2,1,0:T(8,128)(2,1)S(1)}, u32[]{:S(2)}, u32[]{:S(2)}) async-start(bf16[8,8,1024]{2,1,0:T(8,128)(2,1)} %fusion), calls=%async_computation.1 | async-start | bytes 262144 | tf_op jit(solution)/shard_map/all_to_all | solution.py:36
